TPU v7x, 32 devices: a whole 2x2x4 slice. The times are simulated.
32 devices in a mesh: py: 4 (over y, core), px: 8 (over z, x).
Axes of the slice: x: 2, y: 2, z: 4, core: 2. Of those that a mesh axis runs over, the one named last changes fastest.
Arguments:
- pieces: bfloat16 [2048, 128, 128], P(('py', 'px')), may hold values from -6 to 6
- owner_map: int32 [2048], P(('py', 'px')), may hold values from 0 to 31, as said below
- offsets: int32 [2048], P(('py', 'px')), may hold values from 0 to 63
- template: bfloat16 [4096, 8192], P('py', 'px'), may hold values from -32 to 32
- coefficients: float32 [3, 15], replicated, may hold values from -3 to 3
Outputs:
- difference: float32 [4096, 8192], P('py', 'px')
Inputs may be any that keep to these rules, and one draw needn't show every extreme that they name: owner_map[p] is the tile of the device holding p or one of the eight tiles around it inside the grid; no device sends more than 16 pieces to one tile, and every device sends exactly 16 to one of its tiles.
All inputs are finite; a program needn't handle non-finite values.
Results may differ from a plain program's by a relative error of at most 0.0021.
Values may be sent and summed in bfloat16 or wider, within the bound.
No kernel may reach another device: no remote copies, remote signals or barrier semaphores. Data moves between devices by JAX's collectives and lax.ppermute only.
A program may use at most 128 MiB of HBM per device.

v0:
```python
import jax
import jax.numpy as jnp
from jax import lax
from jax.sharding import PartitionSpec as P

HALO = 16
CAP = 16


sigma_fractions = (0.09375, 0.1875, 0.375)
term_powers = [(degree - power_v, power_v) for degree in range(5) for power_v in range(degree + 1)]


def from_behind(array, axis, by):
    length = lax.axis_size(axis)
    pairs = [(i, i + by) for i in range(length) if 0 <= i + by < length]
    return lax.ppermute(array, axis, pairs)


def with_halo(block, sides, width):
    for axis, dim in sides:
        count = lax.axis_size(axis)
        forward = [(i, i + 1) for i in range(count - 1)]
        backward = [(target, source) for source, target in forward]
        low = lax.ppermute(
            lax.slice_in_dim(block, block.shape[dim] - width, None, axis=dim), axis, forward
        )
        high = lax.ppermute(lax.slice_in_dim(block, 0, width, axis=dim), axis, backward)
        block = jnp.concatenate([low, block, high], axis=dim)
    return block


def gauss_taps():
    positions = jnp.arange(-HALO, HALO + 1).astype(jnp.float32)
    stacked = []
    for fraction in sigma_fractions:
        sigma = fraction * HALO
        values = jnp.exp(-positions * positions / (2.0 * sigma * sigma))
        stacked.append(values / jnp.sum(values))
    return jnp.stack(stacked).astype(jnp.bfloat16)


def spatial_weight(coef_row, rows_coord, cols_coord):
    rows_pow = [jnp.ones_like(rows_coord)]
    cols_pow = [jnp.ones_like(cols_coord)]
    for degree in range(1, 5):
        rows_pow.append(rows_pow[-1] * rows_coord)
        cols_pow.append(cols_pow[-1] * cols_coord)
    running = jnp.zeros((rows_coord.shape[0], cols_coord.shape[0]), jnp.float32)
    for power_v in range(5):
        inner_sum = jnp.zeros_like(cols_coord)
        for power_u in range(5 - power_v):
            inner_sum = (
                inner_sum + coef_row[term_powers.index((power_u, power_v))] * cols_pow[power_u]
            )
        running = running + rows_pow[power_v][:, None] * inner_sum[None, :]
    return running


def banded(tap_row, out_count, widened):
    line = jnp.concatenate([tap_row, jnp.zeros((widened + 1 - tap_row.shape[0],), tap_row.dtype)])
    repeated = jnp.tile(line, out_count)[: out_count * widened]
    return repeated.reshape(out_count, widened)


def along_rows(piece_pair, offset_by):
    return from_behind((piece_pair[0], piece_pair[1]), "py", offset_by)


def along_cols(piece_pair, offset_by):
    return from_behind((piece_pair[0], piece_pair[1]), "px", offset_by)


def corner_rows(piece_pair, offset_by):
    return from_behind((piece_pair[0], piece_pair[1]), "py", offset_by)


def corner_cols(piece_pair, offset_by):
    return from_behind((piece_pair[0], piece_pair[1]), "px", offset_by)


def on_device(pieces, owner_map, offsets, template, coefficients):
    rows_total = lax.axis_size("py")
    cols_total = lax.axis_size("px")
    my_row = lax.axis_index("py")
    my_col = lax.axis_index("px")
    block_side = pieces.shape[1]
    tile_side = template.shape[0]
    blocks_side = tile_side // block_side
    step_row = owner_map // cols_total - my_row
    step_col = owner_map % cols_total - my_col
    bucket = 3 * (step_row + 1) + (step_col + 1)
    piece_order = jnp.arange(owner_map.shape[0], dtype=jnp.int32)
    earlier = (owner_map[:, None] == owner_map[None, :]) & (
        piece_order[:, None] > piece_order[None, :]
    )
    position = jnp.sum(earlier.astype(jnp.int32), axis=1)
    slot_index = bucket * CAP + position
    outgoing = jnp.zeros((9 * CAP, block_side, block_side), jnp.bfloat16).at[slot_index].set(pieces)
    outgoing = outgoing.reshape(3, 3, CAP, block_side, block_side)
    labels = jnp.zeros((9 * CAP,), jnp.int32).at[slot_index].set(offsets + 1).reshape(3, 3, CAP)
    collected = [(outgoing[1, 1], labels[1, 1])]
    collected.append(along_rows((outgoing[2, 1], labels[2, 1]), 1))
    collected.append(along_rows((outgoing[0, 1], labels[0, 1]), -1))
    collected.append(along_cols((outgoing[1, 2], labels[1, 2]), 1))
    collected.append(along_cols((outgoing[1, 0], labels[1, 0]), -1))
    for row_pick, col_pick in ((2, 2), (2, 0), (0, 2), (0, 0)):
        moved = corner_rows(
            (outgoing[row_pick, col_pick], labels[row_pick, col_pick]), row_pick - 1
        )
        collected.append(corner_cols((moved[0], moved[1]), col_pick - 1))
    slot_pieces = jnp.stack([entry[0] for entry in collected])
    slot_labels = jnp.stack([entry[1] for entry in collected])
    received = slot_pieces.reshape(-1, block_side * block_side)
    received_labels = slot_labels.reshape(-1)
    block_ids = jnp.arange(blocks_side * blocks_side, dtype=jnp.int32) + 1
    selector = received_labels[None, :] == block_ids[:, None]
    block_sums = jnp.dot(
        selector.astype(jnp.bfloat16), received, preferred_element_type=jnp.float32
    )
    coverage = jnp.sum(selector.astype(jnp.float32), axis=1)
    science = block_sums / jnp.maximum(coverage, 1.0)[:, None]
    science = (
        science.reshape(blocks_side, blocks_side, block_side, block_side)
        .transpose(0, 2, 1, 3)
        .reshape(tile_side, tile_side)
    )
    padded = with_halo(template, (("py", 0), ("px", 1)), HALO)
    widened = tile_side + 2 * HALO
    taps = gauss_taps()
    band_tables = [
        banded(taps[basis_index], tile_side, widened) for basis_index in range(len(sigma_fractions))
    ]
    stacked_bands = jnp.concatenate(band_tables, axis=0)
    across_all = lax.dot_general(
        padded, stacked_bands, (((1,), (1,)), ((), ())), preferred_element_type=jnp.float32
    ).astype(jnp.bfloat16)
    rows_coord = (
        (my_row * tile_side + jnp.arange(tile_side, dtype=jnp.int32)).astype(jnp.float32) + 0.5
    ) * (2.0 / (tile_side * rows_total)) - 1.0
    cols_coord = (
        (my_col * tile_side + jnp.arange(tile_side, dtype=jnp.int32)).astype(jnp.float32) + 0.5
    ) * (2.0 / (tile_side * cols_total)) - 1.0
    matched = jnp.zeros((tile_side, tile_side), jnp.float32)
    for basis_index in range(len(sigma_fractions)):
        across_part = across_all[:, basis_index * tile_side : (basis_index + 1) * tile_side]
        smoothed = jnp.dot(
            band_tables[basis_index], across_part, preferred_element_type=jnp.float32
        )
        matched = (
            matched + spatial_weight(coefficients[basis_index], rows_coord, cols_coord) * smoothed
        )
    return science - matched


def solution(mesh):
    in_specs = (P(("py", "px"), None, None), P(("py", "px")), P(("py", "px")), P("py", "px"), P())
    out_specs = P("py", "px")
    return jax.shard_map(
        on_device, mesh=mesh, in_specs=in_specs, out_specs=out_specs, check_vma=False
    )
```

profile of v0, /device:TPU:1, one launch (start us, length us, event | category | flops | bytes accessed | tf_op | source)
XLA Modules:
  0.0 263.8 jit_solution(14447199516536210130)
XLA Ops:
  1.7 3.3 %broadcast_in_dim.8 = bf16[144,128,128]{2,1,0:T(8,128)(2,1)} broadcast(bf16[]{:T(256)} %constant.63.clone.1), dimensions={} | broadcast | bytes 4718594 | tf_op jit(solution)/shard_map/broadcast_in_dim | solution.py:99
  5.0 8.6 %scatter_fusion = bf16[144,128,128]{2,1,0:T(8,128)(2,1)} fusion(bf16[144,128,128]{2,1,0:T(8,128)(2,1)} %broadcast_in_dim.8, s32[64]{0:T(128)S(1)} %get-tuple-element.71, bf16[64,128,128]{2,1,0:T(8,128)(2,1)S(1)} %copy-done.3), kind=kCustom, calls=%fused_computation.1 | custom fusion | bytes 6291712 | tf_op jit(solution)/shard_map/scatter | solution.py:99
  13.6 4.1 %slice_bitcast_fusion = (bf16[16,128,128]{2,1,0:T(8,128)(2,1)S(1)}, bf16[16,128,128]{2,1,0:T(8,128)(2,1)}, bf16[16,128,128]{2,1,0:T(8,128)(2,1)}, bf16[16,128,12...) fusion(bf16[3,3,16,128,128]{4,3,2,1,0:T(8,128)(2,1)} %bitcast.130), kind=kLoop, calls=%fused_computation.18 | loop fusion | bytes 8388608 | tf_op jit(solution)/shard_map/squeeze | solution.py:109
  17.7 4.5 %collective-permute-start.12 = (bf16[16,128,128]{2,1,0:T(8,128)(2,1)}, bf16[16,128,128]{2,1,0:T(8,128)(2,1)}, u32[]{:S(2)}, u32[]{:S(2)}) collective-permute-start(bf16[16,128,128]{2,1,0:T(8,128)(2,1)} %get-tuple-element.12), channel_id=1, source_target_pairs={{0,8},{8,16},{16,24},{1,9},{9,17},{17,25},{2,10},{10,18},{18,26},{... | collective-permute-start | bytes 1572872 | tf_op jit(solution)/shard_map/ppermute | solution.py:17
  22.2 1.9 collective-permute-start.13
  24.1 3.9 %collective-permute-start.14 = (bf16[16,128,128]{2,1,0:T(8,128)(2,1)}, bf16[16,128,128]{2,1,0:T(8,128)(2,1)}, u32[]{:S(2)}, u32[]{:S(2)}) collective-permute-start(bf16[16,128,128]{2,1,0:T(8,128)(2,1)} %get-tuple-element.10), channel_id=1, source_target_pairs={{0,1},{1,2},{2,3},{3,4},{4,5},{5,6},{6,7},{8,9},{9,10},{10,11},{11... | collective-permute-start | bytes 1572872 | tf_op jit(solution)/shard_map/ppermute | solution.py:17
  28.9 3.9 %collective-permute-start = (s32[16]{0:T(128)S(1)}, s32[16]{0:T(128)S(1)}, u32[]{:S(2)}, u32[]{:S(2)}) collective-permute-start(s32[16]{0:T(128)S(1)} %get-tuple-element.24), channel_id=1, source_target_pairs={{0,8},{8,16},{16,24},{1,9},{9,17},{17,25},{2,10},{10,18},{18,26},{... | collective-permute-start | bytes 200 | tf_op jit(solution)/shard_map/ppermute | solution.py:17
  32.8 1.9 collective-permute-start.1
  34.8 1.9 fusion.15
  41.6 4.5 %tile.30 = bf16[1082368]{0:T(1024)(128)(2,1)} reshape(bf16[1024,1057]{1,0:T(8,128)(2,1)S(1)} %tile.14) | data formatting | bytes 4329472 | tf_op jit(solution)/shard_map/tile | solution.py:62
  47.7 4.0 %reshape.288 = bf16[1024,1056]{1,0:T(8,128)(2,1)} reshape(bf16[1081344]{0:T(1024)(128)(2,1)S(1)} %slice-done) | data formatting | bytes 4325376 | tf_op jit(solution)/shard_map/reshape | solution.py:63
  53.4 4.5 %tile.32 = bf16[1082368]{0:T(1024)(128)(2,1)} reshape(bf16[1024,1057]{1,0:T(8,128)(2,1)S(1)} %tile.31) | data formatting | bytes 4329472 | tf_op jit(solution)/shard_map/tile | solution.py:62
  59.5 4.0 %reshape.289 = bf16[1024,1056]{1,0:T(8,128)(2,1)} reshape(bf16[1081344]{0:T(1024)(128)(2,1)S(1)} %slice-done.1) | data formatting | bytes 4325376 | tf_op jit(solution)/shard_map/reshape | solution.py:63
  64.4 4.5 %tile.13 = bf16[1082368]{0:T(1024)(128)(2,1)} reshape(bf16[1024,1057]{1,0:T(8,128)(2,1)S(1)} %tile.12) | data formatting | bytes 4329472 | tf_op jit(solution)/shard_map/tile | solution.py:62
  70.8 3.1 %multiply_add_fusion = (f32[1024]{0:T(1024)S(1)}, f32[1024]{0:T(1024)S(1)}) fusion(f32[]{:T(128)} %bitcast.83, f32[]{:T(128)} %bitcast.82, s32[]{:T(128)S(6)} %mul.731, f32[]{:T(128)} %bitcast.81, f32[]{:T(128)} %bitcast.80, f32[]{:T(128)} %bitcast.79), kind=kLoop, calls=%fused_computation.47 | loop fusion | flops 12288 | bytes 8216 | tf_op jit(solution)/shard_map/add | solution.py:54
  73.9 3.0 %multiply_add_fusion.4 = (f32[1024]{0:T(1024)S(1)}, f32[1024]{0:T(1024)S(1)}) fusion(f32[]{:T(128)} %bitcast.68, f32[]{:T(128)} %bitcast.67, s32[]{:T(128)S(6)} %mul.731, f32[]{:T(128)} %bitcast.66, f32[]{:T(128)} %bitcast.65, f32[]{:T(128)} %bitcast.64), kind=kLoop, calls=%fused_computation.51 | loop fusion | flops 12288 | bytes 8216 | tf_op jit(solution)/shard_map/add | solution.py:54
  76.9 3.3 %multiply_add_fusion.8 = (f32[1024]{0:T(1024)S(1)}, f32[1024]{0:T(1024)S(1)}) fusion(f32[]{:T(128)} %bitcast.50, f32[]{:T(128)} %bitcast.49, s32[]{:T(128)S(6)} %mul.731, f32[]{:T(128)} %bitcast.48, f32[]{:T(128)} %bitcast.47, f32[]{:T(128)} %bitcast.46), kind=kLoop, calls=%fused_computation.55 | loop fusion | flops 12288 | bytes 8216 | tf_op jit(solution)/shard_map/add | solution.py:54
  80.2 5.5 %multiply_add_fusion.2 = (f32[1024]{0:T(1024)S(1)}, f32[1024]{0:T(1024)S(1)}) fusion(f32[]{:T(128)} %bitcast.78, f32[]{:T(128)} %bitcast.77, f32[]{:T(128)} %bitcast.76, f32[]{:T(128)} %bitcast.75, s32[]{:T(128)S(6)} %mul.731, f32[]{:T(128)} %bitcast.74, f32[]{:T(128)} %bitcast.73, f32[]{:T(128)} %bitcast.72, f32[]{:T(128)} %bitcast.71, f32[]{:T(128)} %bitcast.70), kind=kLoop, calls=%fused_computation.49 | loop fusion | flops 22528 | bytes 8232 | tf_op jit(solution)/shard_map/add | solution.py:54
  85.7 5.7 %multiply_add_fusion.6 = (f32[1024]{0:T(1024)S(1)}, f32[1024]{0:T(1024)S(1)}) fusion(f32[]{:T(128)} %bitcast.63, f32[]{:T(128)} %bitcast.62, f32[]{:T(128)} %bitcast.61, f32[]{:T(128)} %bitcast.60, s32[]{:T(128)S(6)} %mul.731, f32[]{:T(128)} %bitcast.59, f32[]{:T(128)} %bitcast.58, f32[]{:T(128)} %bitcast.57, f32[]{:T(128)} %bitcast.56, f32[]{:T(128)} %bitcast.55), kind=kLoop, calls=%fused_computation.53 | loop fusion | flops 22528 | bytes 8232 | tf_op jit(solution)/shard_map/add | solution.py:54
  91.4 5.8 %multiply_add_fusion.10 = (f32[1024]{0:T(1024)S(1)}, f32[1024]{0:T(1024)S(1)}) fusion(f32[]{:T(128)} %bitcast.45, f32[]{:T(128)} %bitcast.44, f32[]{:T(128)} %bitcast.43, f32[]{:T(128)} %bitcast.42, s32[]{:T(128)S(6)} %mul.731, f32[]{:T(128)} %bitcast.41, f32[]{:T(128)} %bitcast.40, f32[]{:T(128)} %bitcast.39, f32[]{:T(128)} %bitcast.38, f32[]{:T(128)} %bitcast.37), kind=kLoop, calls=%fused_computation.57 | loop fusion | flops 22528 | bytes 8232 | tf_op jit(solution)/shard_map/add | solution.py:54
  97.2 4.1 %reshape.287 = bf16[1024,1056]{1,0:T(8,128)(2,1)} reshape(bf16[1081344]{0:T(1024)(128)(2,1)S(1)} %slice-done.2) | data formatting | bytes 4325376 | tf_op jit(solution)/shard_map/reshape | solution.py:63
  101.3 2.4 collective-permute-start.2
  105.0 3.9 %collective-permute-start.4 = (s32[16]{0:T(128)S(1)}, s32[16]{0:T(128)S(1)}, u32[]{:S(2)}, u32[]{:S(2)}) collective-permute-start(s32[16]{0:T(128)S(1)} %get-tuple-element.20), channel_id=1, source_target_pairs={{0,8},{8,16},{16,24},{1,9},{9,17},{17,25},{2,10},{10,18},{18,26},{... | collective-permute-start | bytes 200 | tf_op jit(solution)/shard_map/ppermute | solution.py:17
  109.0 4.1 %collective-permute-start.6 = (s32[16]{0:T(128)S(1)}, s32[16]{0:T(128)S(1)}, u32[]{:S(2)}, u32[]{:S(2)}) collective-permute-start(s32[16]{0:T(128)S(1)} %get-tuple-element.19), channel_id=1, source_target_pairs={{0,8},{8,16},{16,24},{1,9},{9,17},{17,25},{2,10},{10,18},{18,26},{... | collective-permute-start | bytes 200 | tf_op jit(solution)/shard_map/ppermute | solution.py:17
  113.1 1.9 collective-permute-start.8
  115.0 1.9 collective-permute-start.10
  117.9 4.0 %collective-permute-start.5 = (s32[16]{0:T(128)S(1)}, s32[16]{0:T(128)S(1)}, u32[]{:S(2)}, u32[]{:S(2)}) collective-permute-start(s32[16]{0:T(128)S(1)} %collective-permute-done.4), channel_id=1, source_target_pairs={{0,1},{1,2},{2,3},{3,4},{4,5},{5,6},{6,7},{8,9},{9,10},{10,11},{11... | collective-permute-start | bytes 200 | tf_op jit(solution)/shard_map/ppermute | solution.py:17
  123.3 4.0 %collective-permute-start.9 = (s32[16]{0:T(128)S(1)}, s32[16]{0:T(128)S(1)}, u32[]{:S(2)}, u32[]{:S(2)}) collective-permute-start(s32[16]{0:T(128)S(1)} %collective-permute-done.8), channel_id=1, source_target_pairs={{0,1},{1,2},{2,3},{3,4},{4,5},{5,6},{6,7},{8,9},{9,10},{10,11},{11... | collective-permute-start | bytes 200 | tf_op jit(solution)/shard_map/ppermute | solution.py:17
  128.6 3.5 %collective-permute-start.24 = (bf16[16,1024]{1,0:T(8,128)(2,1)S(1)}, bf16[16,1024]{1,0:T(8,128)(2,1)S(1)}, u32[]{:S(2)}, u32[]{:S(2)}) collective-permute-start(bf16[16,1024]{1,0:T(8,128)(2,1)S(1)} %get-tuple-element.16), channel_id=1, source_target_pairs={{0,8},{8,16},{16,24},{1,9},{9,17},{17,25},{2,10},{10,18},{18,26},{... | collective-permute-start | bytes 98312 | tf_op jit(solution)/shard_map/ppermute | solution.py:25
  132.1 1.9 collective-permute-start.25
  134.4 1.8 constant_dynamic-update-slice_fusion.1
  136.1 1.7 collective-permute-done.25
  138.0 5.1 %collective-permute-start.26 = (bf16[1056,16]{1,0:T(8,128)(2,1)S(1)}, bf16[1056,16]{1,0:T(8,128)(2,1)}, u32[]{:S(2)}, u32[]{:S(2)}) collective-permute-start(bf16[1056,16]{1,0:T(8,128)(2,1)S(1)} %get-tuple-element.14), channel_id=1, source_target_pairs={{0,1},{1,2},{2,3},{3,4},{4,5},{5,6},{6,7},{8,9},{9,10},{10,11},{11... | collective-permute-start | bytes 101384 | tf_op jit(solution)/shard_map/ppermute | solution.py:25
  144.4 2.1 collective-permute-done.26
  146.4 10.8 %collective-permute-start.16 = (bf16[16,128,128]{2,1,0:T(8,128)(2,1)}, bf16[16,128,128]{2,1,0:T(8,128)(2,1)}, u32[]{:S(2)}, u32[]{:S(2)}) collective-permute-start(bf16[16,128,128]{2,1,0:T(8,128)(2,1)} %get-tuple-element.8), channel_id=1, source_target_pairs={{0,8},{8,16},{16,24},{1,9},{9,17},{17,25},{2,10},{10,18},{18,26},{... | collective-permute-start | bytes 1572872 | tf_op jit(solution)/shard_map/ppermute | solution.py:17
  157.3 1.9 collective-permute-start.18
  159.2 5.2 %concatenate.20 = bf16[1056,1056]{1,0:T(8,128)(2,1)} concatenate(bf16[1056,16]{1,0:T(8,128)(2,1)} %collective-permute-done.26, bf16[1056,1024]{1,0:T(8,128)(2,1)S(1)} %constant_dynamic-update-slice_fusion, bf16[1056,16]{1,0:T(8,128)(2,1)} %collective-permute-done.27), dimensions={1} | concatenate | bytes 4460544 | tf_op jit(solution)/shard_map/concatenate | solution.py:29
  164.4 14.0 %convolution_convert_fusion = bf16[1056,3072]{1,0:T(8,128)(2,1)} fusion(bf16[1056,1056]{1,0:T(8,128)(2,1)} %concatenate.20, bf16[1024,1056]{1,0:T(8,128)(2,1)} %reshape.289, bf16[1024,1056]{1,0:T(8,128)(2,1)} %reshape.288, bf16[1024,1056]{1,0:T(8,128)(2,1)} %reshape.287), kind=kOutput, calls=%fused_computation.3 | convolution fusion | flops 6874103808 | bytes 15206400 | tf_op jit(solution)/shard_map/dot_general | solution.py:135
  178.4 4.6 %fusion.11 = f32[1024,1024]{1,0:T(8,128)S(1)} fusion(bf16[1024,1056]{1,0:T(8,128)(2,1)S(1)} %copy-done.1, bf16[1056,3072]{1,0:T(8,128)(2,1)} %convolution_convert_fusion), kind=kOutput, calls=%fused_computation.14 | convolution fusion | flops 2214592512 | bytes 8519680 | tf_op jit(solution)/shard_map/dot_general | solution.py:147
  183.1 3.2 %collective-permute-start.20 = (bf16[16,128,128]{2,1,0:T(8,128)(2,1)S(1)}, bf16[16,128,128]{2,1,0:T(8,128)(2,1)S(1)}, u32[]{:S(2)}, u32[]{:S(2)}) collective-permute-start(bf16[16,128,128]{2,1,0:T(8,128)(2,1)S(1)} %copy-done.4), channel_id=1, source_target_pairs={{8,0},{16,8},{24,16},{9,1},{17,9},{25,17},{10,2},{18,10},{26,18},{... | collective-permute-start | bytes 1572872 | tf_op jit(solution)/shard_map/ppermute | solution.py:17
  186.3 2.2 collective-permute-start.22
  188.5 2.9 %fusion.13 = f32[1024,1024]{1,0:T(8,128)S(1)} fusion(bf16[1024,1056]{1,0:T(8,128)(2,1)S(1)} %copy-done.2, bf16[1056,3072]{1,0:T(8,128)(2,1)S(1)} %copy-done.6), kind=kOutput, calls=%fused_computation.16 | convolution fusion | flops 2214592512 | bytes 8716288 | tf_op jit(solution)/shard_map/dot_general | solution.py:147
  193.9 4.9 %collective-permute-start.17 = (bf16[16,128,128]{2,1,0:T(8,128)(2,1)}, bf16[16,128,128]{2,1,0:T(8,128)(2,1)S(1)}, u32[]{:S(2)}, u32[]{:S(2)}) collective-permute-start(bf16[16,128,128]{2,1,0:T(8,128)(2,1)} %collective-permute-done.16), channel_id=1, source_target_pairs={{0,1},{1,2},{2,3},{3,4},{4,5},{5,6},{6,7},{8,9},{9,10},{10,11},{11... | collective-permute-start | bytes 1572872 | tf_op jit(solution)/shard_map/ppermute | solution.py:17
  201.2 4.9 %collective-permute-start.21 = (bf16[16,128,128]{2,1,0:T(8,128)(2,1)S(1)}, bf16[16,128,128]{2,1,0:T(8,128)(2,1)S(1)}, u32[]{:S(2)}, u32[]{:S(2)}) collective-permute-start(bf16[16,128,128]{2,1,0:T(8,128)(2,1)S(1)} %collective-permute-done.20), channel_id=1, source_target_pairs={{0,1},{1,2},{2,3},{3,4},{4,5},{5,6},{6,7},{8,9},{9,10},{10,11},{11... | collective-permute-start | bytes 1572872 | tf_op jit(solution)/shard_map/ppermute | solution.py:17
  208.9 32.5 %collective-permute-done.17 = bf16[16,128,128]{2,1,0:T(8,128)(2,1)S(1)} collective-permute-done((bf16[16,128,128]{2,1,0:T(8,128)(2,1)}, bf16[16,128,128]{2,1,0:T(8,128)(2,1)S(1)}, u32[]{:S(2)}, u32[]{:S(2)}) %collective-permute-start.17) | collective-permute-done | bytes 524320 | tf_op jit(solution)/shard_map/ppermute | solution.py:17
  241.5 10.9 %collective-permute-done.21 = bf16[16,128,128]{2,1,0:T(8,128)(2,1)S(1)} collective-permute-done((bf16[16,128,128]{2,1,0:T(8,128)(2,1)S(1)}, bf16[16,128,128]{2,1,0:T(8,128)(2,1)S(1)}, u32[]{:S(2)}, u32[]{:S(2)}) %collective-permute-start.21) | collective-permute-done | bytes 524320 | tf_op jit(solution)/shard_map/ppermute | solution.py:17
  252.7 3.2 %convolution_divide_fusion = f32[64,16384]{1,0:T(8,128)S(1)} fusion(bf16[18,8,128,128]{3,2,1,0:T(8,128)(2,1)S(1)} %bitcast.134, f32[64]{0:T(128)S(1)} %broadcast_maximum_fusion, s32[144]{0:T(256)S(1)} %eq.33, s32[64]{0:T(128)S(1)} %iota_add_fusion), kind=kOutput, calls=%fused_computation.2 | convolution fusion | flops 303047680 | bytes 8913984 | tf_op jit(solution)/shard_map/dot_general | solution.py:118
  255.9 7.9 %bitcast_subtract_fusion = f32[1024,1024]{1,0:T(8,128)} fusion(f32[128,8,8,128]{3,2,1,0:T(8,128)S(1)} %bitcast.143, f32[1024,1024]{1,0:T(8,128)S(1)} %fusion.11, f32[1024,1024]{1,0:T(8,128)S(1)} %fusion.13, bf16[1024,1056]{1,0:T(8,128)(2,1)S(1)} %copy-done, bf16[1056,3072]{1,0:T(8,128)(2,1)S(1)} %copy-done.6, f32[1024]{0:T(1024)S(1)} %get-tuple-element.76, ...), kind=kOutput, calls=%fused_computation.11 | convolution fusion | flops 2242904064 | bytes 21372928 | tf_op jit(solution)/shard_map/dot_general | solution.py:147
  (96 shorter events, 29.7 us)
Async XLA Ops:
  0.0 5.0 %copy-start.3 = (bf16[64,128,128]{2,1,0:T(8,128)(2,1)S(1)}, bf16[64,128,128]{2,1,0:T(8,128)(2,1)}, u32[]{:S(2)}) copy-start(bf16[64,128,128]{2,1,0:T(8,128)(2,1)} %param.5) | copy-start | bytes 6291460
  13.6 25.0 %copy-start.5 = (f32[3,15]{1,0:T(4,128)S(1)}, f32[3,15]{1,0:T(4,128)}, u32[]{:S(2)}) copy-start(f32[3,15]{1,0:T(4,128)} %param.9) | copy-start | bytes 544
  17.7 165.4 %collective-permute-start.12 = (bf16[16,128,128]{2,1,0:T(8,128)(2,1)}, bf16[16,128,128]{2,1,0:T(8,128)(2,1)}, u32[]{:S(2)}, u32[]{:S(2)}) collective-permute-start(bf16[16,128,128]{2,1,0:T(8,128)(2,1)} %get-tuple-element.12), channel_id=1, source_target_pairs={{0,8},{8,16},{16,24},{1,9},{9,17},{17,25},{2,10},{10,18},{18,26},{... | collective-permute-start | bytes 1572872 | tf_op jit(solution)/shard_map/ppermute | solution.py:17
  22.2 164.1 %collective-permute-start.13 = (bf16[16,128,128]{2,1,0:T(8,128)(2,1)}, bf16[16,128,128]{2,1,0:T(8,128)(2,1)}, u32[]{:S(2)}, u32[]{:S(2)}) collective-permute-start(bf16[16,128,128]{2,1,0:T(8,128)(2,1)} %get-tuple-element.11), channel_id=1, source_target_pairs={{8,0},{16,8},{24,16},{9,1},{17,9},{25,17},{10,2},{18,10},{26,18},{... | collective-permute-start | bytes 1572872 | tf_op jit(solution)/shard_map/ppermute | solution.py:17
  24.1 167.3 %collective-permute-start.14 = (bf16[16,128,128]{2,1,0:T(8,128)(2,1)}, bf16[16,128,128]{2,1,0:T(8,128)(2,1)}, u32[]{:S(2)}, u32[]{:S(2)}) collective-permute-start(bf16[16,128,128]{2,1,0:T(8,128)(2,1)} %get-tuple-element.10), channel_id=1, source_target_pairs={{0,1},{1,2},{2,3},{3,4},{4,5},{5,6},{6,7},{8,9},{9,10},{10,11},{11... | collective-permute-start | bytes 1572872 | tf_op jit(solution)/shard_map/ppermute | solution.py:17
  28.9 72.4 %collective-permute-start = (s32[16]{0:T(128)S(1)}, s32[16]{0:T(128)S(1)}, u32[]{:S(2)}, u32[]{:S(2)}) collective-permute-start(s32[16]{0:T(128)S(1)} %get-tuple-element.24), channel_id=1, source_target_pairs={{0,8},{8,16},{16,24},{1,9},{9,17},{17,25},{2,10},{10,18},{18,26},{... | collective-permute-start | bytes 200 | tf_op jit(solution)/shard_map/ppermute | solution.py:17
  32.8 70.9 %collective-permute-start.1 = (s32[16]{0:T(128)S(1)}, s32[16]{0:T(128)S(1)}, u32[]{:S(2)}, u32[]{:S(2)}) collective-permute-start(s32[16]{0:T(128)S(1)} %get-tuple-element.23), channel_id=1, source_target_pairs={{8,0},{16,8},{24,16},{9,1},{17,9},{25,17},{10,2},{18,10},{26,18},{... | collective-permute-start | bytes 200 | tf_op jit(solution)/shard_map/ppermute | solution.py:17
  46.1 1.6 slice-start
  57.9 1.6 slice-start.1
  68.9 28.3 %slice-start.2 = ((bf16[1082368]{0:T(1024)(128)(2,1)}), bf16[1081344]{0:T(1024)(128)(2,1)S(1)}, s32[]{:S(2)}) async-start(bf16[1082368]{0:T(1024)(128)(2,1)} %tile.13), calls=%async_computation.2 | async-start | bytes 4325376 | tf_op jit(solution)/shard_map/slice | solution.py:62
  101.3 3.7 %collective-permute-start.2 = (s32[16]{0:T(128)S(1)}, s32[16]{0:T(128)S(1)}, u32[]{:S(2)}, u32[]{:S(2)}) collective-permute-start(s32[16]{0:T(128)S(1)} %get-tuple-element.22), channel_id=1, source_target_pairs={{0,1},{1,2},{2,3},{3,4},{4,5},{5,6},{6,7},{8,9},{9,10},{10,11},{11... | collective-permute-start | bytes 200 | tf_op jit(solution)/shard_map/ppermute | solution.py:17
  103.7 5.2 %collective-permute-start.3 = (s32[16]{0:T(128)S(1)}, s32[16]{0:T(128)S(1)}, u32[]{:S(2)}, u32[]{:S(2)}) collective-permute-start(s32[16]{0:T(128)S(1)} %get-tuple-element.21), channel_id=1, source_target_pairs={{1,0},{2,1},{3,2},{4,3},{5,4},{6,5},{7,6},{9,8},{10,9},{11,10},{12... | collective-permute-start | bytes 200 | tf_op jit(solution)/shard_map/ppermute | solution.py:17
  105.0 8.0 %collective-permute-start.4 = (s32[16]{0:T(128)S(1)}, s32[16]{0:T(128)S(1)}, u32[]{:S(2)}, u32[]{:S(2)}) collective-permute-start(s32[16]{0:T(128)S(1)} %get-tuple-element.20), channel_id=1, source_target_pairs={{0,8},{8,16},{16,24},{1,9},{9,17},{17,25},{2,10},{10,18},{18,26},{... | collective-permute-start | bytes 200 | tf_op jit(solution)/shard_map/ppermute | solution.py:17
  109.0 6.0 %collective-permute-start.6 = (s32[16]{0:T(128)S(1)}, s32[16]{0:T(128)S(1)}, u32[]{:S(2)}, u32[]{:S(2)}) collective-permute-start(s32[16]{0:T(128)S(1)} %get-tuple-element.19), channel_id=1, source_target_pairs={{0,8},{8,16},{16,24},{1,9},{9,17},{17,25},{2,10},{10,18},{18,26},{... | collective-permute-start | bytes 200 | tf_op jit(solution)/shard_map/ppermute | solution.py:17
  113.1 4.9 %collective-permute-start.8 = (s32[16]{0:T(128)S(1)}, s32[16]{0:T(128)S(1)}, u32[]{:S(2)}, u32[]{:S(2)}) collective-permute-start(s32[16]{0:T(128)S(1)} %get-tuple-element.18), channel_id=1, source_target_pairs={{8,0},{16,8},{24,16},{9,1},{17,9},{25,17},{10,2},{18,10},{26,18},{... | collective-permute-start | bytes 200 | tf_op jit(solution)/shard_map/ppermute | solution.py:17
  115.0 6.9 %collective-permute-start.10 = (s32[16]{0:T(128)S(1)}, s32[16]{0:T(128)S(1)}, u32[]{:S(2)}, u32[]{:S(2)}) collective-permute-start(s32[16]{0:T(128)S(1)} %get-tuple-element.17), channel_id=1, source_target_pairs={{8,0},{16,8},{24,16},{9,1},{17,9},{25,17},{10,2},{18,10},{26,18},{... | collective-permute-start | bytes 200 | tf_op jit(solution)/shard_map/ppermute | solution.py:17
  117.9 5.3 %collective-permute-start.5 = (s32[16]{0:T(128)S(1)}, s32[16]{0:T(128)S(1)}, u32[]{:S(2)}, u32[]{:S(2)}) collective-permute-start(s32[16]{0:T(128)S(1)} %collective-permute-done.4), channel_id=1, source_target_pairs={{0,1},{1,2},{2,3},{3,4},{4,5},{5,6},{6,7},{8,9},{9,10},{10,11},{11... | collective-permute-start | bytes 200 | tf_op jit(solution)/shard_map/ppermute | solution.py:17
  122.0 5.3 %collective-permute-start.7 = (s32[16]{0:T(128)S(1)}, s32[16]{0:T(128)S(1)}, u32[]{:S(2)}, u32[]{:S(2)}) collective-permute-start(s32[16]{0:T(128)S(1)} %collective-permute-done.6), channel_id=1, source_target_pairs={{1,0},{2,1},{3,2},{4,3},{5,4},{6,5},{7,6},{9,8},{10,9},{11,10},{12... | collective-permute-start | bytes 200 | tf_op jit(solution)/shard_map/ppermute | solution.py:17
  123.3 5.3 %collective-permute-start.9 = (s32[16]{0:T(128)S(1)}, s32[16]{0:T(128)S(1)}, u32[]{:S(2)}, u32[]{:S(2)}) collective-permute-start(s32[16]{0:T(128)S(1)} %collective-permute-done.8), channel_id=1, source_target_pairs={{0,1},{1,2},{2,3},{3,4},{4,5},{5,6},{6,7},{8,9},{9,10},{10,11},{11... | collective-permute-start | bytes 200 | tf_op jit(solution)/shard_map/ppermute | solution.py:17
  127.3 4.8 %collective-permute-start.11 = (s32[16]{0:T(128)S(1)}, s32[16]{0:T(128)S(1)}, u32[]{:S(2)}, u32[]{:S(2)}) collective-permute-start(s32[16]{0:T(128)S(1)} %collective-permute-done.10), channel_id=1, source_target_pairs={{1,0},{2,1},{3,2},{4,3},{5,4},{6,5},{7,6},{9,8},{10,9},{11,10},{12... | collective-permute-start | bytes 200 | tf_op jit(solution)/shard_map/ppermute | solution.py:17
  128.6 5.8 %collective-permute-start.24 = (bf16[16,1024]{1,0:T(8,128)(2,1)S(1)}, bf16[16,1024]{1,0:T(8,128)(2,1)S(1)}, u32[]{:S(2)}, u32[]{:S(2)}) collective-permute-start(bf16[16,1024]{1,0:T(8,128)(2,1)S(1)} %get-tuple-element.16), channel_id=1, source_target_pairs={{0,8},{8,16},{16,24},{1,9},{9,17},{17,25},{2,10},{10,18},{18,26},{... | collective-permute-start | bytes 98312 | tf_op jit(solution)/shard_map/ppermute | solution.py:25
  132.1 5.7 %collective-permute-start.25 = (bf16[16,1024]{1,0:T(8,128)(2,1)S(1)}, bf16[16,1024]{1,0:T(8,128)(2,1)S(1)}, u32[]{:S(2)}, u32[]{:S(2)}) collective-permute-start(bf16[16,1024]{1,0:T(8,128)(2,1)S(1)} %get-tuple-element.15), channel_id=1, source_target_pairs={{8,0},{16,8},{24,16},{9,1},{17,9},{25,17},{10,2},{18,10},{26,18},{... | collective-permute-start | bytes 98312 | tf_op jit(solution)/shard_map/ppermute | solution.py:28
  138.0 8.5 %collective-permute-start.26 = (bf16[1056,16]{1,0:T(8,128)(2,1)S(1)}, bf16[1056,16]{1,0:T(8,128)(2,1)}, u32[]{:S(2)}, u32[]{:S(2)}) collective-permute-start(bf16[1056,16]{1,0:T(8,128)(2,1)S(1)} %get-tuple-element.14), channel_id=1, source_target_pairs={{0,1},{1,2},{2,3},{3,4},{4,5},{5,6},{6,7},{8,9},{9,10},{10,11},{11... | collective-permute-start | bytes 101384 | tf_op jit(solution)/shard_map/ppermute | solution.py:25
  143.1 14.2 %collective-permute-start.27 = (bf16[1056,16]{1,0:T(8,128)(2,1)S(1)}, bf16[1056,16]{1,0:T(8,128)(2,1)}, u32[]{:S(2)}, u32[]{:S(2)}) collective-permute-start(bf16[1056,16]{1,0:T(8,128)(2,1)S(1)} %get-tuple-element.13), channel_id=1, source_target_pairs={{1,0},{2,1},{3,2},{4,3},{5,4},{6,5},{7,6},{9,8},{10,9},{11,10},{12... | collective-permute-start | bytes 101384 | tf_op jit(solution)/shard_map/ppermute | solution.py:28
  146.4 47.4 %collective-permute-start.16 = (bf16[16,128,128]{2,1,0:T(8,128)(2,1)}, bf16[16,128,128]{2,1,0:T(8,128)(2,1)}, u32[]{:S(2)}, u32[]{:S(2)}) collective-permute-start(bf16[16,128,128]{2,1,0:T(8,128)(2,1)} %get-tuple-element.8), channel_id=1, source_target_pairs={{0,8},{8,16},{16,24},{1,9},{9,17},{17,25},{2,10},{10,18},{18,26},{... | collective-permute-start | bytes 1572872 | tf_op jit(solution)/shard_map/ppermute | solution.py:17
  157.3 42.6 %collective-permute-start.18 = (bf16[16,128,128]{2,1,0:T(8,128)(2,1)}, bf16[16,128,128]{2,1,0:T(8,128)(2,1)}, u32[]{:S(2)}, u32[]{:S(2)}) collective-permute-start(bf16[16,128,128]{2,1,0:T(8,128)(2,1)} %get-tuple-element.7), channel_id=1, source_target_pairs={{0,8},{8,16},{16,24},{1,9},{9,17},{17,25},{2,10},{10,18},{18,26},{... | collective-permute-start | bytes 1572872 | tf_op jit(solution)/shard_map/ppermute | solution.py:17
  164.4 14.0 %copy-start.1 = (bf16[1024,1056]{1,0:T(8,128)(2,1)S(1)}, bf16[1024,1056]{1,0:T(8,128)(2,1)}, u32[]{:S(2)}) copy-start(bf16[1024,1056]{1,0:T(8,128)(2,1)} %reshape.288) | copy-start | bytes 6488068
  178.4 4.7 %copy-start.4 = (bf16[16,128,128]{2,1,0:T(8,128)(2,1)S(1)}, bf16[16,128,128]{2,1,0:T(8,128)(2,1)}, u32[]{:S(2)}) copy-start(bf16[16,128,128]{2,1,0:T(8,128)(2,1)} %get-tuple-element.6) | copy-start | bytes 1572868
  178.4 10.1 %copy-start.2 = (bf16[1024,1056]{1,0:T(8,128)(2,1)S(1)}, bf16[1024,1056]{1,0:T(8,128)(2,1)}, u32[]{:S(2)}) copy-start(bf16[1024,1056]{1,0:T(8,128)(2,1)} %reshape.287) | copy-start | bytes 6488068
  178.4 10.1 %copy-start.6 = (bf16[1056,3072]{1,0:T(8,128)(2,1)S(1)}, bf16[1056,3072]{1,0:T(8,128)(2,1)}, u32[]{:S(2)}) copy-start(bf16[1056,3072]{1,0:T(8,128)(2,1)} %convolution_convert_fusion) | copy-start | bytes 19464196
  183.1 18.1 %collective-permute-start.20 = (bf16[16,128,128]{2,1,0:T(8,128)(2,1)S(1)}, bf16[16,128,128]{2,1,0:T(8,128)(2,1)S(1)}, u32[]{:S(2)}, u32[]{:S(2)}) collective-permute-start(bf16[16,128,128]{2,1,0:T(8,128)(2,1)S(1)} %copy-done.4), channel_id=1, source_target_pairs={{8,0},{16,8},{24,16},{9,1},{17,9},{25,17},{10,2},{18,10},{26,18},{... | collective-permute-start | bytes 1572872 | tf_op jit(solution)/shard_map/ppermute | solution.py:17
  186.3 6.4 %slice-start.3 = ((s8[4718592]{0:T(1024)(128)(4,1)}), s8[4194304]{0:T(1024)(128)(4,1)S(1)}, s32[]{:S(2)}) async-start(s8[4718592]{0:T(1024)(128)(4,1)} %bitcast.132), calls=%async_computation.3 | async-start | bytes 8388608
  186.3 6.4 %slice-start.4 = ((s8[4718592]{0:T(1024)(128)(4,1)}), s8[524288]{0:T(1024)(128)(4,1)S(1)}, s32[]{:S(2)}) async-start(s8[4718592]{0:T(1024)(128)(4,1)} %bitcast.132), calls=%async_computation.4 | async-start | bytes 1048576
  186.3 19.8 %collective-permute-start.22 = (bf16[16,128,128]{2,1,0:T(8,128)(2,1)S(1)}, bf16[16,128,128]{2,1,0:T(8,128)(2,1)S(1)}, u32[]{:S(2)}, u32[]{:S(2)}) collective-permute-start(bf16[16,128,128]{2,1,0:T(8,128)(2,1)S(1)} %get-tuple-element.5), channel_id=1, source_target_pairs={{8,0},{16,8},{24,16},{9,1},{17,9},{25,17},{10,2},{18,10},{26,18},{... | collective-permute-start | bytes 1572872 | tf_op jit(solution)/shard_map/ppermute | solution.py:17
  191.4 17.4 %collective-permute-start.15 = (bf16[16,128,128]{2,1,0:T(8,128)(2,1)S(1)}, bf16[16,128,128]{2,1,0:T(8,128)(2,1)S(1)}, u32[]{:S(2)}, u32[]{:S(2)}) collective-permute-start(bf16[16,128,128]{2,1,0:T(8,128)(2,1)S(1)} %get-tuple-element.9), channel_id=1, source_target_pairs={{1,0},{2,1},{3,2},{4,3},{5,4},{6,5},{7,6},{9,8},{10,9},{11,10},{12... | collective-permute-start | bytes 1572872 | tf_op jit(solution)/shard_map/ppermute | solution.py:17
  193.9 47.5 %collective-permute-start.17 = (bf16[16,128,128]{2,1,0:T(8,128)(2,1)}, bf16[16,128,128]{2,1,0:T(8,128)(2,1)S(1)}, u32[]{:S(2)}, u32[]{:S(2)}) collective-permute-start(bf16[16,128,128]{2,1,0:T(8,128)(2,1)} %collective-permute-done.16), channel_id=1, source_target_pairs={{0,1},{1,2},{2,3},{3,4},{4,5},{5,6},{6,7},{8,9},{9,10},{10,11},{11... | collective-permute-start | bytes 1572872 | tf_op jit(solution)/shard_map/ppermute | solution.py:17
  199.9 41.5 %collective-permute-start.19 = (bf16[16,128,128]{2,1,0:T(8,128)(2,1)}, bf16[16,128,128]{2,1,0:T(8,128)(2,1)S(1)}, u32[]{:S(2)}, u32[]{:S(2)}) collective-permute-start(bf16[16,128,128]{2,1,0:T(8,128)(2,1)} %collective-permute-done.18), channel_id=1, source_target_pairs={{1,0},{2,1},{3,2},{4,3},{5,4},{6,5},{7,6},{9,8},{10,9},{11,10},{12... | collective-permute-start | bytes 1572872 | tf_op jit(solution)/shard_map/ppermute | solution.py:17
  201.2 51.3 %collective-permute-start.21 = (bf16[16,128,128]{2,1,0:T(8,128)(2,1)S(1)}, bf16[16,128,128]{2,1,0:T(8,128)(2,1)S(1)}, u32[]{:S(2)}, u32[]{:S(2)}) collective-permute-start(bf16[16,128,128]{2,1,0:T(8,128)(2,1)S(1)} %collective-permute-done.20), channel_id=1, source_target_pairs={{0,1},{1,2},{2,3},{3,4},{4,5},{5,6},{6,7},{8,9},{9,10},{10,11},{11... | collective-permute-start | bytes 1572872 | tf_op jit(solution)/shard_map/ppermute | solution.py:17
  206.1 46.5 %collective-permute-start.23 = (bf16[16,128,128]{2,1,0:T(8,128)(2,1)S(1)}, bf16[16,128,128]{2,1,0:T(8,128)(2,1)S(1)}, u32[]{:S(2)}, u32[]{:S(2)}) collective-permute-start(bf16[16,128,128]{2,1,0:T(8,128)(2,1)S(1)} %collective-permute-done.22), channel_id=1, source_target_pairs={{1,0},{2,1},{3,2},{4,3},{5,4},{6,5},{7,6},{9,8},{10,9},{11,10},{12... | collective-permute-start | bytes 1572872 | tf_op jit(solution)/shard_map/ppermute | solution.py:17
  252.7 3.2 %copy-start = (bf16[1024,1056]{1,0:T(8,128)(2,1)S(1)}, bf16[1024,1056]{1,0:T(8,128)(2,1)}, u32[]{:S(2)}) copy-start(bf16[1024,1056]{1,0:T(8,128)(2,1)} %reshape.289) | copy-start | bytes 6488068
where the time goes:
time: 266 us; the launch traced here: 264 us
  starting transfers between devices  86 us (32%)
  local copies, waits for them, and re-layouts  62 us (23%)
  waiting for transfers between devices  48.2 us (18%)
  other arithmetic  34.2 us (13%)
  matrix products  32.7 us (12%)
    ppermute x24, starting transfers between devices, from_behind(): return lax.ppermute(array, axis, pairs)  74.2 us
    ppermute x24, waiting for transfers between devices, from_behind(): return lax.ppermute(array, axis, pairs)  44.5 us
    add x6, other arithmetic, spatial_weight(): inner_sum + coef_row[term_powers.index((power_u, power_v))] * cols_pow[po...  26.4 us
    dot_general x3, matrix products, on_device(): jnp.dot(band_tables[basis_index], across_part, preferred_element_type=jnp...  15.5 us
    dot_general x1, matrix products, on_device(): lax.dot_general(padded, stacked_bands, (((1,), (1,)), ((), ())), preferre...  14 us
    another operation x6, local copies, waits for them, and re-layouts, banded(): repeated = jnp.tile(line, out_count)[:out_count * widened]  14 us
    reshape x3, local copies, waits for them, and re-layouts, banded(): return repeated.reshape(out_count, widened)  12.2 us
    scatter x1, local copies, waits for them, and re-layouts, on_device(): jnp.zeros((9 * CAP, block_side, block_side), jnp.bfloat16).at[slot_index]  8.62 us
  transfers between devices with their start and end apart: 28, of which 5 were waited for; matrix products, arithmetic and copies ran while one was open for 37% of the time, Pallas kernels for 0%

commit v1 on v0

v1 whole, which is shorter than its diff:
```python
import functools

import jax
import jax.numpy as jnp
import ml_dtypes
import numpy as np
from jax import lax
from jax.experimental import pallas as pl
from jax.experimental.pallas import tpu as pltpu
from jax.sharding import PartitionSpec as P

HALO = 16
CAP = 16
BASES = 3
DEGREE = 4
LANES = 128

sigma_fractions = (0.09375, 0.1875, 0.375)
term_powers = [(degree - power_v, power_v) for degree in range(5) for power_v in range(degree + 1)]


def gauss_taps():
    positions = np.arange(-HALO, HALO + 1).astype(np.float32)
    stacked = []
    for fraction in sigma_fractions:
        sigma = fraction * HALO
        values = np.exp(-positions * positions / np.float32(2.0 * sigma * sigma))
        stacked.append(values / np.sum(values))
    return np.stack(stacked).astype(ml_dtypes.bfloat16)


def across_band(taps):
    band = np.zeros((3 * LANES, BASES * LANES), taps.dtype)
    for b in range(BASES):
        for out in range(LANES):
            first = LANES + out - HALO
            band[first : first + 2 * HALO + 1, b * LANES + out] = taps[b]
    return band


def down_band(taps):
    band = np.zeros((BASES, LANES, LANES + 2 * HALO), taps.dtype)
    for b in range(BASES):
        for out in range(LANES):
            band[b, out, out : out + 2 * HALO + 1] = taps[b]
    return band


def order_kernel(cols_total, per_tile, owner_ref, offset_ref, pos_ref, pieces_ref, first_ref, order_ref, code_ref, sem):
    count = owner_ref.shape[0]
    my_row = pos_ref[0]
    my_col = pos_ref[1]
    odd_col = lax.rem(my_col, 2)
    odd_row = lax.rem(my_row, 2)
    near = 1 - 2 * odd_col
    core = 1 - 2 * odd_row

    def steps(p):
        owner = owner_ref[p]
        return owner, lax.div(owner, cols_total) - my_row, lax.rem(owner, cols_total) - my_col

    def one(flag):
        return jnp.where(flag, 1, 0).astype(jnp.int32)

    def counting(p, counts):
        _, dy, dx = steps(p)
        far_diag, far_flat, near_flat = counts
        far = dx == -near
        return (
            far_diag + one(far & (dy != 0)),
            far_flat + one(far & (dy == 0)),
            near_flat + one((dx == near) & (dy == 0)),
        )

    zero = jnp.int32(0)
    far_diag, far_flat, near_flat = lax.fori_loop(0, count, counting, (zero, zero, zero))
    starts = (
        zero,
        far_diag,
        far_diag + far_flat,
        far_diag + far_flat + near_flat,
        zero + (count - 1),
        zero + count,
        zero + count + CAP,
    )
    for slot in range(count, order_ref.shape[0]):
        order_ref[slot] = 0
        code_ref[slot] = -1

    def placing(p, at):
        owner, dy, dx = steps(p)
        a, b, d, e, c, core_at, other_at = at
        flat = dy == 0
        is_far = dx == -near
        is_near = dx == near
        here = dx == 0
        is_a = is_far & (dy != 0)
        is_b = is_far & flat
        is_d = is_near & flat
        is_c = is_near & (dy != 0)
        slot = jnp.where(is_a, a, jnp.where(is_b, b, jnp.where(is_d, d, jnp.where(is_c, c, e))))
        code = owner * per_tile + offset_ref[p]
        order_ref[slot] = p
        code_ref[slot] = code
        to_core = here & (dy == core)
        to_other = here & (dy == -core)

        @pl.when(to_core | to_other)
        def _():
            extra = jnp.where(to_core, core_at, other_at)
            order_ref[extra] = p
            code_ref[extra] = code

        return (
            a + one(is_a),
            b + one(is_b),
            d + one(is_d),
            e + one(here),
            c - one(is_c),
            core_at + one(to_core),
            other_at + one(to_other),
        )

    lax.fori_loop(0, count, placing, starts)
    gather(order_ref, 0, pieces_ref, first_ref, sem)


def gather(order_ref, base, pieces_ref, out_ref, sem):
    def start(slot, carry):
        pltpu.make_async_copy(pieces_ref.at[order_ref[base + slot]], out_ref.at[slot], sem).start()
        return carry

    lax.fori_loop(0, out_ref.shape[0], start, 0)
    pltpu.make_async_copy(out_ref, out_ref, sem).wait()


def gather_kernel(bases, order_ref, pieces_ref, *refs):
    outs, sems = refs[:-1], refs[-1]
    for index, (base, out_ref) in enumerate(zip(bases, outs)):

        def start(slot, carry, base=base, out_ref=out_ref, index=index):
            pltpu.make_async_copy(
                pieces_ref.at[order_ref[base + slot]], out_ref.at[slot], sems.at[index]
            ).start()
            return carry

        lax.fori_loop(0, out_ref.shape[0], start, 0)
    for index, out_ref in enumerate(outs):
        pltpu.make_async_copy(out_ref, out_ref, sems.at[index]).wait()


SMEM = pl.BlockSpec(memory_space=pltpu.SMEM)
VMEM = pl.BlockSpec(memory_space=pltpu.VMEM)
ANY = pl.BlockSpec(memory_space=pl.ANY)


def order_pieces(owner_map, offsets, position, pieces, cols_total, per_tile):
    count, side, _ = pieces.shape
    chunk = jax.ShapeDtypeStruct((CAP, side, side), pieces.dtype)
    table = jax.ShapeDtypeStruct((2 * count,), jnp.int32)
    first, order, codes = pl.pallas_call(
        functools.partial(order_kernel, cols_total, per_tile),
        out_shape=(chunk, table, table),
        in_specs=[SMEM, SMEM, SMEM, ANY],
        out_specs=(ANY, SMEM, SMEM),
        scratch_shapes=[pltpu.SemaphoreType.DMA],
        name="order_pieces",
    )(owner_map, offsets, position, pieces)
    bases = tuple(range(CAP, count + 2 * CAP, CAP))
    rest = pl.pallas_call(
        functools.partial(gather_kernel, bases),
        out_shape=(chunk,) * len(bases),
        in_specs=[SMEM, ANY],
        out_specs=(ANY,) * len(bases),
        scratch_shapes=[pltpu.SemaphoreType.DMA((len(bases),))],
        name="gather_pieces",
    )(order, pieces)
    chunks = (first,) + tuple(rest[: count // CAP - 1])
    return chunks, rest[-2], rest[-1], codes


def matched_kernel(
    extent, coef_ref, pos_ref, centre_ref, top_ref, bottom_ref, left_ref, right_ref, across_ref, down_ref, out_ref,
    padded, across, polys,
):
    side = centre_ref.shape[0]
    tall = side + 2 * HALO
    rows_total, cols_total = extent
    padded[:, :LANES] = left_ref[...]
    padded[:, LANES + side :] = right_ref[...]
    padded[:HALO, LANES : LANES + side] = top_ref[...]
    padded[HALO + side :, LANES : LANES + side] = bottom_ref[...]
    padded[HALO : HALO + side, LANES : LANES + side] = centre_ref[...]

    col = lax.broadcasted_iota(jnp.int32, (1, side), 1) + pos_ref[1] * side
    u = (col.astype(jnp.float32) + 0.5) * (2.0 / (side * cols_total)) - 1.0
    powers = [jnp.ones_like(u)]
    for _ in range(DEGREE):
        powers.append(powers[-1] * u)
    for b in range(BASES):
        for j in range(DEGREE + 1):
            total = jnp.zeros_like(u)
            for i in range(DEGREE + 1 - j):
                total = total + coef_ref[b, term_powers.index((i, j))] * powers[i]
            polys[b * (DEGREE + 1) + j : b * (DEGREE + 1) + j + 1, :] = total

    def across_rows(start, rows):
        for j in range(side // LANES):
            window = padded[pl.ds(start, rows), j * LANES : (j + 3) * LANES]
            summed = jnp.dot(window, across_ref[...], preferred_element_type=jnp.float32)
            for b in range(BASES):
                across[b, pl.ds(start, rows), j * LANES : (j + 1) * LANES] = summed[
                    :, b * LANES : (b + 1) * LANES
                ].astype(jnp.bfloat16)

    def across_step(step, carry):
        across_rows(pl.multiple_of(step * LANES, LANES), LANES)
        return carry

    lax.fori_loop(0, side // LANES, across_step, 0)
    across_rows(side, tall - side)

    wide = 256

    def down_step(step, carry):
        start = pl.multiple_of(step * LANES, LANES)
        row = lax.broadcasted_iota(jnp.int32, (LANES, wide), 0) + start + pos_ref[0] * side
        v = (row.astype(jnp.float32) + 0.5) * (2.0 / (side * rows_total)) - 1.0
        for n in range(side // wide):
            cols = slice(n * wide, (n + 1) * wide)
            total = jnp.zeros((LANES, wide), jnp.float32)
            for b in range(BASES):
                smoothed = jnp.dot(
                    down_ref[b], across[b, pl.ds(start, LANES + 2 * HALO), cols], preferred_element_type=jnp.float32
                )
                first = b * (DEGREE + 1)
                weight = polys[first + DEGREE : first + DEGREE + 1, cols] * v
                for j in range(DEGREE - 1, 0, -1):
                    weight = (weight + polys[first + j : first + j + 1, cols]) * v
                weight = weight + polys[first : first + 1, cols]
                total = total + weight * smoothed
            out_ref[pl.ds(start, LANES), cols] = -total
        return carry

    lax.fori_loop(0, side // LANES, down_step, 0)


def minus_matched(extent, coefficients, position, centre, top, bottom, left, right):
    side = centre.shape[0]
    tall = side + 2 * HALO
    taps = gauss_taps()
    return pl.pallas_call(
        functools.partial(matched_kernel, extent),
        out_shape=jax.ShapeDtypeStruct((side, side), jnp.float32),
        in_specs=[SMEM, SMEM] + [VMEM] * 7,
        out_specs=VMEM,
        scratch_shapes=[
            pltpu.VMEM((tall, side + 2 * LANES), jnp.bfloat16),
            pltpu.VMEM((BASES, tall, side), jnp.bfloat16),
            pltpu.VMEM((16, side), jnp.float32),
        ],
        compiler_params=pltpu.CompilerParams(vmem_limit_bytes=40 << 20),
        cost_estimate=pl.CostEstimate(flops=8 << 30, bytes_accessed=8 << 20, transcendentals=0),
        name="matched_template",
    )(
        coefficients, position, centre, top, bottom, left, right,
        jnp.asarray(across_band(taps)), jnp.asarray(down_band(taps)),
    )


def add_kernel(plan, per_tile, blocks_side, pos_ref, codes_ref, share_ref, base_ref, *refs):
    count = len(plan)
    messages, out_ref, held, sems = refs[:count], refs[count], refs[count + 1], refs[count + 2]
    side = held.shape[0]
    fetch = pltpu.make_async_copy(base_ref, held, sems.at[0])
    fetch.start()
    fetch.wait()
    mine = pos_ref[2]
    block_side = side // blocks_side
    for message, (source, first) in zip(messages, plan):

        def visit(slot, carry, message=message, source=source, first=first):
            code = codes_ref[source, first + slot]
            block = code - mine * per_tile

            @pl.when((block >= 0) & (block < per_tile))
            def _():
                rows = pl.ds(pl.multiple_of(lax.div(block, blocks_side) * block_side, block_side), block_side)
                cols = pl.ds(pl.multiple_of(lax.rem(block, blocks_side) * block_side, block_side), block_side)
                held[rows, cols] = held[rows, cols] + message[slot].astype(jnp.float32) * share_ref[block]

            return carry

        lax.fori_loop(0, message.shape[0], visit, 0)
    store = pltpu.make_async_copy(held, out_ref, sems.at[1])
    store.start()
    store.wait()


def add_pieces(name, base, position, codes, shares, messages, blocks_side, cost):
    side = base.shape[0]
    plan = tuple((source, first) for _, source, first in messages)
    arrays = [array for array, _, _ in messages]
    return pl.pallas_call(
        functools.partial(add_kernel, plan, blocks_side * blocks_side, blocks_side),
        out_shape=jax.ShapeDtypeStruct(base.shape, base.dtype),
        in_specs=[SMEM, SMEM, SMEM, ANY] + [VMEM] * len(arrays),
        out_specs=ANY,
        scratch_shapes=[pltpu.VMEM((side, side), jnp.float32), pltpu.SemaphoreType.DMA((2,))],
        input_output_aliases={3: 0},
        compiler_params=pltpu.CompilerParams(vmem_limit_bytes=40 << 20),
        cost_estimate=pl.CostEstimate(flops=cost, bytes_accessed=8 << 20, transcendentals=0),
        name=name,
    )(position, codes, shares, base, *arrays)


class Grid:
    def __init__(self, rows, cols):
        self.rows, self.cols = rows, cols

    def pairs(self, target):
        found = []
        for row in range(self.rows):
            for col in range(self.cols):
                to_row, to_col = target(row, col)
                if 0 <= to_row < self.rows and 0 <= to_col < self.cols:
                    found.append((row * self.cols + col, to_row * self.cols + to_col))
        return found

    def near(self, array):
        return lax.ppermute(array, ("py", "px"), self.pairs(lambda r, c: (r, c ^ 1)))

    def far(self, array):
        return lax.ppermute(array, ("py", "px"), self.pairs(lambda r, c: (r, c + 1 if c % 2 else c - 1)))

    def beyond(self, array):
        return lax.ppermute(array, ("py", "px"), self.pairs(lambda r, c: (r, c - 2 if c % 2 else c + 2)))

    def core(self, array):
        return lax.ppermute(array, ("py", "px"), self.pairs(lambda r, c: (r ^ 1, c)))

    def other(self, array):
        return lax.ppermute(array, ("py", "px"), self.pairs(lambda r, c: (r + 1 if r % 2 else r - 1, c)))


def on_device(pieces, owner_map, offsets, template, coefficients):
    bar = lax.optimization_barrier
    rows_total = lax.axis_size("py")
    cols_total = lax.axis_size("px")
    grid = Grid(rows_total, cols_total)
    my_row = lax.axis_index("py")
    my_col = lax.axis_index("px")
    position = jnp.stack([my_row, my_col, my_row * cols_total + my_col]).astype(jnp.int32)
    even_row = my_row % 2 == 0
    even_col = my_col % 2 == 0
    count, block_side, _ = pieces.shape
    side = template.shape[0]
    blocks_side = side // block_side
    per_tile = blocks_side * blocks_side

    chunks, own_core, own_other, codes = order_pieces(owner_map, offsets, position, pieces, cols_total, per_tile)

    left_strip = template[:, :HALO].T
    right_strip = template[:, side - HALO :].T
    near_strip = grid.near(jnp.where(even_col, right_strip, left_strip))
    far_strip = grid.far(jnp.where(even_col, left_strip, right_strip))

    near_parts = [grid.near(chunk) for chunk in chunks]
    far_parts = [grid.beyond(part) for part in near_parts[:-1]]
    own_from = (grid.core(own_core), grid.other(own_other))

    top_rows = jnp.concatenate([template[:HALO], near_strip[:, :HALO], far_strip[:, :HALO]], axis=1)
    low = side - HALO
    low_rows = jnp.concatenate([template[low:], near_strip[:, low:], far_strip[:, low:]], axis=1)
    core_rows = grid.core(jnp.where(even_row, low_rows, top_rows))
    other_rows = grid.other(jnp.where(even_row, top_rows, low_rows))
    above = jnp.where(even_row, other_rows, core_rows)
    below = jnp.where(even_row, core_rows, other_rows)
    near_full = jnp.concatenate([above[:, side : side + HALO], near_strip, below[:, side : side + HALO]], axis=1)
    far_full = jnp.concatenate([above[:, side + HALO :], far_strip, below[:, side + HALO :]], axis=1)
    left = jnp.where(even_col, far_full, near_full).T
    right = jnp.where(even_col, near_full, far_full).T
    left = jnp.pad(left, ((0, 0), (LANES - HALO, 0)))
    right = jnp.pad(right, ((0, 0), (0, LANES - HALO)))
    base = minus_matched(
        (rows_total, cols_total), coefficients, position, template, above[:, :side], below[:, :side], left, right
    )

    everyone = lax.all_gather(codes, ("py", "px"))
    near_col = my_col + jnp.where(even_col, 1, -1)
    far_col = my_col - jnp.where(even_col, 1, -1)
    core_row = my_row + jnp.where(even_row, 1, -1)
    other_row = my_row - jnp.where(even_row, 1, -1)
    cols9 = jnp.stack([my_col, near_col, far_col] * 3)
    rows9 = jnp.repeat(jnp.stack([my_row, core_row, other_row]), 3)
    inside = (cols9 >= 0) & (cols9 < cols_total) & (rows9 >= 0) & (rows9 < rows_total)
    around = everyone[jnp.where(inside, rows9 * cols_total + cols9, 0)]
    around = jnp.where(inside[:, None], around, -1)
    blocks = around[:, :count].reshape(-1) - position[2] * per_tile
    coverage = jnp.sum(
        (blocks[:, None] == jnp.arange(per_tile, dtype=jnp.int32)[None, :]).astype(jnp.float32), axis=0
    )
    shares = 1.0 / jnp.maximum(coverage, 1.0)

    own, near, far = 0, 1, 2
    core, other = 3, 6
    early = [(chunk, own, i * CAP) for i, chunk in enumerate(chunks)]
    early += [(own_from[0], core, count), (own_from[1], other, count + CAP)]
    early += [(part, near, i * CAP) for i, part in enumerate(near_parts[:2])]
    early += [(far_parts[0], far, 0)]
    base = add_pieces("add_early", base, position, around, shares, early, blocks_side, 2 << 30)

    late = [(near_parts[2], near, 2 * CAP), (far_parts[1], far, CAP)]
    last = []
    for index in (0, 1):
        (late if index == 0 else last).extend(
            [
                (grid.core(far_parts[index]), core + far, index * CAP),
                (grid.other(far_parts[index]), other + far, index * CAP),
            ]
        )
    base = add_pieces("add_late", base, position, around, shares, late, blocks_side, 2 << 30)
    last += [(near_parts[3], near, 3 * CAP), (far_parts[2], far, 2 * CAP)]
    for index in (2, 3):
        last.extend(
            [
                (grid.core(near_parts[index]), core + near, index * CAP),
                (grid.other(near_parts[index]), other + near, index * CAP),
            ]
        )
    return add_pieces("add_last", base, position, around, shares, last, blocks_side, 2 << 30)


def solution(mesh):
    in_specs = (P(("py", "px"), None, None), P(("py", "px")), P(("py", "px")), P("py", "px"), P())
    out_specs = P("py", "px")
    return jax.shard_map(on_device, mesh=mesh, in_specs=in_specs, out_specs=out_specs, check_vma=False)
```

time: 266 us -> 285 us (1.071)
  Pallas kernels: 0 us -> 136 us
  blocking collectives: 0 us -> 73.6 us
  local copies, waits for them, and re-layouts: 62 us -> 13 us
  starting transfers between devices: 86 us -> 38 us
  matrix products: 32.7 us -> 0 us
  other arithmetic: 34.2 us -> 2.03 us
  waiting for transfers between devices: 48.2 us -> 17.5 us
    pallas_call x0 -> x6, Pallas kernels: none -> 136 us  [the longest x1 81.2 us: order_pieces(): pl.pallas_call(functools.partial(gather_kernel, bases), out_shape=(chunk,...]
    all_gather x0 -> x1, blocking collectives: none -> 73.6 us  [on_device(): everyone = lax.all_gather(codes, ('py', 'px'))]
    ppermute x28 -> x21, starting transfers between devices: 86 us -> 38 us  [the longest x6 20.9 us: other(): lax.ppermute(array, ('py', 'px'), self.pairs(lambda r, c: (r + 1 if r % 2...]
    dot_general x5 -> x0, matrix products: 32.7 us -> none  [the longest x3 15.5 us: on_device(): jnp.dot(band_tables[basis_index], across_part, preferred_element_type=jnp...]
    ppermute x28 -> x21, waiting for transfers between devices: 48.2 us -> 17.5 us  [the longest x5 13.3 us: near(): lax.ppermute(array, ('py', 'px'), self.pairs(lambda r, c: (r, c ^ 1)))]
    add x7 -> x0, other arithmetic: 26.4 us -> none  [the longest x6 26.4 us: spatial_weight(): inner_sum + coef_row[term_powers.index((power_u, power_v))] * cols_pow[po...]
    another operation x8 -> x2, local copies, waits for them, and re-layouts: 14.1 us -> 0.19 us  [on_device(): cols9 = jnp.stack([my_col, near_col, far_col] * 3)]
    reshape x4 -> x0, local copies, waits for them, and re-layouts: 12.2 us -> none  [the longest x3 12.2 us: banded(): return repeated.reshape(out_count, widened)]
  transfers between devices with their start and end apart: 28 -> 21, of which waited for: 5 -> 4; matrix products, arithmetic and copies ran while one was open for 37% -> 4% of each run, Pallas kernels for 0% -> 46%
where the time goes in v1:
time: 285 us; the launch traced here: 281 us
  Pallas kernels  136 us (48%)
  blocking collectives  73.6 us (26%)
  starting transfers between devices  38 us (13%)
  waiting for transfers between devices  17.5 us (6%)
  local copies, waits for them, and re-layouts  13 us (5%)
    pallas_call x1, Pallas kernels, order_pieces(): pl.pallas_call(functools.partial(gather_kernel, bases), out_shape=(chunk,...  81.2 us
    all_gather x1, blocking collectives, on_device(): everyone = lax.all_gather(codes, ('py', 'px'))  73.6 us
    ppermute x6, starting transfers between devices, other(): lax.ppermute(array, ('py', 'px'), self.pairs(lambda r, c: (r + 1 if r % 2...  20.9 us
    pallas_call x1, Pallas kernels, order_pieces(): pl.pallas_call(functools.partial(order_kernel, cols_total, per_tile), out...  20.8 us
    pallas_call x3, Pallas kernels, add_pieces(): pl.pallas_call(functools.partial(add_kernel, plan, blocks_side * blocks_s...  19.9 us
    pallas_call x1, Pallas kernels, minus_matched(): pl.pallas_call(functools.partial(matched_kernel, extent), out_shape=jax.S...  14.5 us
    ppermute x5, waiting for transfers between devices, near(): lax.ppermute(array, ('py', 'px'), self.pairs(lambda r, c: (r, c ^ 1)))  13.3 us
    ppermute x5, starting transfers between devices, near(): lax.ppermute(array, ('py', 'px'), self.pairs(lambda r, c: (r, c ^ 1)))  7.97 us
  transfers between devices with their start and end apart: 21, of which 4 were waited for; matrix products, arithmetic and copies ran while one was open for 4% of the time, Pallas kernels for 46%

profile of v1, /device:TPU:1, one launch (start us, length us, event | category | flops | bytes accessed | tf_op | source)
XLA Modules:
  0.0 280.9 jit_solution(1784626543550897278)
XLA Ops:
  0.0 1.2 fusion.2
  1.2 0.1 copy.28
  1.3 0.1 copy.29
  1.4 0.8 collective-permute-start.1
  2.2 4.6 %collective-permute-start = (bf16[16,1024]{1,0:T(8,128)(2,1)S(1)}, bf16[16,1024]{1,0:T(8,128)(2,1)S(1)}, u32[]{:S(2)}, u32[]{:S(2)}) collective-permute-start(bf16[16,1024]{1,0:T(8,128)(2,1)S(1)} %get-tuple-element.34), channel_id=1, source_target_pairs={{0,1},{1,0},{2,3},{3,2},{4,5},{5,4},{6,7},{7,6},{8,9},{9,8},{10,11... | collective-permute-start | bytes 98312 | tf_op jit(solution)/shard_map/ppermute | solution.py:331
  6.9 0.6 pad_add_fusion.pos_ref
  7.5 20.8 %order_pieces.1 = (bf16[16,128,128]{2,1,0:T(8,128)(2,1)}, s32[128]{0:T(128)}, s32[128]{0:T(128)}) custom-call(s32[64]{0:T(128)} %owner_ref.1, s32[64]{0:T(128)} %offset_ref.1, s32[3]{0:T(128)} %pad_add_fusion.pos_ref, bf16[64,128,128]{2,1,0:T(8,128)(2,1)} %pieces_ref.3), custom_call_target="tpu_custom_call" | custom-call | tf_op jit(solution)/shard_map/order_pieces/pallas_call | solution.py:161
  28.2 81.2 %gather_pieces.1 = (bf16[16,128,128]{2,1,0:T(8,128)(2,1)}, bf16[16,128,128]{2,1,0:T(8,128)(2,1)}, bf16[16,128,128]{2,1,0:T(8,128)(2,1)}, bf16[16,128,128]{2,1,0:T(8,128)(2,1)}, bf16[16,128,128]{2,1,0:T(8,128)(2,1)}) custom-call(s32[128]{0:T(128)} %get-tuple-element.15.order_ref, bf16[64,128,128]{2,1,0:T(8,128)(2,1)} %pieces_ref.3), custom_call_target="tpu_custom_call" | custom-call | tf_op jit(solution)/shard_map/gather_pieces/pallas_call | solution.py:170
  109.5 0.1 collective-permute-start.7
  109.6 1.3 collective-permute-start.4
  110.9 1.7 collective-permute-start.6
  112.5 0.8 fusion.1
  113.5 0.1 lt.62
  114.1 0.1 stack.59
  114.2 73.6 %all-gather.1 = s32[32,1,128]{2,1,0:T(1,128)S(1)} all-gather(s32[1,1,128]{2,1,0:T(1,128)} %bitcast.23), channel_id=2, replica_groups=mesh['py'=4,'px'=8] {'py','px'}, dimensions={0}, use_global_device_ids=true | all-gather | bytes 16896 | tf_op jit(solution)/shard_map/all_gather | solution.py:389
  187.8 0.6 gather_fusion
  188.4 0.1 stack.52
  188.8 0.1 concatenate.36
  188.9 0.1 concatenate.37
  189.0 7.5 %collective-permute-start.2 = (bf16[16,1056]{1,0:T(8,128)(2,1)S(1)}, bf16[16,1056]{1,0:T(8,128)(2,1)S(1)}, u32[]{:S(2)}, u32[]{:S(2)}) collective-permute-start(bf16[16,1056]{1,0:T(8,128)(2,1)S(1)} %get-tuple-element.32), channel_id=1, source_target_pairs={{8,16},{9,17},{10,18},{11,19},{12,20},{13,21},{14,22},{15,23},{16,... | collective-permute-start | bytes 101384 | tf_op jit(solution)/shard_map/ppermute | solution.py:343
  196.6 0.1 convert_reduce_fusion
  196.8 1.4 collective-permute-done.2
  198.2 3.6 %collective-permute-start.5 = (bf16[16,128,128]{2,1,0:T(8,128)(2,1)}, bf16[16,128,128]{2,1,0:T(8,128)(2,1)S(1)}, u32[]{:S(2)}, u32[]{:S(2)}) collective-permute-start(bf16[16,128,128]{2,1,0:T(8,128)(2,1)} %get-tuple-element.20), channel_id=1, source_target_pairs={{8,16},{9,17},{10,18},{11,19},{12,20},{13,21},{14,22},{15,23},{16,... | collective-permute-start | bytes 1572872 | tf_op jit(solution)/shard_map/ppermute | solution.py:343
  201.8 0.9 collective-permute-start.9
  202.7 0.7 collective-permute-start.15
  203.5 2.1 collective-permute-start.8
  205.6 10.5 %collective-permute-done.9.refs_0_ = bf16[16,128,128]{2,1,0:T(8,128)(2,1)S(1)} collective-permute-done((bf16[16,128,128]{2,1,0:T(8,128)(2,1)}, bf16[16,128,128]{2,1,0:T(8,128)(2,1)S(1)}, u32[]{:S(2)}, u32[]{:S(2)}) %collective-permute-start.9) | collective-permute-done | bytes 524320 | tf_op jit(solution)/shard_map/ppermute | solution.py:331
  216.1 2.1 collective-permute-start.16
  218.2 2.1 collective-permute-start.10
  220.3 0.5 collective-permute-start.11
  220.8 2.8 collective-permute-done.15.refs_2_
  223.6 1.9 collective-permute-start.12
  225.6 1.5 concatenate.38
  227.1 1.6 copy.24
  228.7 1.5 concatenate.39
  230.2 1.6 copy.25
  231.8 1.1 select_bitcast_fusion
  232.9 0.1 pad.8.left_ref
  233.1 2.7 collective-permute-done.10.refs_1_
  235.8 2.3 collective-permute-start.18
  238.2 3.3 %collective-permute-start.20 = (bf16[16,128,128]{2,1,0:T(8,128)(2,1)S(1)}, bf16[16,128,128]{2,1,0:T(8,128)(2,1)S(1)}, u32[]{:S(2)}, u32[]{:S(2)}) collective-permute-start(bf16[16,128,128]{2,1,0:T(8,128)(2,1)S(1)} %collective-permute-done.15.refs_2_), channel_id=1, source_target_pairs={{8,16},{9,17},{10,18},{11,19},{12,20},{13,21},{14,22},{15,23},{16,... | collective-permute-start | bytes 1572872 | tf_op jit(solution)/shard_map/ppermute | solution.py:343
  241.6 2.3 collective-permute-start.14
  243.9 1.6 copy-done.4
  245.5 0.9 copy-done.8
  246.4 14.5 %matched_template.1.base_ref = f32[1024,1024]{1,0:T(8,128)} custom-call(f32[3,15]{1,0:T(4,128)S(1)} %copy-done.6, s32[3]{0:T(128)S(1)} %copy-done.5, bf16[1024,1024]{1,0:T(8,128)(2,1)S(1)} %copy-done.4, bf16[16,1024]{1,0:T(8,128)(2,1)S(1)} %slice.67.top_ref, bf16[16,1024]{1,0:T(8,128)(2,1)S(1)} %slice.68.bottom_ref, bf16[1056,128]{1,0:T(8,128)(2,1)S(1)} %pad.8.left_ref, ...), custom_call_target="tpu_custom_call" | custom-call | flops 8589934592 | bytes 8388608 | tf_op jit(solution)/shard_map/matched_template/pallas_call | solution.py:252
  260.9 8.0 %add_early.1.base_ref = f32[1024,1024]{1,0:T(8,128)} custom-call(s32[3]{0:T(128)S(1)} %copy-done.5, s32[9,128]{1,0:T(8,128)S(1)} %broadcast_select_fusion.4.codes_ref, f32[64]{0:T(128)S(1)} %maximum_divide_fusion.share_ref, f32[1024,1024]{1,0:T(8,128)} %matched_template.1.base_ref, ...), custom_call_target="tpu_custom_call", output_to_operand_aliasing={{}: (3, {})} | custom-call | flops 2147483648 | bytes 8388608 | tf_op jit(solution)/shard_map/add_early/pallas_call | solution.py:304
  269.0 5.6 %add_late.1.base_ref = f32[1024,1024]{1,0:T(8,128)} custom-call(s32[3]{0:T(128)S(1)} %copy-done.5, s32[9,128]{1,0:T(8,128)S(1)} %broadcast_select_fusion.4.codes_ref, f32[64]{0:T(128)S(1)} %maximum_divide_fusion.share_ref, f32[1024,1024]{1,0:T(8,128)} %add_early.1.base_ref, ...), custom_call_target="tpu_custom_call", output_to_operand_aliasing={{}: (3, {})} | custom-call | flops 2147483648 | bytes 8388608 | tf_op jit(solution)/shard_map/add_late/pallas_call | solution.py:304
  274.6 6.3 %add_last.1 = f32[1024,1024]{1,0:T(8,128)} custom-call(s32[3]{0:T(128)S(1)} %copy-done.5, s32[9,128]{1,0:T(8,128)S(1)} %broadcast_select_fusion.4.codes_ref, f32[64]{0:T(128)S(1)} %maximum_divide_fusion.share_ref, f32[1024,1024]{1,0:T(8,128)} %add_late.1.base_ref, ...), custom_call_target="tpu_custom_call", output_to_operand_aliasing={{}: (3, {})} | custom-call | flops 2147483648 | bytes 8388608 | tf_op jit(solution)/shard_map/add_last/pallas_call | solution.py:304
  (67 shorter events, 1.5 us)
Async XLA Ops:
  1.4 242.5 %copy-start.6 = (f32[3,15]{1,0:T(4,128)S(1)}, f32[3,15]{1,0:T(4,128)}, u32[]{:S(2)}) copy-start(f32[3,15]{1,0:T(4,128)} %coef_ref.1) | copy-start | bytes 544
  1.4 242.5 %copy-start.7 = (bf16[384,384]{1,0:T(8,128)(2,1)S(1)}, bf16[384,384]{1,0:T(8,128)(2,1)}, u32[]{:S(2)}) copy-start(bf16[384,384]{1,0:T(8,128)(2,1)} %constant.49.clone.across_ref) | copy-start | bytes 884740
  1.4 187.2 %collective-permute-start.1 = (bf16[16,1024]{1,0:T(8,128)(2,1)S(1)}, bf16[16,1024]{1,0:T(8,128)(2,1)S(1)}, u32[]{:S(2)}, u32[]{:S(2)}) collective-permute-start(bf16[16,1024]{1,0:T(8,128)(2,1)S(1)} %get-tuple-element.33), channel_id=1, source_target_pairs={{1,2},{2,1},{3,4},{4,3},{5,6},{6,5},{9,10},{10,9},{11,12},{12,11},... | collective-permute-start | bytes 98312 | tf_op jit(solution)/shard_map/ppermute | solution.py:334
  2.2 186.5 %collective-permute-start = (bf16[16,1024]{1,0:T(8,128)(2,1)S(1)}, bf16[16,1024]{1,0:T(8,128)(2,1)S(1)}, u32[]{:S(2)}, u32[]{:S(2)}) collective-permute-start(bf16[16,1024]{1,0:T(8,128)(2,1)S(1)} %get-tuple-element.34), channel_id=1, source_target_pairs={{0,1},{1,0},{2,3},{3,2},{4,5},{5,4},{6,7},{7,6},{8,9},{9,8},{10,11... | collective-permute-start | bytes 98312 | tf_op jit(solution)/shard_map/ppermute | solution.py:331
  7.5 236.4 %copy-start.5 = (s32[3]{0:T(128)S(1)}, s32[3]{0:T(128)}, u32[]{:S(2)}) copy-start(s32[3]{0:T(128)} %pad_add_fusion.pos_ref) | copy-start | bytes 40
  109.5 93.2 %collective-permute-start.7 = (bf16[16,128,128]{2,1,0:T(8,128)(2,1)}, bf16[16,128,128]{2,1,0:T(8,128)(2,1)S(1)}, u32[]{:S(2)}, u32[]{:S(2)}) collective-permute-start(bf16[16,128,128]{2,1,0:T(8,128)(2,1)} %get-tuple-element.16.refs_1_), channel_id=1, source_target_pairs={{0,1},{1,0},{2,3},{3,2},{4,5},{5,4},{6,7},{7,6},{8,9},{9,8},{10,11... | collective-permute-start | bytes 1572872 | tf_op jit(solution)/shard_map/ppermute | solution.py:331
  109.6 108.6 %collective-permute-start.4 = (bf16[16,128,128]{2,1,0:T(8,128)(2,1)}, bf16[16,128,128]{2,1,0:T(8,128)(2,1)S(1)}, u32[]{:S(2)}, u32[]{:S(2)}) collective-permute-start(bf16[16,128,128]{2,1,0:T(8,128)(2,1)} %get-tuple-element.19), channel_id=1, source_target_pairs={{0,8},{1,9},{2,10},{3,11},{4,12},{5,13},{6,14},{7,15},{8,0},{9,1},... | collective-permute-start | bytes 1572872 | tf_op jit(solution)/shard_map/ppermute | solution.py:340
  110.9 92.6 %collective-permute-start.6 = (bf16[16,128,128]{2,1,0:T(8,128)(2,1)}, bf16[16,128,128]{2,1,0:T(8,128)(2,1)S(1)}, u32[]{:S(2)}, u32[]{:S(2)}) collective-permute-start(bf16[16,128,128]{2,1,0:T(8,128)(2,1)} %get-tuple-element.14.refs_0_), channel_id=1, source_target_pairs={{0,1},{1,0},{2,3},{3,2},{4,5},{5,4},{6,7},{7,6},{8,9},{9,8},{10,11... | collective-permute-start | bytes 1572872 | tf_op jit(solution)/shard_map/ppermute | solution.py:331
  188.6 14.1 %copy-start.10 = (bf16[16,1024]{1,0:T(8,128)(2,1)}, bf16[16,1024]{1,0:T(8,128)(2,1)S(1)}, u32[]{:S(2)}) copy-start(bf16[16,1024]{1,0:T(8,128)(2,1)S(1)} %collective-permute-done.1) | copy-start | bytes 98308
  188.7 14.0 %copy-start.9 = (bf16[16,1024]{1,0:T(8,128)(2,1)}, bf16[16,1024]{1,0:T(8,128)(2,1)S(1)}, u32[]{:S(2)}) copy-start(bf16[16,1024]{1,0:T(8,128)(2,1)S(1)} %collective-permute-done) | copy-start | bytes 98308
  189.0 9.2 %collective-permute-start.2 = (bf16[16,1056]{1,0:T(8,128)(2,1)S(1)}, bf16[16,1056]{1,0:T(8,128)(2,1)S(1)}, u32[]{:S(2)}, u32[]{:S(2)}) collective-permute-start(bf16[16,1056]{1,0:T(8,128)(2,1)S(1)} %get-tuple-element.32), channel_id=1, source_target_pairs={{8,16},{9,17},{10,18},{11,19},{12,20},{13,21},{14,22},{15,23},{16,... | collective-permute-start | bytes 101384 | tf_op jit(solution)/shard_map/ppermute | solution.py:343
  196.6 5.3 %collective-permute-start.3 = (bf16[16,1056]{1,0:T(8,128)(2,1)S(1)}, bf16[16,1056]{1,0:T(8,128)(2,1)S(1)}, u32[]{:S(2)}, u32[]{:S(2)}) collective-permute-start(bf16[16,1056]{1,0:T(8,128)(2,1)S(1)} %get-tuple-element.31), channel_id=1, source_target_pairs={{0,8},{1,9},{2,10},{3,11},{4,12},{5,13},{6,14},{7,15},{8,0},{9,1},... | collective-permute-start | bytes 101384 | tf_op jit(solution)/shard_map/ppermute | solution.py:340
  198.2 20.0 %collective-permute-start.5 = (bf16[16,128,128]{2,1,0:T(8,128)(2,1)}, bf16[16,128,128]{2,1,0:T(8,128)(2,1)S(1)}, u32[]{:S(2)}, u32[]{:S(2)}) collective-permute-start(bf16[16,128,128]{2,1,0:T(8,128)(2,1)} %get-tuple-element.20), channel_id=1, source_target_pairs={{8,16},{9,17},{10,18},{11,19},{12,20},{13,21},{14,22},{15,23},{16,... | collective-permute-start | bytes 1572872 | tf_op jit(solution)/shard_map/ppermute | solution.py:343
  201.8 14.3 %collective-permute-start.9 = (bf16[16,128,128]{2,1,0:T(8,128)(2,1)}, bf16[16,128,128]{2,1,0:T(8,128)(2,1)S(1)}, u32[]{:S(2)}, u32[]{:S(2)}) collective-permute-start(bf16[16,128,128]{2,1,0:T(8,128)(2,1)} %get-tuple-element.17.refs_2_), channel_id=1, source_target_pairs={{0,1},{1,0},{2,3},{3,2},{4,5},{5,4},{6,7},{7,6},{8,9},{9,8},{10,11... | collective-permute-start | bytes 1572872 | tf_op jit(solution)/shard_map/ppermute | solution.py:331
  202.7 20.9 %collective-permute-start.15 = (bf16[16,128,128]{2,1,0:T(8,128)(2,1)}, bf16[16,128,128]{2,1,0:T(8,128)(2,1)S(1)}, u32[]{:S(2)}, u32[]{:S(2)}) collective-permute-start(bf16[16,128,128]{2,1,0:T(8,128)(2,1)} %get-tuple-element.18.refs_3_), channel_id=1, source_target_pairs={{0,1},{1,0},{2,3},{3,2},{4,5},{5,4},{6,7},{7,6},{8,9},{9,8},{10,11... | collective-permute-start | bytes 1572872 | tf_op jit(solution)/shard_map/ppermute | solution.py:331
  203.5 16.9 %collective-permute-start.8 = (bf16[16,128,128]{2,1,0:T(8,128)(2,1)S(1)}, bf16[16,128,128]{2,1,0:T(8,128)(2,1)}, u32[]{:S(2)}, u32[]{:S(2)}) collective-permute-start(bf16[16,128,128]{2,1,0:T(8,128)(2,1)S(1)} %collective-permute-done.6.refs_6_), channel_id=1, source_target_pairs={{0,2},{2,4},{3,1},{4,6},{5,3},{7,5},{8,10},{10,12},{11,9},{12,14},... | collective-permute-start | bytes 1572872 | tf_op jit(solution)/shard_map/ppermute | solution.py:337
  216.1 22.0 %collective-permute-start.16 = (bf16[16,128,128]{2,1,0:T(8,128)(2,1)S(1)}, bf16[16,128,128]{2,1,0:T(8,128)(2,1)}, u32[]{:S(2)}, u32[]{:S(2)}) collective-permute-start(bf16[16,128,128]{2,1,0:T(8,128)(2,1)S(1)} %collective-permute-done.9.refs_0_), channel_id=1, source_target_pairs={{0,2},{2,4},{3,1},{4,6},{5,3},{7,5},{8,10},{10,12},{11,9},{12,14},... | collective-permute-start | bytes 1572872 | tf_op jit(solution)/shard_map/ppermute | solution.py:337
  218.2 20.0 %collective-permute-start.17 = (bf16[16,128,128]{2,1,0:T(8,128)(2,1)S(1)}, bf16[16,128,128]{2,1,0:T(8,128)(2,1)}, u32[]{:S(2)}, u32[]{:S(2)}) collective-permute-start(bf16[16,128,128]{2,1,0:T(8,128)(2,1)S(1)} %collective-permute-done.9.refs_0_), channel_id=1, source_target_pairs={{0,8},{1,9},{2,10},{3,11},{4,12},{5,13},{6,14},{7,15},{8,0},{9,1},... | collective-permute-start | bytes 1572872 | tf_op jit(solution)/shard_map/ppermute | solution.py:340
  218.2 17.6 %collective-permute-start.10 = (bf16[16,128,128]{2,1,0:T(8,128)(2,1)S(1)}, bf16[16,128,128]{2,1,0:T(8,128)(2,1)}, u32[]{:S(2)}, u32[]{:S(2)}) collective-permute-start(bf16[16,128,128]{2,1,0:T(8,128)(2,1)S(1)} %collective-permute-done.7.refs_7_), channel_id=1, source_target_pairs={{0,2},{2,4},{3,1},{4,6},{5,3},{7,5},{8,10},{10,12},{11,9},{12,14},... | collective-permute-start | bytes 1572872 | tf_op jit(solution)/shard_map/ppermute | solution.py:337
  220.3 21.2 %collective-permute-start.11 = (bf16[16,128,128]{2,1,0:T(8,128)(2,1)}, bf16[16,128,128]{2,1,0:T(8,128)(2,1)}, u32[]{:S(2)}, u32[]{:S(2)}) collective-permute-start(bf16[16,128,128]{2,1,0:T(8,128)(2,1)} %collective-permute-done.8.refs_8_), channel_id=1, source_target_pairs={{0,8},{1,9},{2,10},{3,11},{4,12},{5,13},{6,14},{7,15},{8,0},{9,1},... | collective-permute-start | bytes 1572872 | tf_op jit(solution)/shard_map/ppermute | solution.py:340
  223.6 18.0 %collective-permute-start.12 = (bf16[16,128,128]{2,1,0:T(8,128)(2,1)}, bf16[16,128,128]{2,1,0:T(8,128)(2,1)}, u32[]{:S(2)}, u32[]{:S(2)}) collective-permute-start(bf16[16,128,128]{2,1,0:T(8,128)(2,1)} %collective-permute-done.8.refs_8_), channel_id=1, source_target_pairs={{8,16},{9,17},{10,18},{11,19},{12,20},{13,21},{14,22},{15,23},{16,... | collective-permute-start | bytes 1572872 | tf_op jit(solution)/shard_map/ppermute | solution.py:343
  233.1 27.8 %copy-start = (bf16[16,128,128]{2,1,0:T(8,128)(2,1)S(1)}, bf16[16,128,128]{2,1,0:T(8,128)(2,1)}, u32[]{:S(2)}) copy-start(bf16[16,128,128]{2,1,0:T(8,128)(2,1)} %get-tuple-element.14.refs_0_) | copy-start | bytes 1572868
  233.1 27.8 %copy-start.1 = (bf16[16,128,128]{2,1,0:T(8,128)(2,1)S(1)}, bf16[16,128,128]{2,1,0:T(8,128)(2,1)}, u32[]{:S(2)}) copy-start(bf16[16,128,128]{2,1,0:T(8,128)(2,1)} %get-tuple-element.16.refs_1_) | copy-start | bytes 1572868
  233.1 27.8 %copy-start.2 = (bf16[16,128,128]{2,1,0:T(8,128)(2,1)S(1)}, bf16[16,128,128]{2,1,0:T(8,128)(2,1)}, u32[]{:S(2)}) copy-start(bf16[16,128,128]{2,1,0:T(8,128)(2,1)} %get-tuple-element.17.refs_2_) | copy-start | bytes 1572868
  233.1 27.8 %copy-start.3 = (bf16[16,128,128]{2,1,0:T(8,128)(2,1)S(1)}, bf16[16,128,128]{2,1,0:T(8,128)(2,1)}, u32[]{:S(2)}) copy-start(bf16[16,128,128]{2,1,0:T(8,128)(2,1)} %get-tuple-element.18.refs_3_) | copy-start | bytes 1572868
  235.8 38.8 %collective-permute-start.18 = (bf16[16,128,128]{2,1,0:T(8,128)(2,1)S(1)}, bf16[16,128,128]{2,1,0:T(8,128)(2,1)S(1)}, u32[]{:S(2)}, u32[]{:S(2)}) collective-permute-start(bf16[16,128,128]{2,1,0:T(8,128)(2,1)S(1)} %collective-permute-done.9.refs_0_), channel_id=1, source_target_pairs={{8,16},{9,17},{10,18},{11,19},{12,20},{13,21},{14,22},{15,23},{16,... | collective-permute-start | bytes 1572872 | tf_op jit(solution)/shard_map/ppermute | solution.py:343
  238.1 36.5 %collective-permute-start.19 = (bf16[16,128,128]{2,1,0:T(8,128)(2,1)S(1)}, bf16[16,128,128]{2,1,0:T(8,128)(2,1)S(1)}, u32[]{:S(2)}, u32[]{:S(2)}) collective-permute-start(bf16[16,128,128]{2,1,0:T(8,128)(2,1)S(1)} %collective-permute-done.15.refs_2_), channel_id=1, source_target_pairs={{0,8},{1,9},{2,10},{3,11},{4,12},{5,13},{6,14},{7,15},{8,0},{9,1},... | collective-permute-start | bytes 1572872 | tf_op jit(solution)/shard_map/ppermute | solution.py:340
  238.2 36.4 %collective-permute-start.20 = (bf16[16,128,128]{2,1,0:T(8,128)(2,1)S(1)}, bf16[16,128,128]{2,1,0:T(8,128)(2,1)S(1)}, u32[]{:S(2)}, u32[]{:S(2)}) collective-permute-start(bf16[16,128,128]{2,1,0:T(8,128)(2,1)S(1)} %collective-permute-done.15.refs_2_), channel_id=1, source_target_pairs={{8,16},{9,17},{10,18},{11,19},{12,20},{13,21},{14,22},{15,23},{16,... | collective-permute-start | bytes 1572872 | tf_op jit(solution)/shard_map/ppermute | solution.py:343
  241.5 33.1 %collective-permute-start.13 = (bf16[16,128,128]{2,1,0:T(8,128)(2,1)}, bf16[16,128,128]{2,1,0:T(8,128)(2,1)S(1)}, u32[]{:S(2)}, u32[]{:S(2)}) collective-permute-start(bf16[16,128,128]{2,1,0:T(8,128)(2,1)} %collective-permute-done.10.refs_1_), channel_id=1, source_target_pairs={{0,8},{1,9},{2,10},{3,11},{4,12},{5,13},{6,14},{7,15},{8,0},{9,1},... | collective-permute-start | bytes 1572872 | tf_op jit(solution)/shard_map/ppermute | solution.py:340
  241.6 33.0 %collective-permute-start.14 = (bf16[16,128,128]{2,1,0:T(8,128)(2,1)}, bf16[16,128,128]{2,1,0:T(8,128)(2,1)S(1)}, u32[]{:S(2)}, u32[]{:S(2)}) collective-permute-start(bf16[16,128,128]{2,1,0:T(8,128)(2,1)} %collective-permute-done.10.refs_1_), channel_id=1, source_target_pairs={{8,16},{9,17},{10,18},{11,19},{12,20},{13,21},{14,22},{15,23},{16,... | collective-permute-start | bytes 1572872 | tf_op jit(solution)/shard_map/ppermute | solution.py:343
  243.9 1.6 copy-start.4
  245.5 0.9 copy-start.8

commit v2 on v0

v2 whole, which is shorter than its diff:
```python
import functools

import jax
import jax.numpy as jnp
import ml_dtypes
import numpy as np
from jax import lax
from jax.experimental import pallas as pl
from jax.experimental.pallas import tpu as pltpu
from jax.sharding import PartitionSpec as P

HALO = 16
CAP = 16
BASES = 3
DEGREE = 4
LANES = 128

sigma_fractions = (0.09375, 0.1875, 0.375)
term_powers = [(degree - power_v, power_v) for degree in range(5) for power_v in range(degree + 1)]


def gauss_taps():
    positions = np.arange(-HALO, HALO + 1).astype(np.float32)
    stacked = []
    for fraction in sigma_fractions:
        sigma = fraction * HALO
        values = np.exp(-positions * positions / np.float32(2.0 * sigma * sigma))
        stacked.append(values / np.sum(values))
    return np.stack(stacked).astype(ml_dtypes.bfloat16)


def across_band(taps):
    band = np.zeros((2 * LANES, BASES * LANES), taps.dtype)
    for b in range(BASES):
        for out in range(LANES):
            band[out : out + 2 * HALO + 1, b * LANES + out] = taps[b]
    return band


def down_band(taps):
    band = np.zeros((BASES, LANES, LANES + 2 * HALO), taps.dtype)
    for b in range(BASES):
        for out in range(LANES):
            band[b, out, out : out + 2 * HALO + 1] = taps[b]
    return band


SMEM = pl.BlockSpec(memory_space=pltpu.SMEM)
VMEM = pl.BlockSpec(memory_space=pltpu.VMEM)
ANY = pl.BlockSpec(memory_space=pl.ANY)
CHEAP = pl.CostEstimate(flops=0, bytes_accessed=0, transcendentals=0)


def split_index(index, size):
    if size & (size - 1) == 0:
        return jnp.right_shift(index, size.bit_length() - 1), jnp.bitwise_and(index, size - 1)
    return lax.div(index, size), lax.rem(index, size)


def piece_at(message, slot, block_side):
    if len(message.shape) == 3:
        return message.at[slot]
    start = slot * block_side
    if not isinstance(slot, int):
        start = pl.multiple_of(start, block_side)
    return message.at[pl.ds(start, block_side), :]


def order_kernel(cols_total, owner_ref, offset_ref, pos_ref, pieces_ref, template_ref, *refs):
    outs = refs[:-9]
    near_ref, far_ref, label_ref, held, edges, meta, order_v, order_s, sems = refs[-9:]
    count = held.shape[0]
    fetch = pltpu.make_async_copy(pieces_ref, held, sems.at[len(outs)])
    fetch.start()
    side = edges.shape[1]
    rims = [
        pltpu.make_async_copy(template_ref.at[:, :LANES], edges.at[0], sems.at[len(outs) + 2]),
        pltpu.make_async_copy(template_ref.at[:, side - LANES :], edges.at[1], sems.at[len(outs) + 3]),
    ]
    for rim in rims:
        rim.start()
    my_row, my_col = pos_ref[0], pos_ref[1]
    even_col = jnp.bitwise_and(my_col, 1) == 0
    near = 1 - 2 * jnp.bitwise_and(my_col, 1)
    core = 1 - 2 * jnp.bitwise_and(my_row, 1)

    meta[...] = jnp.zeros_like(meta)
    meta[0:1, :count] = owner_ref[...]
    meta[1:2, :count] = offset_ref[...]
    lane = lax.broadcasted_iota(jnp.int32, (1, LANES), 1)
    row, col = split_index(meta[0:1, :], cols_total)
    dy, dx = row - my_row, col - my_col
    flat = dy == 0
    to_core = dy == core
    kind = jnp.where(
        dx == 0,
        jnp.where(flat, 4, jnp.where(to_core, 5, 6)),
        jnp.where(
            dx == near,
            jnp.where(flat, 3, jnp.where(to_core, 8, 7)),
            jnp.where(flat, 2, jnp.where(to_core, 1, 0)),
        ),
    )
    kind = jnp.where(lane < count, kind, 9)
    packed = (3 * (dy + 1) + dx + 2) * 256 + meta[1:2, :]

    def both(line):
        across = jnp.broadcast_to(line.astype(jnp.float32), (LANES, LANES))
        return across, across.T

    kind_l, kind_s = both(kind)
    _, packed_s = both(packed)
    sub = lax.broadcasted_iota(jnp.int32, (LANES, LANES), 0)
    lan = lax.broadcasted_iota(jnp.int32, (LANES, LANES), 1)

    def total(flags):
        return jnp.sum(jnp.where(flags, 1.0, 0.0), axis=1, keepdims=True)

    rank = total((kind_l == kind_s) & (lan < sub))
    mine = kind_s[:, 0:1]
    before = total((kind_l < kind_s) & ((kind_l >= 7.0) | (kind_s < 7.0)))
    slot = jnp.where(mine < 7.0, before + rank, jnp.where(mine < 9.0, (count - 1.0) - before - rank, -1.0))
    extra = jnp.where(
        mine == 5.0, count + rank, jnp.where(mine == 6.0, (count + CAP) + rank, -1.0)
    )
    place = lan.astype(jnp.float32)
    here = (place == slot) | (place == extra)
    order = jnp.sum(jnp.where(here, sub.astype(jnp.float32), 0.0), axis=0, keepdims=True)
    labels = jnp.sum(jnp.where(here, packed_s, 0.0), axis=0, keepdims=True)
    order_v[...] = jnp.broadcast_to(order, order_v.shape).astype(jnp.int32)
    to_smem = pltpu.make_async_copy(order_v, order_s, sems.at[len(outs) + 1])
    to_smem.start()
    labels = labels.astype(jnp.int32)
    which = lax.broadcasted_iota(jnp.int32, label_ref.shape, 0)
    label_rows = jnp.where(
        which == 0, jnp.right_shift(labels, 8), jnp.where(which == 1, jnp.bitwise_and(labels, 255), 0)
    ).astype(jnp.float32).astype(jnp.bfloat16)
    label_ref[...] = label_rows
    near_ref[:, side:] = label_rows
    far_ref[:, side:] = label_rows
    to_smem.wait()
    fetch.wait()
    for index, out_ref in enumerate(outs):
        for slot_at in range(CAP):
            pltpu.make_async_copy(
                held.at[order_s[0, index * CAP + slot_at]], piece_at(out_ref, slot_at, held.shape[1]), sems.at[index]
            ).start()
    for rim in rims:
        rim.wait()
    for block in range(side // LANES):
        rows = slice(block * LANES, (block + 1) * LANES)
        left = edges[0, rows, :].astype(jnp.float32).T[:HALO]
        right = edges[1, rows, :].astype(jnp.float32).T[LANES - HALO :]
        near_ref[:, rows] = jnp.where(even_col, right, left).astype(near_ref.dtype)
        far_ref[:, rows] = jnp.where(even_col, left, right).astype(far_ref.dtype)
    for index, out_ref in enumerate(outs):
        pltpu.make_async_copy(outs[0], outs[0], sems.at[index]).wait()


def order_pieces(owner_map, offsets, position, pieces, template, cols_total):
    count, block_side, _ = pieces.shape
    side = template.shape[0]
    parts = count // CAP + 2
    chunk = jax.ShapeDtypeStruct((CAP, block_side, block_side), pieces.dtype)
    mail = chunk
    rim = jax.ShapeDtypeStruct((HALO, side + LANES), template.dtype)
    *outs, near, far, labels = pl.pallas_call(
        functools.partial(order_kernel, cols_total),
        out_shape=(chunk,) * (parts - 2)
        + (mail, mail)
        + (rim, rim, jax.ShapeDtypeStruct((HALO, LANES), template.dtype)),
        in_specs=[VMEM, VMEM, SMEM, ANY, ANY],
        out_specs=(ANY,) * parts + (VMEM,) * 3,
        scratch_shapes=[
            pltpu.VMEM(pieces.shape, pieces.dtype),
            pltpu.VMEM((2, side, LANES), template.dtype),
            pltpu.VMEM((8, LANES), jnp.int32),
            pltpu.VMEM((8, LANES), jnp.int32),
            pltpu.SMEM((8, LANES), jnp.int32),
            pltpu.SemaphoreType.DMA((parts + 4,)),
        ],
        compiler_params=pltpu.CompilerParams(vmem_limit_bytes=58 << 20),
        cost_estimate=CHEAP,
        name="order_pieces",
    )(owner_map.reshape(1, -1), offsets.reshape(1, -1), position, pieces, template)
    return outs[:-2], outs[-2], outs[-1], near, far, labels


def rim_rows(side):
    return HALO * (side // LANES + 3)


def row_rims_kernel(
    pos_ref, template_ref, near_ref, far_ref, label_ref, core_out, other_out, edges, packed, sems
):
    side = edges.shape[2]
    tiles = side // LANES
    fetches = [
        pltpu.make_async_copy(template_ref.at[:HALO, :], edges.at[0], sems.at[0]),
        pltpu.make_async_copy(template_ref.at[side - HALO :, :], edges.at[1], sems.at[1]),
    ]
    for fetch in fetches:
        fetch.start()
    even_row = jnp.bitwise_and(pos_ref[0], 1) == 0
    sub = lax.broadcasted_iota(jnp.int32, (HALO, LANES), 0)
    own = label_ref[...].astype(jnp.float32)
    near = near_ref[:, side:].astype(jnp.float32)
    far = far_ref[:, side:].astype(jnp.float32)
    pairs = own
    for index, table in ((1, near), (2, far)):
        for row in (0, 1):
            pairs = jnp.where(sub == 2 * index + row, table[row : row + 1, :], pairs)
    pairs = pairs.astype(label_ref.dtype)
    corners = []
    for strip in (near_ref, far_ref):
        low = strip[:, side - LANES : side].astype(jnp.float32)
        low = jnp.concatenate([low[:, LANES - HALO :], low[:, : LANES - HALO]], axis=1).astype(strip.dtype)
        corners.append((strip[:, :LANES], low))
    for fetch in fetches:
        fetch.wait()
    stores = []
    for index, (out_ref, upper) in enumerate(((core_out, jnp.logical_not(even_row)), (other_out, even_row))):
        for tile in range(tiles):
            cols = slice(tile * LANES, (tile + 1) * LANES)
            packed[index, tile * HALO : (tile + 1) * HALO, :] = jnp.where(upper, edges[0, :, cols], edges[1, :, cols])
        for corner, (top, low) in enumerate(corners):
            start = (tiles + corner) * HALO
            packed[index, start : start + HALO, :] = jnp.where(upper, top, low)
        packed[index, (tiles + 2) * HALO :, :] = pairs
        rows = out_ref.shape[0]
        stores.append(
            pltpu.make_async_copy(
                packed.at[index], out_ref.at[rows - packed.shape[1] : rows, :], sems.at[2 + index]
            )
        )
        stores[-1].start()
    for store in stores:
        store.wait()


def row_rims(position, template, near, far, labels):
    side = template.shape[0]
    message = jax.ShapeDtypeStruct((rim_rows(side), LANES), template.dtype)
    return pl.pallas_call(
        row_rims_kernel,
        out_shape=(message, message),
        in_specs=[SMEM, ANY, VMEM, VMEM, VMEM],
        out_specs=(ANY, ANY),
        scratch_shapes=[
            pltpu.VMEM((2, HALO, side), template.dtype),
            pltpu.VMEM((2, rim_rows(side), LANES), template.dtype),
            pltpu.SemaphoreType.DMA((4,)),
        ],
        compiler_params=pltpu.CompilerParams(vmem_limit_bytes=58 << 20),
        cost_estimate=CHEAP,
        name="row_rims",
    )(position, template, near, far, labels)


def fill_tables(even_row, even_col, own_ref, core_ref, other_ref, blocks_ref, share_ref):
    near_step = jnp.where(even_col, 1, -1)
    core_step = jnp.where(even_row, 1, -1)
    sub = lax.broadcasted_iota(jnp.int32, (LANES, LANES), 0)
    lane = lax.broadcasted_iota(jnp.int32, (LANES, LANES), 1)
    table = jnp.full((LANES, LANES), -1.0, jnp.float32)
    for group, (ref, row_step) in enumerate(((own_ref, 0), (core_ref, core_step), (other_ref, -core_step))):
        rows = ref[ref.shape[0] - HALO :, :].astype(jnp.float32)
        for index, col_step in enumerate((0, near_step, -near_step)):
            wanted = (5 - 3 * row_step - col_step) * jnp.int32(1)
            match = rows[2 * index : 2 * index + 1, :] == wanted.astype(jnp.float32)
            line = jnp.where(match, rows[2 * index + 1 : 2 * index + 2, :], -1.0)
            table = jnp.where(sub == 3 * group + index, line, table)
    blocks_ref[...] = table[: blocks_ref.shape[0]].astype(jnp.int32)
    upright = table.T
    counts = jnp.zeros((1, LANES), jnp.float32)
    for source in range(9):
        column = upright[: LANES // 2, source : source + 1]
        counts = counts + jnp.sum(
            jnp.where(column == lane[: LANES // 2].astype(jnp.float32), 1.0, 0.0), axis=0, keepdims=True
        )
    share_ref[...] = jnp.broadcast_to(1.0 / jnp.maximum(counts, 1.0), share_ref.shape)


def weight_rows(coef_ref, start, width, side, cols_total, my_col):
    col = lax.broadcasted_iota(jnp.int32, (1, width), 1) + (start + my_col * side)
    u = (col.astype(jnp.float32) + 0.5) * (2.0 / (side * cols_total)) - 1.0
    powers = [jnp.ones_like(u)]
    for _ in range(DEGREE):
        powers.append(powers[-1] * u)
    rows = []
    for b in range(BASES):
        for j in range(DEGREE + 1):
            total = jnp.zeros_like(u)
            for i in range(DEGREE + 1 - j):
                total = total + coef_ref[b, term_powers.index((i, j))] * powers[i]
            rows.append(total)
    return rows


def minus_weighted(smoothed, polys, cols, start, side, rows_total, my_row):
    shape = smoothed[0].shape
    row = lax.broadcasted_iota(jnp.int32, shape, 0) + (start + my_row * side)
    v = (row.astype(jnp.float32) + 0.5) * (2.0 / (side * rows_total)) - 1.0
    total = jnp.zeros(shape, jnp.float32)
    for b in range(BASES):
        power = b * (DEGREE + 1)
        weight = polys[power + DEGREE : power + DEGREE + 1, cols] * v
        for j in range(DEGREE - 1, 0, -1):
            weight = (weight + polys[power + j : power + j + 1, cols]) * v
        weight = weight + polys[power : power + 1, cols]
        total = total - weight * smoothed[b]
    return total


def interior_kernel(
    extent, coef_ref, pos_ref, centre_ref, across_ref, down_ref, out_ref, padded, across, polys, ready, sems
):
    side = centre_ref.shape[0]
    rows_total, cols_total = extent
    inner = side - 2 * LANES
    reach = inner + LANES
    padded[:, :reach] = centre_ref[:, LANES - HALO : LANES - HALO + reach]
    for index, line in enumerate(weight_rows(coef_ref, LANES, inner, side, cols_total, pos_ref[1])):
        polys[index : index + 1, :] = line
    for b in range(BASES):
        across[b, :HALO, :] = jnp.zeros((HALO, inner), across.dtype)
        across[b, HALO + side :, :] = jnp.zeros((HALO, inner), across.dtype)

    tall = side // 2
    for start in (0, tall):
        for j in range(inner // LANES):
            window = padded[start : start + tall, j * LANES : (j + 2) * LANES]
            summed = jnp.dot(window, across_ref[...], preferred_element_type=jnp.float32)
            for b in range(BASES):
                across[b, HALO + start : HALO + start + tall, j * LANES : (j + 1) * LANES] = summed[
                    :, b * LANES : (b + 1) * LANES
                ].astype(across.dtype)

    wide = 256

    def send(start, slot):
        return pltpu.make_async_copy(
            ready.at[slot], out_ref.at[pl.ds(start, LANES), LANES : LANES + inner], sems.at[slot]
        )

    def down_step(step, carry):
        start = pl.multiple_of(step * LANES, LANES)
        slot = jnp.bitwise_and(step, 1)

        @pl.when(step >= 2)
        def _():
            send(start, slot).wait()

        for n in range(inner // wide):
            cols = slice(n * wide, (n + 1) * wide)
            smoothed = [
                jnp.dot(
                    down_ref[b], across[b, pl.ds(start, LANES + 2 * HALO), cols], preferred_element_type=jnp.float32
                )
                for b in range(BASES)
            ]
            ready[slot, :, cols] = minus_weighted(smoothed, polys, cols, start, side, rows_total, pos_ref[0])
        send(start, slot).start()
        return carry

    lax.fori_loop(0, side // LANES, down_step, 0)
    for slot in (0, 1):
        send(0, slot).wait()


def interior(extent, coefficients, position, centre):
    side = centre.shape[0]
    inner = side - 2 * LANES
    taps = gauss_taps()
    return pl.pallas_call(
        functools.partial(interior_kernel, extent),
        out_shape=jax.ShapeDtypeStruct((side, side), jnp.float32),
        in_specs=[SMEM, SMEM] + [VMEM] * 3,
        out_specs=ANY,
        scratch_shapes=[
            pltpu.VMEM((side, inner + LANES), jnp.bfloat16),
            pltpu.VMEM((BASES, side + 2 * HALO, inner), jnp.bfloat16),
            pltpu.VMEM((16, inner), jnp.float32),
            pltpu.VMEM((2, LANES, inner), jnp.float32),
            pltpu.SemaphoreType.DMA((2,)),
        ],
        compiler_params=pltpu.CompilerParams(vmem_limit_bytes=58 << 20),
        cost_estimate=pl.CostEstimate(flops=int(8e9), bytes_accessed=1, transcendentals=0),
        name="matched_inside",
    )(coefficients, position, centre, jnp.asarray(across_band(taps)), jnp.asarray(down_band(taps)))


def frame_kernel(
    extent, coef_ref, pos_ref, near_ref, far_ref, core_ref, other_ref, sent_ref, across_ref, down_ref, template_ref,
    base_ref, out_ref, blocks_ref, share_ref, sides, ends, rims, padded, across, polys, columns, lines, sems,
):
    side = template_ref.shape[0]
    rows_total, cols_total = extent
    deep = 3 * HALO
    inner = side - 2 * LANES
    fetches = [
        pltpu.make_async_copy(template_ref.at[:, : 2 * LANES], sides.at[0], sems.at[0]),
        pltpu.make_async_copy(template_ref.at[:, side - 2 * LANES :], sides.at[1], sems.at[1]),
        pltpu.make_async_copy(template_ref.at[: 2 * HALO, :], ends.at[0], sems.at[2]),
        pltpu.make_async_copy(template_ref.at[side - 2 * HALO :, :], ends.at[1], sems.at[3]),
    ]
    rim_fetches = []
    for index, ref in enumerate((sent_ref, core_ref, other_ref)):
        rows = ref.shape[0]
        rim_fetches.append(
            pltpu.make_async_copy(ref.at[rows - rims.shape[1] : rows, :], rims.at[index], sems.at[4 + index])
        )
    for fetch in rim_fetches + fetches:
        fetch.start()
    even_row = jnp.bitwise_and(pos_ref[0], 1) == 0
    even_col = jnp.bitwise_and(pos_ref[1], 1) == 0
    for fetch in rim_fetches:
        fetch.wait()
    fill_tables(even_row, even_col, rims.at[0], rims.at[1], rims.at[2], blocks_ref, share_ref)
    core_rim, other_rim = rims[1], rims[2]
    tiles = side // LANES

    def lines_of(rim):
        return jnp.concatenate([rim[tile * HALO : (tile + 1) * HALO] for tile in range(tiles)], axis=1)
    for start, first in ((0, 0), (side - LANES, LANES)):
        for index, line in enumerate(weight_rows(coef_ref, start, LANES, side, cols_total, pos_ref[1])):
            polys[index : index + 1, first : first + LANES] = line

    def upright(near_block, far_block, start, rows):
        near_block = near_block.astype(jnp.float32)
        far_block = far_block.astype(jnp.float32)
        empty = jnp.zeros((LANES - HALO, LANES), jnp.float32)
        left = jnp.concatenate([jnp.where(even_col, far_block, near_block), empty], axis=0).T
        right = jnp.concatenate([jnp.where(even_col, near_block, far_block), empty], axis=0).T
        padded[0, start : start + rows, :HALO] = left[:rows, :HALO].astype(padded.dtype)
        padded[1, start : start + rows, LANES + HALO :] = right[:rows, : LANES - HALO].astype(padded.dtype)

    for block in range(side // LANES):
        cols = slice(block * LANES, (block + 1) * LANES)
        upright(near_ref[:, cols], far_ref[:, cols], HALO + block * LANES, LANES)
    near_corner = slice(tiles * HALO, (tiles + 1) * HALO)
    far_corner = slice((tiles + 1) * HALO, (tiles + 2) * HALO)
    for upper, start in ((even_row, 0), (jnp.logical_not(even_row), HALO + side)):
        upright(
            jnp.where(upper, other_rim[near_corner], core_rim[near_corner]),
            jnp.where(upper, other_rim[far_corner], core_rim[far_corner]),
            start,
            HALO,
        )
    above = lines_of(jnp.where(even_row, other_rim, core_rim))
    below = lines_of(jnp.where(even_row, core_rim, other_rim))
    for fetch in fetches:
        fetch.wait()
    reach = 2 * LANES - HALO
    padded[0, HALO : HALO + side, HALO:] = sides[0, :, :reach]
    padded[0, :HALO, HALO:] = above[:, :reach]
    padded[0, HALO + side :, HALO:] = below[:, :reach]
    padded[1, HALO : HALO + side, : LANES + HALO] = sides[1, :, LANES - HALO :]
    padded[1, :HALO, : LANES + HALO] = above[:, side - LANES - HALO :]
    padded[1, HALO + side :, : LANES + HALO] = below[:, side - LANES - HALO :]

    tall = side // 2 + HALO
    for end in (0, 1):
        for start in (0, tall):
            summed = jnp.dot(padded[end, start : start + tall, :], across_ref[...], preferred_element_type=jnp.float32)
            for b in range(BASES):
                across[b, start : start + tall, end * LANES : (end + 1) * LANES] = summed[
                    :, b * LANES : (b + 1) * LANES
                ].astype(across.dtype)
    both = slice(0, 2 * LANES)

    def down_step(step, carry):
        start = pl.multiple_of(step * LANES, LANES)
        smoothed = [
            jnp.dot(down_ref[b], across[b, pl.ds(start, LANES + 2 * HALO), :], preferred_element_type=jnp.float32)
            for b in range(BASES)
        ]
        columns[pl.ds(start, LANES), :] = minus_weighted(smoothed, polys, both, start, side, rows_total, pos_ref[0])
        return carry

    lax.fori_loop(0, side // LANES, down_step, 0)
    stores = [
        pltpu.make_async_copy(columns.at[:, :LANES], out_ref.at[:, :LANES], sems.at[0]),
        pltpu.make_async_copy(columns.at[:, LANES:], out_ref.at[:, side - LANES :], sems.at[1]),
    ]
    for store in stores:
        store.start()

    for index, line in enumerate(weight_rows(coef_ref, 0, side, side, cols_total, pos_ref[1])):
        polys[index : index + 1, :] = line
    zeros = jnp.zeros((deep, HALO), ends.dtype)
    for end in (0, 1):
        near_rows = ends[end]
        window = jnp.concatenate([above, near_rows] if end == 0 else [near_rows, below], axis=0)
        window = jnp.concatenate([zeros, window, jnp.zeros((deep, LANES - HALO), ends.dtype)], axis=1)
        parts = [[] for _ in range(BASES)]
        for j in range(1, side // LANES - 1):
            summed = jnp.dot(
                window[:, j * LANES : (j + 2) * LANES], across_ref[...], preferred_element_type=jnp.float32
            )
            for b in range(BASES):
                parts[b].append(summed[:, b * LANES : (b + 1) * LANES].astype(ends.dtype))
        smoothed = [
            jnp.dot(
                down_ref[b, :HALO, :deep], jnp.concatenate(parts[b], axis=1), preferred_element_type=jnp.float32
            )
            for b in range(BASES)
        ]
        lines[end] = minus_weighted(
            smoothed, polys, slice(LANES, LANES + inner), 0 if end == 0 else side - HALO, side, rows_total, pos_ref[0]
        )
        store = pltpu.make_async_copy(
            lines.at[end],
            out_ref.at[pl.ds((side - HALO) * end, HALO), pl.ds(LANES, inner)],
            sems.at[2 + end],
        )
        store.start()
        stores.append(store)
    for store in stores:
        store.wait()


def frame(extent, base, sent, coefficients, position, template, near, far, core, other):
    side = template.shape[0]
    taps = gauss_taps()
    return pl.pallas_call(
        functools.partial(frame_kernel, extent),
        out_shape=(
            jax.ShapeDtypeStruct((side, side), jnp.float32),
            jax.ShapeDtypeStruct((HALO, LANES), jnp.int32),
            jax.ShapeDtypeStruct((8, LANES), jnp.float32),
        ),
        in_specs=[SMEM, SMEM, VMEM, VMEM, ANY, ANY, ANY, VMEM, VMEM, ANY, ANY],
        out_specs=(ANY, VMEM, VMEM),
        scratch_shapes=[
            pltpu.VMEM((2, side, 2 * LANES), jnp.bfloat16),
            pltpu.VMEM((2, 2 * HALO, side), jnp.bfloat16),
            pltpu.VMEM((3, rim_rows(side), LANES), jnp.bfloat16),
            pltpu.VMEM((2, side + 2 * HALO, 2 * LANES), jnp.bfloat16),
            pltpu.VMEM((BASES, side + 2 * HALO, 2 * LANES), jnp.bfloat16),
            pltpu.VMEM((16, side), jnp.float32),
            pltpu.VMEM((side, 2 * LANES), jnp.float32),
            pltpu.VMEM((2, HALO, side - 2 * LANES), jnp.float32),
            pltpu.SemaphoreType.DMA((7,)),
        ],
        input_output_aliases={10: 0},
        compiler_params=pltpu.CompilerParams(vmem_limit_bytes=58 << 20),
        cost_estimate=CHEAP,
        name="matched_frame",
    )(
        coefficients, position, near, far, core, other, sent,
        jnp.asarray(across_band(taps)), jnp.asarray(down_band(taps)), template, base,
    )


def add_kernel(plan, blocks_side, blocks_ref, share_ref, base_ref, *refs):
    count = len(plan)
    messages = refs[:count]
    out_ref, held, staged, hits, slots, seen, base_sems, piece_sems = refs[count:]
    block_side = held.shape[0] // blocks_side

    def area(block):
        row, col = split_index(block, blocks_side)
        rows = pl.ds(pl.multiple_of(row * block_side, block_side), block_side)
        cols = pl.ds(pl.multiple_of(col * block_side, block_side), block_side)
        return rows, cols

    for block in range(blocks_side * blocks_side):
        seen[block] = 0

    found = jnp.int32(0)
    ends = []
    for message, (source, first) in zip(messages, plan):
        for slot in range(CAP):
            block = blocks_ref[source, first + slot]
            hits[found] = block
            slots[found] = slot
            found = found + jnp.where(block >= 0, 1, 0)
        ends.append(found)

    def fetch_base(block):
        rows, cols = area(block)
        return pltpu.make_async_copy(base_ref.at[rows, cols], held.at[rows, cols], base_sems.at[block])

    def store_base(block):
        rows, cols = area(block)
        return pltpu.make_async_copy(held.at[rows, cols], out_ref.at[rows, cols], base_sems.at[block])

    start = jnp.int32(0)
    for message, end in zip(messages, ends):

        def begin(index, carry, message=message):
            block = hits[index]
            piece = piece_at(message, slots[index], block_side)
            pltpu.make_async_copy(piece, staged.at[index], piece_sems.at[index]).start()

            @pl.when(seen[block] == 0)
            def _():
                fetch_base(block).start()
                seen[block] = 1

            return carry

        lax.fori_loop(start, end, begin, 0)
        start = end

    def add(index, carry):
        block = hits[index]
        rows, cols = area(block)
        pltpu.make_async_copy(staged.at[index], staged.at[index], piece_sems.at[index]).wait()

        @pl.when(seen[block] == 1)
        def _():
            fetch_base(block).wait()
            seen[block] = 2

        held[rows, cols] = held[rows, cols] + staged[index].astype(jnp.float32) * share_ref[0, block]
        return carry

    def store(index, carry):
        block = hits[index]

        @pl.when(seen[block] == 2)
        def _():
            store_base(block).start()
            seen[block] = 3

        return carry

    def finish(index, carry):
        block = hits[index]

        @pl.when(seen[block] == 3)
        def _():
            store_base(block).wait()
            seen[block] = 4

        return carry

    for step in (add, store, finish):
        lax.fori_loop(0, found, step, 0)


def add_pieces(name, base, blocks, shares, messages, blocks_side):
    side = base.shape[0]
    plan = tuple((source, first) for _, source, first in messages)
    arrays = [array for array, _, _ in messages]
    room = CAP * len({source for source, _ in plan}) + 8
    per_tile = blocks_side * blocks_side
    return pl.pallas_call(
        functools.partial(add_kernel, plan, blocks_side),
        out_shape=jax.ShapeDtypeStruct(base.shape, base.dtype),
        in_specs=[SMEM, SMEM, ANY] + [ANY] * len(arrays),
        out_specs=ANY,
        scratch_shapes=[
            pltpu.VMEM((side, side), jnp.float32),
            pltpu.VMEM((room, side // blocks_side, side // blocks_side), arrays[0].dtype),
            pltpu.SMEM((room,), jnp.int32),
            pltpu.SMEM((room,), jnp.int32),
            pltpu.SMEM((per_tile,), jnp.int32),
            pltpu.SemaphoreType.DMA((per_tile,)),
            pltpu.SemaphoreType.DMA((room,)),
        ],
        input_output_aliases={2: 0},
        compiler_params=pltpu.CompilerParams(vmem_limit_bytes=58 << 20),
        cost_estimate=CHEAP,
        name=name,
    )(blocks, shares, base, *arrays)


class Grid:
    def __init__(self, rows, cols):
        self.rows, self.cols = rows, cols

    def pairs(self, target):
        found = []
        for row in range(self.rows):
            for col in range(self.cols):
                to_row, to_col = target(row, col)
                if 0 <= to_row < self.rows and 0 <= to_col < self.cols:
                    found.append((row * self.cols + col, to_row * self.cols + to_col))
        return found

    def near(self, array):
        return lax.ppermute(array, ("py", "px"), self.pairs(lambda r, c: (r, c ^ 1)))

    def far(self, array):
        return lax.ppermute(array, ("py", "px"), self.pairs(lambda r, c: (r, c + 1 if c % 2 else c - 1)))

    def beyond(self, array):
        return lax.ppermute(array, ("py", "px"), self.pairs(lambda r, c: (r, c - 2 if c % 2 else c + 2)))

    def core(self, array):
        return lax.ppermute(array, ("py", "px"), self.pairs(lambda r, c: (r ^ 1, c)))

    def other(self, array):
        return lax.ppermute(array, ("py", "px"), self.pairs(lambda r, c: (r + 1 if r % 2 else r - 1, c)))


def on_device(pieces, owner_map, offsets, template, coefficients):
    bar = lax.optimization_barrier
    rows_total = lax.axis_size("py")
    cols_total = lax.axis_size("px")
    grid = Grid(rows_total, cols_total)
    my_row = lax.axis_index("py")
    my_col = lax.axis_index("px")
    position = jnp.stack([my_row, my_col]).astype(jnp.int32)
    count, block_side, _ = pieces.shape
    side = template.shape[0]
    blocks_side = side // block_side

    chunks, own_core, own_other, near_rim, far_rim, labels = order_pieces(
        owner_map, offsets, position, pieces, template, cols_total
    )

    near_strip = grid.near(near_rim)
    far_strip = grid.far(far_rim)
    x0 = grid.near(chunks[0])
    extent = (rows_total, cols_total)
    template, labels = bar((template, labels))
    base = interior(extent, coefficients, position, template)
    rest = chunks[1:]
    x1, x2, x3 = [grid.near(chunk) for chunk in rest]
    own_from = (grid.core(own_core), grid.other(own_other))
    x0, near_strip, far_strip, base, *own_from = bar((x0, near_strip, far_strip, base, *own_from))
    to_core, to_other = row_rims(position, template, near_strip, far_strip, labels)
    core_rows, other_rows = grid.core(to_core), grid.other(to_other)
    z0 = grid.beyond(x0)

    own, near, far = 0, 1, 2
    core, other = 3, 6

    x1, core_rows, other_rows = bar((x1, core_rows, other_rows))
    z1 = grid.beyond(x1)
    base, blocks, shares = frame(
        extent, base, to_core, coefficients, position, template, near_strip, far_strip, core_rows, other_rows
    )

    z0, base = bar((z0, base))
    vz0 = (grid.core(z0), grid.other(z0))
    x2, base = bar((x2, base))
    z2 = grid.beyond(x2)
    vx2 = grid.core(x2)
    z1, base = bar((z1, base))
    early = [(chunk, own, i * CAP) for i, chunk in enumerate(chunks)]
    early += [(own_from[0], core, count), (own_from[1], other, count + CAP)]
    early += [(x0, near, 0), (x1, near, CAP), (x2, near, 2 * CAP), (z0, far, 0)]
    base = add_pieces("add_early", base, blocks, shares, early, blocks_side)

    x3, base = bar((x3, base))
    vx3 = (grid.core(x3), grid.other(x3))
    vz1 = grid.core(z1)
    late = [(x3, near, 3 * CAP), (z1, far, CAP), (z2, far, 2 * CAP), (vx2, core + near, 2 * CAP)]
    late += [(vz0[0], core + far, 0), (vz0[1], other + far, 0), (vz1, core + far, CAP)]
    base = add_pieces("add_late", base, blocks, shares, late, blocks_side)
    last = [(vx3[0], core + near, 3 * CAP), (vx3[1], other + near, 3 * CAP)]
    return add_pieces("add_last", base, blocks, shares, last, blocks_side)


def solution(mesh):
    in_specs = (P(("py", "px"), None, None), P(("py", "px")), P(("py", "px")), P("py", "px"), P())
    out_specs = P("py", "px")
    return jax.shard_map(on_device, mesh=mesh, in_specs=in_specs, out_specs=out_specs, check_vma=False)
```

time: 266 us -> 80 us (0.30)
  local copies, waits for them, and re-layouts: 62 us -> 2.64 us
  starting transfers between devices: 86 us -> 32.2 us
  waiting for transfers between devices: 48.2 us -> 6.25 us
  Pallas kernels: 0 us -> 36.3 us
  other arithmetic: 34.2 us -> 0.65 us
  matrix products: 32.7 us -> 0 us
    ppermute x28 -> x19, starting transfers between devices: 86 us -> 32.2 us  [the longest x4 13.3 us: other(): lax.ppermute(array, ('py', 'px'), self.pairs(lambda r, c: (r + 1 if r % 2...]
    ppermute x28 -> x19, waiting for transfers between devices: 48.2 us -> 6.25 us  [the longest x4 6.21 us: other(): lax.ppermute(array, ('py', 'px'), self.pairs(lambda r, c: (r + 1 if r % 2...]
    pallas_call x0 -> x7, Pallas kernels: none -> 36.3 us  [the longest x3 12.7 us: add_pieces(): pl.pallas_call(functools.partial(add_kernel, plan, blocks_side), out_shap...]
    dot_general x5 -> x0, matrix products: 32.7 us -> none  [the longest x3 15.5 us: on_device(): jnp.dot(band_tables[basis_index], across_part, preferred_element_type=jnp...]
    add x7 -> x0, other arithmetic: 26.4 us -> none  [the longest x6 26.4 us: spatial_weight(): inner_sum + coef_row[term_powers.index((power_u, power_v))] * cols_pow[po...]
    another operation x8 -> x0, local copies, waits for them, and re-layouts: 14.1 us -> none  [the longest x6 14 us: banded(): repeated = jnp.tile(line, out_count)[:out_count * widened]]
    reshape x4 -> x0, local copies, waits for them, and re-layouts: 12.2 us -> none  [the longest x3 12.2 us: banded(): return repeated.reshape(out_count, widened)]
    scatter x2 -> x0, local copies, waits for them, and re-layouts: 9.39 us -> none  [the longest x1 8.62 us: on_device(): jnp.zeros((9 * CAP, block_side, block_side), jnp.bfloat16).at[slot_index]]
  transfers between devices with their start and end apart: 28 -> 19, of which waited for: 5 -> 2; matrix products, arithmetic and copies ran while one was open for 37% -> 0% of each run, Pallas kernels for 0% -> 35%
where the time goes in v2:
time: 80 us; the launch traced here: 78.6 us
  Pallas kernels  36.3 us (45%)
  starting transfers between devices  32.2 us (40%)
  waiting for transfers between devices  6.25 us (8%)
  local copies, waits for them, and re-layouts  2.64 us (3%)
    ppermute x4, starting transfers between devices, other(): lax.ppermute(array, ('py', 'px'), self.pairs(lambda r, c: (r + 1 if r % 2...  13.3 us
    pallas_call x3, Pallas kernels, add_pieces(): pl.pallas_call(functools.partial(add_kernel, plan, blocks_side), out_shap...  12.7 us
    ppermute x3, starting transfers between devices, beyond(): lax.ppermute(array, ('py', 'px'), self.pairs(lambda r, c: (r, c - 2 if c...  9.94 us
    pallas_call x1, Pallas kernels, interior(): pl.pallas_call(functools.partial(interior_kernel, extent), out_shape=jax....  9.3 us
    pallas_call x1, Pallas kernels, frame(): pl.pallas_call(functools.partial(frame_kernel, extent), out_shape=(jax.Sh...  7.28 us
    ppermute x4, waiting for transfers between devices, other(): lax.ppermute(array, ('py', 'px'), self.pairs(lambda r, c: (r + 1 if r % 2...  6.21 us
    ppermute x5, starting transfers between devices, near(): lax.ppermute(array, ('py', 'px'), self.pairs(lambda r, c: (r, c ^ 1)))  6.11 us
    pallas_call x1, Pallas kernels, order_pieces(): pl.pallas_call(functools.partial(order_kernel, cols_total), out_shape=(ch...  4.76 us
  transfers between devices with their start and end apart: 19, of which 2 were waited for; matrix products, arithmetic and copies ran while one was open for 0% of the time, Pallas kernels for 35%

profile of v2, /device:TPU:1, one launch (start us, length us, event | category | flops | bytes accessed | tf_op | source)
XLA Modules:
  0.0 78.6 jit_solution(10762983593865702042)
XLA Ops:
  0.0 0.6 pad_add_fusion.pos_ref
  0.6 4.8 %order_pieces.1 = (bf16[16,128,128]{2,1,0:T(8,128)(2,1)}, bf16[16,128,128]{2,1,0:T(8,128)(2,1)}, bf16[16,128,128]{2,1,0:T(8,128)(2,1)}, bf16[16,128,128]{2,1,0:T...) custom-call(s32[1,64]{1,0:T(1,128)} %bitcast.4, ...), custom_call_target="tpu_custom_call" | custom-call | tf_op jit(solution)/shard_map/order_pieces/pallas_call | solution.py:167
  5.4 2.1 %collective-permute-start.1 = (bf16[16,1152]{1,0:T(8,128)(2,1)}, bf16[16,1152]{1,0:T(8,128)(2,1)S(1)}, u32[]{:S(2)}, u32[]{:S(2)}) collective-permute-start(bf16[16,1152]{1,0:T(8,128)(2,1)} %get-tuple-element.39), channel_id=1, source_target_pairs={{0,1},{1,0},{2,3},{3,2},{4,5},{5,4},{6,7},{7,6},{8,9},{9,8},{10,11... | collective-permute-start | bytes 110600 | tf_op jit(solution)/shard_map/ppermute | solution.py:685
  7.5 0.1 collective-permute-start
  7.6 1.0 %collective-permute-start.3 = (bf16[16,128,128]{2,1,0:T(8,128)(2,1)}, bf16[16,128,128]{2,1,0:T(8,128)(2,1)S(1)}, u32[]{:S(2)}, u32[]{:S(2)}) collective-permute-start(bf16[16,128,128]{2,1,0:T(8,128)(2,1)} %get-tuple-element.43), channel_id=1, source_target_pairs={{0,8},{1,9},{2,10},{3,11},{4,12},{5,13},{6,14},{7,15},{8,0},{9,1},... | collective-permute-start | bytes 1572872 | tf_op jit(solution)/shard_map/ppermute | solution.py:694
  8.6 3.5 %collective-permute-start.4 = (bf16[16,128,128]{2,1,0:T(8,128)(2,1)}, bf16[16,128,128]{2,1,0:T(8,128)(2,1)S(1)}, u32[]{:S(2)}, u32[]{:S(2)}) collective-permute-start(bf16[16,128,128]{2,1,0:T(8,128)(2,1)} %get-tuple-element.44), channel_id=1, source_target_pairs={{8,16},{9,17},{10,18},{11,19},{12,20},{13,21},{14,22},{15,23},{16,... | collective-permute-start | bytes 1572872 | tf_op jit(solution)/shard_map/ppermute | solution.py:697
  12.0 0.7 collective-permute-start.2
  12.7 0.0 collective-permute-done.1.near_ref
  12.8 3.8 %collective-permute-start.5 = (bf16[16,128,128]{2,1,0:T(8,128)(2,1)}, bf16[16,128,128]{2,1,0:T(8,128)(2,1)S(1)}, u32[]{:S(2)}, u32[]{:S(2)}) collective-permute-start(bf16[16,128,128]{2,1,0:T(8,128)(2,1)} %get-tuple-element.47.refs_1_), channel_id=1, source_target_pairs={{0,1},{1,0},{2,3},{3,2},{4,5},{5,4},{6,7},{7,6},{8,9},{9,8},{10,11... | collective-permute-start | bytes 1572872 | tf_op jit(solution)/shard_map/ppermute | solution.py:685
  16.6 9.3 %matched_inside.1.base_ref = f32[1024,1024]{1,0:T(8,128)} custom-call(f32[3,15]{1,0:T(4,128)} %coef_ref.3, s32[2]{0:T(128)} %pad_add_fusion.pos_ref, bf16[1024,1024]{1,0:T(8,128)(2,1)} %template_ref.3, bf16[256,384]{1,0:T(8,128)(2,1)} %constant.12.clone.across_ref, bf16[3,128,160]{2,1,0:T(8,128)(2,1)} %constant.13.clone.down_ref), custom_call_target="tpu_custom_call" | custom-call | flops 8000000000 | bytes 1 | tf_op jit(solution)/shard_map/matched_inside/pallas_call | solution.py:375
  25.9 0.0 collective-permute-done.2.far_ref
  25.9 0.0 collective-permute-done.refs_6_
  25.9 0.0 collective-permute-done.3.refs_4_
  25.9 0.0 collective-permute-done.4.refs_5_
  26.0 3.2 %collective-permute-start.11 = (bf16[16,128,128]{2,1,0:T(8,128)(2,1)S(1)}, bf16[16,128,128]{2,1,0:T(8,128)(2,1)S(1)}, u32[]{:S(2)}, u32[]{:S(2)}) collective-permute-start(bf16[16,128,128]{2,1,0:T(8,128)(2,1)S(1)} %collective-permute-done.refs_6_), channel_id=1, source_target_pairs={{0,2},{2,4},{3,1},{4,6},{5,3},{7,5},{8,10},{10,12},{11,9},{12,14},... | collective-permute-start | bytes 1572872 | tf_op jit(solution)/shard_map/ppermute | solution.py:691
  29.2 0.1 collective-permute-start.10
  29.3 2.3 %row_rims.1 = (bf16[176,128]{1,0:T(8,128)(2,1)}, bf16[176,128]{1,0:T(8,128)(2,1)}) custom-call(s32[2]{0:T(128)} %pad_add_fusion.pos_ref, bf16[1024,1024]{1,0:T(8,128)(2,1)} %template_ref.3, bf16[16,1152]{1,0:T(8,128)(2,1)} %copy-done.17, bf16[16,1152]{1,0:T(8,128)(2,1)} %copy-done.18, bf16[16,128]{1,0:T(8,128)(2,1)} %get-tuple-element.48.label_ref), custom_call_target="tpu_custom_call" | custom-call | tf_op jit(solution)/shard_map/row_rims/pallas_call | solution.py:244
  31.6 0.1 collective-permute-start.6
  31.7 3.4 %collective-permute-start.7 = (bf16[176,128]{1,0:T(8,128)(2,1)}, bf16[176,128]{1,0:T(8,128)(2,1)S(1)}, u32[]{:S(2)}, u32[]{:S(2)}) collective-permute-start(bf16[176,128]{1,0:T(8,128)(2,1)} %get-tuple-element.50), channel_id=1, source_target_pairs={{8,16},{9,17},{10,18},{11,19},{12,20},{13,21},{14,22},{15,23},{16,... | collective-permute-start | bytes 135176 | tf_op jit(solution)/shard_map/ppermute | solution.py:697
  35.0 0.0 collective-permute-done.5.refs_7_
  35.0 0.0 collective-permute-done.6.core_ref
  35.1 2.5 %collective-permute-done.7.other_ref = bf16[176,128]{1,0:T(8,128)(2,1)S(1)} collective-permute-done((bf16[176,128]{1,0:T(8,128)(2,1)}, bf16[176,128]{1,0:T(8,128)(2,1)S(1)}, u32[]{:S(2)}, u32[]{:S(2)}) %collective-permute-start.7) | collective-permute-done | bytes 45088 | tf_op jit(solution)/shard_map/ppermute | solution.py:697
  37.5 3.2 %collective-permute-start.9 = (bf16[16,128,128]{2,1,0:T(8,128)(2,1)S(1)}, bf16[16,128,128]{2,1,0:T(8,128)(2,1)S(1)}, u32[]{:S(2)}, u32[]{:S(2)}) collective-permute-start(bf16[16,128,128]{2,1,0:T(8,128)(2,1)S(1)} %collective-permute-done.5.refs_7_), channel_id=1, source_target_pairs={{0,2},{2,4},{3,1},{4,6},{5,3},{7,5},{8,10},{10,12},{11,9},{12,14},... | collective-permute-start | bytes 1572872 | tf_op jit(solution)/shard_map/ppermute | solution.py:691
  40.7 0.1 collective-permute-start.8
  40.8 7.3 %matched_frame.1 = (f32[1024,1024]{1,0:T(8,128)}, s32[16,128]{1,0:T(8,128)}, f32[8,128]{1,0:T(8,128)}) custom-call(f32[3,15]{1,0:T(4,128)} %coef_ref.3, s32[2]{0:T(128)} %pad_add_fusion.pos_ref, bf16[16,1152]{1,0:T(8,128)(2,1)} %copy-done.17, bf16[16,1152]{1,0:T(8,128)(2,1)} %copy-done.18, ...), custom_call_target="tpu_custom_call", output_to_operand_aliasing={{0}: (10, {})} | custom-call | tf_op jit(solution)/shard_map/matched_frame/pallas_call | solution.py:526
  48.2 0.0 collective-permute-done.11.refs_9_
  48.2 0.0 collective-permute-done.10.refs_8_
  48.2 3.5 %collective-permute-start.12 = (bf16[16,128,128]{2,1,0:T(8,128)(2,1)S(1)}, bf16[16,128,128]{2,1,0:T(8,128)(2,1)S(1)}, u32[]{:S(2)}, u32[]{:S(2)}) collective-permute-start(bf16[16,128,128]{2,1,0:T(8,128)(2,1)S(1)} %collective-permute-done.10.refs_8_), channel_id=1, source_target_pairs={{0,2},{2,4},{3,1},{4,6},{5,3},{7,5},{8,10},{10,12},{11,9},{12,14},... | collective-permute-start | bytes 1572872 | tf_op jit(solution)/shard_map/ppermute | solution.py:691
  51.7 0.1 collective-permute-start.13
  51.8 0.5 collective-permute-start.14
  52.3 0.0 collective-permute-done.9.refs_1_
  52.3 4.2 %collective-permute-start.15 = (bf16[16,128,128]{2,1,0:T(8,128)(2,1)S(1)}, bf16[16,128,128]{2,1,0:T(8,128)(2,1)S(1)}, u32[]{:S(2)}, u32[]{:S(2)}) collective-permute-start(bf16[16,128,128]{2,1,0:T(8,128)(2,1)S(1)} %collective-permute-done.11.refs_9_), channel_id=1, source_target_pairs={{8,16},{9,17},{10,18},{11,19},{12,20},{13,21},{14,22},{15,23},{16,... | collective-permute-start | bytes 1572872 | tf_op jit(solution)/shard_map/ppermute | solution.py:697
  56.5 6.0 %add_early.1.base_ref = f32[1024,1024]{1,0:T(8,128)} custom-call(s32[16,128]{1,0:T(8,128)} %get-tuple-element.54.blocks_ref, f32[8,128]{1,0:T(8,128)} %get-tuple-element.55.share_ref, f32[1024,1024]{1,0:T(8,128)} %get-tuple-element.63.base_ref, bf16[16,128,128]{2,1,0:T(8,128)(2,1)} %get-tuple-element.38.refs_0_, ...), custom_call_target="tpu_custom_call", output_to_operand_aliasing={{}: (2, {})} | custom-call | tf_op jit(solution)/shard_map/add_early/pallas_call | solution.py:650
  62.5 0.0 collective-permute-done.8.refs_0_
  62.5 0.1 collective-permute-start.16
  62.6 0.0 collective-permute-done.12.refs_2_
  62.6 0.5 collective-permute-start.17
  63.1 0.0 collective-permute-done.13.refs_3_
  63.1 2.3 %collective-permute-start.18 = (bf16[16,128,128]{2,1,0:T(8,128)(2,1)S(1)}, bf16[16,128,128]{2,1,0:T(8,128)(2,1)S(1)}, u32[]{:S(2)}, u32[]{:S(2)}) collective-permute-start(bf16[16,128,128]{2,1,0:T(8,128)(2,1)S(1)} %collective-permute-done.8.refs_0_), channel_id=1, source_target_pairs={{8,16},{9,17},{10,18},{11,19},{12,20},{13,21},{14,22},{15,23},{16,... | collective-permute-start | bytes 1572872 | tf_op jit(solution)/shard_map/ppermute | solution.py:697
  65.4 0.0 collective-permute-done.14.refs_4_
  65.4 0.0 collective-permute-done.15.refs_5_
  65.5 0.7 copy-done.12
  66.2 0.2 copy-done.13
  66.4 0.8 %copy-done.15 = bf16[16,128,128]{2,1,0:T(8,128)(2,1)} copy-done((bf16[16,128,128]{2,1,0:T(8,128)(2,1)}, bf16[16,128,128]{2,1,0:T(8,128)(2,1)S(1)}, u32[]{:S(2)}) %copy-start.15) | copy-done | bytes 524312
  67.2 2.6 %add_late.1.base_ref = f32[1024,1024]{1,0:T(8,128)} custom-call(s32[16,128]{1,0:T(8,128)} %get-tuple-element.54.blocks_ref, f32[8,128]{1,0:T(8,128)} %get-tuple-element.55.share_ref, f32[1024,1024]{1,0:T(8,128)} %add_early.1.base_ref, bf16[16,128,128]{2,1,0:T(8,128)(2,1)} %copy-done.8, ...), custom_call_target="tpu_custom_call", output_to_operand_aliasing={{}: (2, {})} | custom-call | tf_op jit(solution)/shard_map/add_late/pallas_call | solution.py:650
  69.8 3.7 %collective-permute-done.18.refs_1_ = bf16[16,128,128]{2,1,0:T(8,128)(2,1)S(1)} collective-permute-done((bf16[16,128,128]{2,1,0:T(8,128)(2,1)S(1)}, bf16[16,128,128]{2,1,0:T(8,128)(2,1)S(1)}, u32[]{:S(2)}, u32[]{:S(2)}) %collective-permute-start.18) | collective-permute-done | bytes 524320 | tf_op jit(solution)/shard_map/ppermute | solution.py:697
  73.6 0.8 %copy-done.16 = bf16[16,128,128]{2,1,0:T(8,128)(2,1)} copy-done((bf16[16,128,128]{2,1,0:T(8,128)(2,1)}, bf16[16,128,128]{2,1,0:T(8,128)(2,1)S(1)}, u32[]{:S(2)}) %copy-start.16) | copy-done | bytes 524312
  74.4 4.2 %add_last.1 = f32[1024,1024]{1,0:T(8,128)} custom-call(s32[16,128]{1,0:T(8,128)} %get-tuple-element.54.blocks_ref, f32[8,128]{1,0:T(8,128)} %get-tuple-element.55.share_ref, f32[1024,1024]{1,0:T(8,128)} %add_late.1.base_ref, bf16[16,128,128]{2,1,0:T(8,128)(2,1)} %copy-done.14, bf16[16,128,128]{2,1,0:T(8,128)(2,1)} %copy-done.16), custom_call_target="tpu_custom_call", output_to_operand_aliasing={{}: (2, {})} | custom-call | tf_op jit(solution)/shard_map/add_last/pallas_call | solution.py:650
  (40 shorter events, 0.1 us)
Async XLA Ops:
  5.4 7.3 %collective-permute-start.1 = (bf16[16,1152]{1,0:T(8,128)(2,1)}, bf16[16,1152]{1,0:T(8,128)(2,1)S(1)}, u32[]{:S(2)}, u32[]{:S(2)}) collective-permute-start(bf16[16,1152]{1,0:T(8,128)(2,1)} %get-tuple-element.39), channel_id=1, source_target_pairs={{0,1},{1,0},{2,3},{3,2},{4,5},{5,4},{6,7},{7,6},{8,9},{9,8},{10,11... | collective-permute-start | bytes 110600 | tf_op jit(solution)/shard_map/ppermute | solution.py:685
  7.5 18.4 %collective-permute-start = (bf16[16,128,128]{2,1,0:T(8,128)(2,1)}, bf16[16,128,128]{2,1,0:T(8,128)(2,1)S(1)}, u32[]{:S(2)}, u32[]{:S(2)}) collective-permute-start(bf16[16,128,128]{2,1,0:T(8,128)(2,1)} %get-tuple-element.38.refs_0_), channel_id=1, source_target_pairs={{0,1},{1,0},{2,3},{3,2},{4,5},{5,4},{6,7},{7,6},{8,9},{9,8},{10,11... | collective-permute-start | bytes 1572872 | tf_op jit(solution)/shard_map/ppermute | solution.py:685
  7.6 18.3 %collective-permute-start.3 = (bf16[16,128,128]{2,1,0:T(8,128)(2,1)}, bf16[16,128,128]{2,1,0:T(8,128)(2,1)S(1)}, u32[]{:S(2)}, u32[]{:S(2)}) collective-permute-start(bf16[16,128,128]{2,1,0:T(8,128)(2,1)} %get-tuple-element.43), channel_id=1, source_target_pairs={{0,8},{1,9},{2,10},{3,11},{4,12},{5,13},{6,14},{7,15},{8,0},{9,1},... | collective-permute-start | bytes 1572872 | tf_op jit(solution)/shard_map/ppermute | solution.py:694
  8.6 17.4 %collective-permute-start.4 = (bf16[16,128,128]{2,1,0:T(8,128)(2,1)}, bf16[16,128,128]{2,1,0:T(8,128)(2,1)S(1)}, u32[]{:S(2)}, u32[]{:S(2)}) collective-permute-start(bf16[16,128,128]{2,1,0:T(8,128)(2,1)} %get-tuple-element.44), channel_id=1, source_target_pairs={{8,16},{9,17},{10,18},{11,19},{12,20},{13,21},{14,22},{15,23},{16,... | collective-permute-start | bytes 1572872 | tf_op jit(solution)/shard_map/ppermute | solution.py:697
  12.0 13.8 %collective-permute-start.2 = (bf16[16,1152]{1,0:T(8,128)(2,1)}, bf16[16,1152]{1,0:T(8,128)(2,1)S(1)}, u32[]{:S(2)}, u32[]{:S(2)}) collective-permute-start(bf16[16,1152]{1,0:T(8,128)(2,1)} %get-tuple-element.40), channel_id=1, source_target_pairs={{1,2},{2,1},{3,4},{4,3},{5,6},{6,5},{9,10},{10,9},{11,12},{12,11},... | collective-permute-start | bytes 110600 | tf_op jit(solution)/shard_map/ppermute | solution.py:688
  12.7 13.1 %copy-start.17 = (bf16[16,1152]{1,0:T(8,128)(2,1)}, bf16[16,1152]{1,0:T(8,128)(2,1)S(1)}, u32[]{:S(2)}) copy-start(bf16[16,1152]{1,0:T(8,128)(2,1)S(1)} %collective-permute-done.1.near_ref) | copy-start | bytes 110596
  12.7 16.5 %copy-start.1 = (bf16[16,128,128]{2,1,0:T(8,128)(2,1)S(1)}, bf16[16,128,128]{2,1,0:T(8,128)(2,1)}, u32[]{:S(2)}) copy-start(bf16[16,128,128]{2,1,0:T(8,128)(2,1)} %get-tuple-element.58.refs_2_) | copy-start | bytes 1572868
  12.8 28.0 %copy-start = (bf16[16,128,128]{2,1,0:T(8,128)(2,1)S(1)}, bf16[16,128,128]{2,1,0:T(8,128)(2,1)}, u32[]{:S(2)}) copy-start(bf16[16,128,128]{2,1,0:T(8,128)(2,1)} %get-tuple-element.56.refs_3_) | copy-start | bytes 1572868
  12.8 22.3 %collective-permute-start.5 = (bf16[16,128,128]{2,1,0:T(8,128)(2,1)}, bf16[16,128,128]{2,1,0:T(8,128)(2,1)S(1)}, u32[]{:S(2)}, u32[]{:S(2)}) collective-permute-start(bf16[16,128,128]{2,1,0:T(8,128)(2,1)} %get-tuple-element.47.refs_1_), channel_id=1, source_target_pairs={{0,1},{1,0},{2,3},{3,2},{4,5},{5,4},{6,7},{7,6},{8,9},{9,8},{10,11... | collective-permute-start | bytes 1572872 | tf_op jit(solution)/shard_map/ppermute | solution.py:685
  25.9 3.4 %copy-start.18 = (bf16[16,1152]{1,0:T(8,128)(2,1)}, bf16[16,1152]{1,0:T(8,128)(2,1)S(1)}, u32[]{:S(2)}) copy-start(bf16[16,1152]{1,0:T(8,128)(2,1)S(1)} %collective-permute-done.2.far_ref) | copy-start | bytes 110596
  25.9 22.2 %copy-start.2 = (bf16[16,128,128]{2,1,0:T(8,128)(2,1)}, bf16[16,128,128]{2,1,0:T(8,128)(2,1)S(1)}, u32[]{:S(2)}) copy-start(bf16[16,128,128]{2,1,0:T(8,128)(2,1)S(1)} %collective-permute-done.refs_6_) | copy-start | bytes 1572868
  25.9 22.2 %copy-start.3 = (bf16[16,128,128]{2,1,0:T(8,128)(2,1)}, bf16[16,128,128]{2,1,0:T(8,128)(2,1)S(1)}, u32[]{:S(2)}) copy-start(bf16[16,128,128]{2,1,0:T(8,128)(2,1)S(1)} %collective-permute-done.3.refs_4_) | copy-start | bytes 1572868
  25.9 22.2 %copy-start.4 = (bf16[16,128,128]{2,1,0:T(8,128)(2,1)}, bf16[16,128,128]{2,1,0:T(8,128)(2,1)S(1)}, u32[]{:S(2)}) copy-start(bf16[16,128,128]{2,1,0:T(8,128)(2,1)S(1)} %collective-permute-done.4.refs_5_) | copy-start | bytes 1572868
  26.0 22.2 %collective-permute-start.11 = (bf16[16,128,128]{2,1,0:T(8,128)(2,1)S(1)}, bf16[16,128,128]{2,1,0:T(8,128)(2,1)S(1)}, u32[]{:S(2)}, u32[]{:S(2)}) collective-permute-start(bf16[16,128,128]{2,1,0:T(8,128)(2,1)S(1)} %collective-permute-done.refs_6_), channel_id=1, source_target_pairs={{0,2},{2,4},{3,1},{4,6},{5,3},{7,5},{8,10},{10,12},{11,9},{12,14},... | collective-permute-start | bytes 1572872 | tf_op jit(solution)/shard_map/ppermute | solution.py:691
  29.2 19.0 %collective-permute-start.10 = (bf16[16,128,128]{2,1,0:T(8,128)(2,1)S(1)}, bf16[16,128,128]{2,1,0:T(8,128)(2,1)S(1)}, u32[]{:S(2)}, u32[]{:S(2)}) collective-permute-start(bf16[16,128,128]{2,1,0:T(8,128)(2,1)S(1)} %copy-done.1), channel_id=1, source_target_pairs={{0,1},{1,0},{2,3},{3,2},{4,5},{5,4},{6,7},{7,6},{8,9},{9,8},{10,11... | collective-permute-start | bytes 1572872 | tf_op jit(solution)/shard_map/ppermute | solution.py:685
  31.6 3.5 %collective-permute-start.6 = (bf16[176,128]{1,0:T(8,128)(2,1)}, bf16[176,128]{1,0:T(8,128)(2,1)S(1)}, u32[]{:S(2)}, u32[]{:S(2)}) collective-permute-start(bf16[176,128]{1,0:T(8,128)(2,1)} %get-tuple-element.49.sent_ref), channel_id=1, source_target_pairs={{0,8},{1,9},{2,10},{3,11},{4,12},{5,13},{6,14},{7,15},{8,0},{9,1},... | collective-permute-start | bytes 135176 | tf_op jit(solution)/shard_map/ppermute | solution.py:694
  31.7 5.9 %collective-permute-start.7 = (bf16[176,128]{1,0:T(8,128)(2,1)}, bf16[176,128]{1,0:T(8,128)(2,1)S(1)}, u32[]{:S(2)}, u32[]{:S(2)}) collective-permute-start(bf16[176,128]{1,0:T(8,128)(2,1)} %get-tuple-element.50), channel_id=1, source_target_pairs={{8,16},{9,17},{10,18},{11,19},{12,20},{13,21},{14,22},{15,23},{16,... | collective-permute-start | bytes 135176 | tf_op jit(solution)/shard_map/ppermute | solution.py:697
  35.0 21.4 %copy-start.6 = (bf16[16,128,128]{2,1,0:T(8,128)(2,1)}, bf16[16,128,128]{2,1,0:T(8,128)(2,1)S(1)}, u32[]{:S(2)}) copy-start(bf16[16,128,128]{2,1,0:T(8,128)(2,1)S(1)} %collective-permute-done.5.refs_7_) | copy-start | bytes 1572868
  35.1 5.8 %copy-start.19 = (bf16[176,128]{1,0:T(8,128)(2,1)}, bf16[176,128]{1,0:T(8,128)(2,1)S(1)}, u32[]{:S(2)}) copy-start(bf16[176,128]{1,0:T(8,128)(2,1)S(1)} %collective-permute-done.6.core_ref) | copy-start | bytes 135172
  37.5 3.3 %copy-start.20 = (bf16[176,128]{1,0:T(8,128)(2,1)}, bf16[176,128]{1,0:T(8,128)(2,1)S(1)}, u32[]{:S(2)}) copy-start(bf16[176,128]{1,0:T(8,128)(2,1)S(1)} %collective-permute-done.7.other_ref) | copy-start | bytes 135172
  37.5 14.8 %collective-permute-start.9 = (bf16[16,128,128]{2,1,0:T(8,128)(2,1)S(1)}, bf16[16,128,128]{2,1,0:T(8,128)(2,1)S(1)}, u32[]{:S(2)}, u32[]{:S(2)}) collective-permute-start(bf16[16,128,128]{2,1,0:T(8,128)(2,1)S(1)} %collective-permute-done.5.refs_7_), channel_id=1, source_target_pairs={{0,2},{2,4},{3,1},{4,6},{5,3},{7,5},{8,10},{10,12},{11,9},{12,14},... | collective-permute-start | bytes 1572872 | tf_op jit(solution)/shard_map/ppermute | solution.py:691
  40.7 21.7 %collective-permute-start.8 = (bf16[16,128,128]{2,1,0:T(8,128)(2,1)S(1)}, bf16[16,128,128]{2,1,0:T(8,128)(2,1)S(1)}, u32[]{:S(2)}, u32[]{:S(2)}) collective-permute-start(bf16[16,128,128]{2,1,0:T(8,128)(2,1)S(1)} %copy-done), channel_id=1, source_target_pairs={{0,1},{1,0},{2,3},{3,2},{4,5},{5,4},{6,7},{7,6},{8,9},{9,8},{10,11... | collective-permute-start | bytes 1572872 | tf_op jit(solution)/shard_map/ppermute | solution.py:685
  48.2 8.3 %copy-start.5 = (bf16[16,128,128]{2,1,0:T(8,128)(2,1)}, bf16[16,128,128]{2,1,0:T(8,128)(2,1)S(1)}, u32[]{:S(2)}) copy-start(bf16[16,128,128]{2,1,0:T(8,128)(2,1)S(1)} %collective-permute-done.11.refs_9_) | copy-start | bytes 1572868
  48.2 8.3 %copy-start.7 = (bf16[16,128,128]{2,1,0:T(8,128)(2,1)}, bf16[16,128,128]{2,1,0:T(8,128)(2,1)S(1)}, u32[]{:S(2)}) copy-start(bf16[16,128,128]{2,1,0:T(8,128)(2,1)S(1)} %collective-permute-done.10.refs_8_) | copy-start | bytes 1572868
  48.2 14.4 %collective-permute-start.12 = (bf16[16,128,128]{2,1,0:T(8,128)(2,1)S(1)}, bf16[16,128,128]{2,1,0:T(8,128)(2,1)S(1)}, u32[]{:S(2)}, u32[]{:S(2)}) collective-permute-start(bf16[16,128,128]{2,1,0:T(8,128)(2,1)S(1)} %collective-permute-done.10.refs_8_), channel_id=1, source_target_pairs={{0,2},{2,4},{3,1},{4,6},{5,3},{7,5},{8,10},{10,12},{11,9},{12,14},... | collective-permute-start | bytes 1572872 | tf_op jit(solution)/shard_map/ppermute | solution.py:691
  51.7 11.4 %collective-permute-start.13 = (bf16[16,128,128]{2,1,0:T(8,128)(2,1)S(1)}, bf16[16,128,128]{2,1,0:T(8,128)(2,1)S(1)}, u32[]{:S(2)}, u32[]{:S(2)}) collective-permute-start(bf16[16,128,128]{2,1,0:T(8,128)(2,1)S(1)} %collective-permute-done.10.refs_8_), channel_id=1, source_target_pairs={{0,8},{1,9},{2,10},{3,11},{4,12},{5,13},{6,14},{7,15},{8,0},{9,1},... | collective-permute-start | bytes 1572872 | tf_op jit(solution)/shard_map/ppermute | solution.py:694
  51.8 13.6 %collective-permute-start.14 = (bf16[16,128,128]{2,1,0:T(8,128)(2,1)S(1)}, bf16[16,128,128]{2,1,0:T(8,128)(2,1)S(1)}, u32[]{:S(2)}, u32[]{:S(2)}) collective-permute-start(bf16[16,128,128]{2,1,0:T(8,128)(2,1)S(1)} %collective-permute-done.11.refs_9_), channel_id=1, source_target_pairs={{0,8},{1,9},{2,10},{3,11},{4,12},{5,13},{6,14},{7,15},{8,0},{9,1},... | collective-permute-start | bytes 1572872 | tf_op jit(solution)/shard_map/ppermute | solution.py:694
  52.3 10.2 %copy-start.9 = (bf16[16,128,128]{2,1,0:T(8,128)(2,1)}, bf16[16,128,128]{2,1,0:T(8,128)(2,1)S(1)}, u32[]{:S(2)}) copy-start(bf16[16,128,128]{2,1,0:T(8,128)(2,1)S(1)} %collective-permute-done.9.refs_1_) | copy-start | bytes 1572868
  52.3 13.2 %collective-permute-start.15 = (bf16[16,128,128]{2,1,0:T(8,128)(2,1)S(1)}, bf16[16,128,128]{2,1,0:T(8,128)(2,1)S(1)}, u32[]{:S(2)}, u32[]{:S(2)}) collective-permute-start(bf16[16,128,128]{2,1,0:T(8,128)(2,1)S(1)} %collective-permute-done.11.refs_9_), channel_id=1, source_target_pairs={{8,16},{9,17},{10,18},{11,19},{12,20},{13,21},{14,22},{15,23},{16,... | collective-permute-start | bytes 1572872 | tf_op jit(solution)/shard_map/ppermute | solution.py:697
  62.5 3.0 %copy-start.8 = (bf16[16,128,128]{2,1,0:T(8,128)(2,1)}, bf16[16,128,128]{2,1,0:T(8,128)(2,1)S(1)}, u32[]{:S(2)}) copy-start(bf16[16,128,128]{2,1,0:T(8,128)(2,1)S(1)} %collective-permute-done.8.refs_0_) | copy-start | bytes 1572868
  62.5 2.9 %collective-permute-start.16 = (bf16[16,128,128]{2,1,0:T(8,128)(2,1)S(1)}, bf16[16,128,128]{2,1,0:T(8,128)(2,1)S(1)}, u32[]{:S(2)}, u32[]{:S(2)}) collective-permute-start(bf16[16,128,128]{2,1,0:T(8,128)(2,1)S(1)} %collective-permute-done.9.refs_1_), channel_id=1, source_target_pairs={{0,8},{1,9},{2,10},{3,11},{4,12},{5,13},{6,14},{7,15},{8,0},{9,1},... | collective-permute-start | bytes 1572872 | tf_op jit(solution)/shard_map/ppermute | solution.py:694
  62.6 2.9 %copy-start.10 = (bf16[16,128,128]{2,1,0:T(8,128)(2,1)}, bf16[16,128,128]{2,1,0:T(8,128)(2,1)S(1)}, u32[]{:S(2)}) copy-start(bf16[16,128,128]{2,1,0:T(8,128)(2,1)S(1)} %collective-permute-done.12.refs_2_) | copy-start | bytes 1572868
  62.6 7.2 %collective-permute-start.17 = (bf16[16,128,128]{2,1,0:T(8,128)(2,1)S(1)}, bf16[16,128,128]{2,1,0:T(8,128)(2,1)S(1)}, u32[]{:S(2)}, u32[]{:S(2)}) collective-permute-start(bf16[16,128,128]{2,1,0:T(8,128)(2,1)S(1)} %collective-permute-done.8.refs_0_), channel_id=1, source_target_pairs={{0,8},{1,9},{2,10},{3,11},{4,12},{5,13},{6,14},{7,15},{8,0},{9,1},... | collective-permute-start | bytes 1572872 | tf_op jit(solution)/shard_map/ppermute | solution.py:694
  63.1 2.4 %copy-start.11 = (bf16[16,128,128]{2,1,0:T(8,128)(2,1)}, bf16[16,128,128]{2,1,0:T(8,128)(2,1)S(1)}, u32[]{:S(2)}) copy-start(bf16[16,128,128]{2,1,0:T(8,128)(2,1)S(1)} %collective-permute-done.13.refs_3_) | copy-start | bytes 1572868
  63.1 10.5 %collective-permute-start.18 = (bf16[16,128,128]{2,1,0:T(8,128)(2,1)S(1)}, bf16[16,128,128]{2,1,0:T(8,128)(2,1)S(1)}, u32[]{:S(2)}, u32[]{:S(2)}) collective-permute-start(bf16[16,128,128]{2,1,0:T(8,128)(2,1)S(1)} %collective-permute-done.8.refs_0_), channel_id=1, source_target_pairs={{8,16},{9,17},{10,18},{11,19},{12,20},{13,21},{14,22},{15,23},{16,... | collective-permute-start | bytes 1572872 | tf_op jit(solution)/shard_map/ppermute | solution.py:697
  65.4 0.8 %copy-start.12 = (bf16[16,128,128]{2,1,0:T(8,128)(2,1)}, bf16[16,128,128]{2,1,0:T(8,128)(2,1)S(1)}, u32[]{:S(2)}) copy-start(bf16[16,128,128]{2,1,0:T(8,128)(2,1)S(1)} %collective-permute-done.14.refs_4_) | copy-start | bytes 1572868
  65.5 1.0 %copy-start.13 = (bf16[16,128,128]{2,1,0:T(8,128)(2,1)}, bf16[16,128,128]{2,1,0:T(8,128)(2,1)S(1)}, u32[]{:S(2)}) copy-start(bf16[16,128,128]{2,1,0:T(8,128)(2,1)S(1)} %collective-permute-done.15.refs_5_) | copy-start | bytes 1572868
  66.4 0.8 %copy-start.15 = (bf16[16,128,128]{2,1,0:T(8,128)(2,1)}, bf16[16,128,128]{2,1,0:T(8,128)(2,1)S(1)}, u32[]{:S(2)}) copy-start(bf16[16,128,128]{2,1,0:T(8,128)(2,1)S(1)} %collective-permute-done.16.refs_6_) | copy-start | bytes 1572868
  69.8 3.8 %copy-start.14 = (bf16[16,128,128]{2,1,0:T(8,128)(2,1)}, bf16[16,128,128]{2,1,0:T(8,128)(2,1)S(1)}, u32[]{:S(2)}) copy-start(bf16[16,128,128]{2,1,0:T(8,128)(2,1)S(1)} %collective-permute-done.17.refs_0_) | copy-start | bytes 1572868
  73.6 0.8 %copy-start.16 = (bf16[16,128,128]{2,1,0:T(8,128)(2,1)}, bf16[16,128,128]{2,1,0:T(8,128)(2,1)S(1)}, u32[]{:S(2)}) copy-start(bf16[16,128,128]{2,1,0:T(8,128)(2,1)S(1)} %collective-permute-done.18.refs_1_) | copy-start | bytes 1572868

commit v3 on v2

--- a/solution.py
+++ b/solution.py
@@ -162,7 +162,7 @@
     side = template.shape[0]
     parts = count // CAP + 2
     chunk = jax.ShapeDtypeStruct((CAP, block_side, block_side), pieces.dtype)
-    mail = chunk
+    mail = jax.ShapeDtypeStruct((2 * CAP, block_side, block_side), pieces.dtype)
     rim = jax.ShapeDtypeStruct((HALO, side + LANES), template.dtype)
     *outs, near, far, labels = pl.pallas_call(
         functools.partial(order_kernel, cols_total),
@@ -251,10 +251,37 @@
             pltpu.VMEM((2, rim_rows(side), LANES), template.dtype),
             pltpu.SemaphoreType.DMA((4,)),
         ],
-        compiler_params=pltpu.CompilerParams(vmem_limit_bytes=58 << 20),
+        compiler_params=pltpu.CompilerParams(vmem_limit_bytes=6 << 20),
         cost_estimate=CHEAP,
         name="row_rims",
     )(position, template, near, far, labels)
+
+
+def forward_kernel(part_ref, core_in, other_in, core_out, other_out, sems):
+    count = part_ref.shape[0]
+    stores = [
+        pltpu.make_async_copy(part_ref, out_ref.at[pl.ds(count, count)], sems.at[index])
+        for index, out_ref in enumerate((core_out, other_out))
+    ]
+    for store in stores:
+        store.start()
+    for store in stores:
+        store.wait()
+
+
+def add_forwarded(part, to_core, to_other):
+    message = jax.ShapeDtypeStruct(to_core.shape, to_core.dtype)
+    return pl.pallas_call(
+        forward_kernel,
+        out_shape=(message, message),
+        in_specs=[VMEM, ANY, ANY],
+        out_specs=(ANY, ANY),
+        scratch_shapes=[pltpu.SemaphoreType.DMA((2,))],
+        input_output_aliases={1: 0, 2: 1},
+        compiler_params=pltpu.CompilerParams(vmem_limit_bytes=6 << 20),
+        cost_estimate=CHEAP,
+        name="forward_pieces",
+    )(part, to_core, to_other)
 
 
 def fill_tables(even_row, even_col, own_ref, core_ref, other_ref, blocks_ref, share_ref):
@@ -313,11 +340,20 @@
 
 
 def interior_kernel(
-    extent, coef_ref, pos_ref, centre_ref, across_ref, down_ref, out_ref, padded, across, polys, ready, sems
+    extent, coef_ref, pos_ref, centre_ref, across_ref, down_ref, out_ref, sides_ref, ends_ref,
+    padded, across, polys, ready, sems,
 ):
     side = centre_ref.shape[0]
     rows_total, cols_total = extent
     inner = side - 2 * LANES
+    copies = [
+        pltpu.make_async_copy(centre_ref.at[:, : 2 * LANES], sides_ref.at[0], sems.at[2]),
+        pltpu.make_async_copy(centre_ref.at[:, side - 2 * LANES :], sides_ref.at[1], sems.at[3]),
+        pltpu.make_async_copy(centre_ref.at[: 2 * HALO, :], ends_ref.at[0], sems.at[4]),
+        pltpu.make_async_copy(centre_ref.at[side - 2 * HALO :, :], ends_ref.at[1], sems.at[5]),
+    ]
+    for copy in copies:
+        copy.start()
     reach = inner + LANES
     padded[:, :reach] = centre_ref[:, LANES - HALO : LANES - HALO + reach]
     for index, line in enumerate(weight_rows(coef_ref, LANES, inner, side, cols_total, pos_ref[1])):
@@ -366,6 +402,8 @@
     lax.fori_loop(0, side // LANES, down_step, 0)
     for slot in (0, 1):
         send(0, slot).wait()
+    for copy in copies:
+        copy.wait()
 
 
 def interior(extent, coefficients, position, centre):
@@ -374,97 +412,62 @@
     taps = gauss_taps()
     return pl.pallas_call(
         functools.partial(interior_kernel, extent),
-        out_shape=jax.ShapeDtypeStruct((side, side), jnp.float32),
+        out_shape=(
+            jax.ShapeDtypeStruct((side, side), jnp.float32),
+            jax.ShapeDtypeStruct((2, side, 2 * LANES), centre.dtype),
+            jax.ShapeDtypeStruct((2, 2 * HALO, side), centre.dtype),
+        ),
         in_specs=[SMEM, SMEM] + [VMEM] * 3,
-        out_specs=ANY,
+        out_specs=(ANY, ANY, ANY),
         scratch_shapes=[
             pltpu.VMEM((side, inner + LANES), jnp.bfloat16),
             pltpu.VMEM((BASES, side + 2 * HALO, inner), jnp.bfloat16),
             pltpu.VMEM((16, inner), jnp.float32),
             pltpu.VMEM((2, LANES, inner), jnp.float32),
-            pltpu.SemaphoreType.DMA((2,)),
+            pltpu.SemaphoreType.DMA((6,)),
         ],
-        compiler_params=pltpu.CompilerParams(vmem_limit_bytes=58 << 20),
+        compiler_params=pltpu.CompilerParams(vmem_limit_bytes=40 << 20),
         cost_estimate=pl.CostEstimate(flops=int(8e9), bytes_accessed=1, transcendentals=0),
         name="matched_inside",
     )(coefficients, position, centre, jnp.asarray(across_band(taps)), jnp.asarray(down_band(taps)))
 
 
-def frame_kernel(
-    extent, coef_ref, pos_ref, near_ref, far_ref, core_ref, other_ref, sent_ref, across_ref, down_ref, template_ref,
-    base_ref, out_ref, blocks_ref, share_ref, sides, ends, rims, padded, across, polys, columns, lines, sems,
+def upright(near_block, far_block, even_col):
+    near_block = near_block.astype(jnp.float32)
+    far_block = far_block.astype(jnp.float32)
+    empty = jnp.zeros((LANES - HALO, LANES), jnp.float32)
+    left = jnp.concatenate([jnp.where(even_col, far_block, near_block), empty], axis=0).T
+    right = jnp.concatenate([jnp.where(even_col, near_block, far_block), empty], axis=0).T
+    return left.astype(jnp.bfloat16), right.astype(jnp.bfloat16)
+
+
+def sides_kernel(
+    extent, coef_ref, pos_ref, near_ref, far_ref, across_ref, down_ref, sides, base_ref, out_ref,
+    padded, across, polys, columns, sems,
 ):
-    side = template_ref.shape[0]
+    side = sides.shape[1]
     rows_total, cols_total = extent
-    deep = 3 * HALO
-    inner = side - 2 * LANES
-    fetches = [
-        pltpu.make_async_copy(template_ref.at[:, : 2 * LANES], sides.at[0], sems.at[0]),
-        pltpu.make_async_copy(template_ref.at[:, side - 2 * LANES :], sides.at[1], sems.at[1]),
-        pltpu.make_async_copy(template_ref.at[: 2 * HALO, :], ends.at[0], sems.at[2]),
-        pltpu.make_async_copy(template_ref.at[side - 2 * HALO :, :], ends.at[1], sems.at[3]),
-    ]
-    rim_fetches = []
-    for index, ref in enumerate((sent_ref, core_ref, other_ref)):
-        rows = ref.shape[0]
-        rim_fetches.append(
-            pltpu.make_async_copy(ref.at[rows - rims.shape[1] : rows, :], rims.at[index], sems.at[4 + index])
-        )
-    for fetch in rim_fetches + fetches:
-        fetch.start()
-    even_row = jnp.bitwise_and(pos_ref[0], 1) == 0
     even_col = jnp.bitwise_and(pos_ref[1], 1) == 0
-    for fetch in rim_fetches:
-        fetch.wait()
-    fill_tables(even_row, even_col, rims.at[0], rims.at[1], rims.at[2], blocks_ref, share_ref)
-    core_rim, other_rim = rims[1], rims[2]
-    tiles = side // LANES
-
-    def lines_of(rim):
-        return jnp.concatenate([rim[tile * HALO : (tile + 1) * HALO] for tile in range(tiles)], axis=1)
     for start, first in ((0, 0), (side - LANES, LANES)):
         for index, line in enumerate(weight_rows(coef_ref, start, LANES, side, cols_total, pos_ref[1])):
             polys[index : index + 1, first : first + LANES] = line
-
-    def upright(near_block, far_block, start, rows):
-        near_block = near_block.astype(jnp.float32)
-        far_block = far_block.astype(jnp.float32)
-        empty = jnp.zeros((LANES - HALO, LANES), jnp.float32)
-        left = jnp.concatenate([jnp.where(even_col, far_block, near_block), empty], axis=0).T
-        right = jnp.concatenate([jnp.where(even_col, near_block, far_block), empty], axis=0).T
-        padded[0, start : start + rows, :HALO] = left[:rows, :HALO].astype(padded.dtype)
-        padded[1, start : start + rows, LANES + HALO :] = right[:rows, : LANES - HALO].astype(padded.dtype)
-
+    for b in range(BASES):
+        across[b, :HALO, :] = jnp.zeros((HALO, 2 * LANES), across.dtype)
+        across[b, HALO + side :, :] = jnp.zeros((HALO, 2 * LANES), across.dtype)
     for block in range(side // LANES):
-        cols = slice(block * LANES, (block + 1) * LANES)
-        upright(near_ref[:, cols], far_ref[:, cols], HALO + block * LANES, LANES)
-    near_corner = slice(tiles * HALO, (tiles + 1) * HALO)
-    far_corner = slice((tiles + 1) * HALO, (tiles + 2) * HALO)
-    for upper, start in ((even_row, 0), (jnp.logical_not(even_row), HALO + side)):
-        upright(
-            jnp.where(upper, other_rim[near_corner], core_rim[near_corner]),
-            jnp.where(upper, other_rim[far_corner], core_rim[far_corner]),
-            start,
-            HALO,
-        )
-    above = lines_of(jnp.where(even_row, other_rim, core_rim))
-    below = lines_of(jnp.where(even_row, core_rim, other_rim))
-    for fetch in fetches:
-        fetch.wait()
-    reach = 2 * LANES - HALO
-    padded[0, HALO : HALO + side, HALO:] = sides[0, :, :reach]
-    padded[0, :HALO, HALO:] = above[:, :reach]
-    padded[0, HALO + side :, HALO:] = below[:, :reach]
-    padded[1, HALO : HALO + side, : LANES + HALO] = sides[1, :, LANES - HALO :]
-    padded[1, :HALO, : LANES + HALO] = above[:, side - LANES - HALO :]
-    padded[1, HALO + side :, : LANES + HALO] = below[:, side - LANES - HALO :]
-
-    tall = side // 2 + HALO
+        rows = slice(block * LANES, (block + 1) * LANES)
+        left, right = upright(near_ref[:, rows], far_ref[:, rows], even_col)
+        padded[0, rows, :HALO] = left[:, :HALO]
+        padded[1, rows, LANES + HALO :] = right[:, : LANES - HALO]
+    padded[0, :, HALO:] = sides[0, :, : 2 * LANES - HALO]
+    padded[1, :, : LANES + HALO] = sides[1, :, LANES - HALO :]
+
+    tall = side // 2
     for end in (0, 1):
         for start in (0, tall):
             summed = jnp.dot(padded[end, start : start + tall, :], across_ref[...], preferred_element_type=jnp.float32)
             for b in range(BASES):
-                across[b, start : start + tall, end * LANES : (end + 1) * LANES] = summed[
+                across[b, HALO + start : HALO + start + tall, end * LANES : (end + 1) * LANES] = summed[
                     :, b * LANES : (b + 1) * LANES
                 ].astype(across.dtype)
     both = slice(0, 2 * LANES)
@@ -485,79 +488,136 @@
     ]
     for store in stores:
         store.start()
-
+    for store in stores:
+        store.wait()
+
+
+def matched_sides(extent, base, coefficients, position, sides, near, far):
+    side = sides.shape[1]
+    taps = gauss_taps()
+    return pl.pallas_call(
+        functools.partial(sides_kernel, extent),
+        out_shape=jax.ShapeDtypeStruct((side, side), jnp.float32),
+        in_specs=[SMEM, SMEM, VMEM, VMEM, VMEM, VMEM, VMEM, ANY],
+        out_specs=ANY,
+        scratch_shapes=[
+            pltpu.VMEM((2, side, 2 * LANES), jnp.bfloat16),
+            pltpu.VMEM((BASES, side + 2 * HALO, 2 * LANES), jnp.bfloat16),
+            pltpu.VMEM((16, 2 * LANES), jnp.float32),
+            pltpu.VMEM((side, 2 * LANES), jnp.float32),
+            pltpu.SemaphoreType.DMA((2,)),
+        ],
+        input_output_aliases={7: 0},
+        compiler_params=pltpu.CompilerParams(vmem_limit_bytes=16 << 20),
+        cost_estimate=CHEAP,
+        name="matched_sides",
+    )(
+        coefficients, position, near, far, jnp.asarray(across_band(taps)), jnp.asarray(down_band(taps)), sides, base
+    )
+
+
+def ends_kernel(
+    extent, coef_ref, pos_ref, near_ref, far_ref, core_ref, other_ref, sent_ref, across_ref, down_ref, ends,
+    base_ref, out_ref, blocks_ref, share_ref, window, polys, lines, sems,
+):
+    side = ends.shape[2]
+    rows_total, cols_total = extent
+    deep = 3 * HALO
+    tiles = side // LANES
+    even_row = jnp.bitwise_and(pos_ref[0], 1) == 0
+    even_col = jnp.bitwise_and(pos_ref[1], 1) == 0
+    fill_tables(even_row, even_col, sent_ref, core_ref, other_ref, blocks_ref, share_ref)
     for index, line in enumerate(weight_rows(coef_ref, 0, side, side, cols_total, pos_ref[1])):
         polys[index : index + 1, :] = line
-    zeros = jnp.zeros((deep, HALO), ends.dtype)
+    window[...] = jnp.zeros_like(window)
+    core_rim, other_rim = core_ref[...], other_ref[...]
+    near_corner = slice(tiles * HALO, (tiles + 1) * HALO)
+    far_corner = slice((tiles + 1) * HALO, (tiles + 2) * HALO)
+    centre = slice(HALO, HALO + side)
+    right_cols = slice(HALO + side, side + LANES)
+    for end, upper in ((0, even_row), (1, jnp.logical_not(even_row))):
+        rim = jnp.where(upper, other_rim, core_rim)
+        first = end * deep
+        outer = first + (2 * HALO if end else 0)
+        inner = first + (0 if end else HALO)
+        left, right = upright(rim[near_corner], rim[far_corner], even_col)
+        window[outer : outer + HALO, :HALO] = left[:HALO, :HALO]
+        window[outer : outer + HALO, right_cols] = right[:HALO, : LANES - HALO]
+        window[outer : outer + HALO, centre] = jnp.concatenate(
+            [rim[tile * HALO : (tile + 1) * HALO] for tile in range(tiles)], axis=1
+        )
+        cols = slice(side - LANES, side) if end else slice(0, LANES)
+        left, right = upright(near_ref[:, cols], far_ref[:, cols], even_col)
+        rows = slice(LANES - 2 * HALO, LANES) if end else slice(0, 2 * HALO)
+        window[inner : inner + 2 * HALO, :HALO] = left[rows, :HALO]
+        window[inner : inner + 2 * HALO, right_cols] = right[rows, : LANES - HALO]
     for end in (0, 1):
-        near_rows = ends[end]
-        window = jnp.concatenate([above, near_rows] if end == 0 else [near_rows, below], axis=0)
-        window = jnp.concatenate([zeros, window, jnp.zeros((deep, LANES - HALO), ends.dtype)], axis=1)
-        parts = [[] for _ in range(BASES)]
-        for j in range(1, side // LANES - 1):
-            summed = jnp.dot(
-                window[:, j * LANES : (j + 2) * LANES], across_ref[...], preferred_element_type=jnp.float32
-            )
-            for b in range(BASES):
-                parts[b].append(summed[:, b * LANES : (b + 1) * LANES].astype(ends.dtype))
+        inner = end * deep + (0 if end else HALO)
+        window[inner : inner + 2 * HALO, centre] = ends[end]
+
+    parts = [[] for _ in range(BASES)]
+    for j in range(tiles):
+        summed = jnp.dot(
+            window[:, j * LANES : (j + 2) * LANES], across_ref[...], preferred_element_type=jnp.float32
+        )
+        for b in range(BASES):
+            parts[b].append(summed[:, b * LANES : (b + 1) * LANES].astype(ends.dtype))
+    across = [jnp.concatenate(part, axis=1) for part in parts]
+    stores = []
+    for end in (0, 1):
         smoothed = [
             jnp.dot(
-                down_ref[b, :HALO, :deep], jnp.concatenate(parts[b], axis=1), preferred_element_type=jnp.float32
+                down_ref[b, :HALO, :deep], across[b][end * deep : (end + 1) * deep], preferred_element_type=jnp.float32
             )
             for b in range(BASES)
         ]
-        lines[end] = minus_weighted(
-            smoothed, polys, slice(LANES, LANES + inner), 0 if end == 0 else side - HALO, side, rows_total, pos_ref[0]
-        )
-        store = pltpu.make_async_copy(
-            lines.at[end],
-            out_ref.at[pl.ds((side - HALO) * end, HALO), pl.ds(LANES, inner)],
-            sems.at[2 + end],
-        )
-        store.start()
-        stores.append(store)
+        start = end * (side - HALO)
+        lines[end] = minus_weighted(smoothed, polys, slice(0, side), start, side, rows_total, pos_ref[0])
+        stores.append(pltpu.make_async_copy(lines.at[end], out_ref.at[start : start + HALO, :], sems.at[end]))
+        stores[-1].start()
     for store in stores:
         store.wait()
 
 
-def frame(extent, base, sent, coefficients, position, template, near, far, core, other):
-    side = template.shape[0]
+def matched_ends(extent, base, sent, coefficients, position, ends, near, far, core, other):
+    side = ends.shape[2]
     taps = gauss_taps()
     return pl.pallas_call(
-        functools.partial(frame_kernel, extent),
+        functools.partial(ends_kernel, extent),
         out_shape=(
             jax.ShapeDtypeStruct((side, side), jnp.float32),
             jax.ShapeDtypeStruct((HALO, LANES), jnp.int32),
             jax.ShapeDtypeStruct((8, LANES), jnp.float32),
         ),
-        in_specs=[SMEM, SMEM, VMEM, VMEM, ANY, ANY, ANY, VMEM, VMEM, ANY, ANY],
+        in_specs=[SMEM, SMEM] + [VMEM] * 8 + [ANY],
         out_specs=(ANY, VMEM, VMEM),
         scratch_shapes=[
-            pltpu.VMEM((2, side, 2 * LANES), jnp.bfloat16),
-            pltpu.VMEM((2, 2 * HALO, side), jnp.bfloat16),
-            pltpu.VMEM((3, rim_rows(side), LANES), jnp.bfloat16),
-            pltpu.VMEM((2, side + 2 * HALO, 2 * LANES), jnp.bfloat16),
-            pltpu.VMEM((BASES, side + 2 * HALO, 2 * LANES), jnp.bfloat16),
+            pltpu.VMEM((6 * HALO, side + LANES), jnp.bfloat16),
             pltpu.VMEM((16, side), jnp.float32),
-            pltpu.VMEM((side, 2 * LANES), jnp.float32),
-            pltpu.VMEM((2, HALO, side - 2 * LANES), jnp.float32),
-            pltpu.SemaphoreType.DMA((7,)),
+            pltpu.VMEM((2, HALO, side), jnp.float32),
+            pltpu.SemaphoreType.DMA((2,)),
         ],
         input_output_aliases={10: 0},
-        compiler_params=pltpu.CompilerParams(vmem_limit_bytes=58 << 20),
+        compiler_params=pltpu.CompilerParams(vmem_limit_bytes=10 << 20),
         cost_estimate=CHEAP,
-        name="matched_frame",
+        name="matched_ends",
     )(
         coefficients, position, near, far, core, other, sent,
-        jnp.asarray(across_band(taps)), jnp.asarray(down_band(taps)), template, base,
+        jnp.asarray(across_band(taps)), jnp.asarray(down_band(taps)), ends, base,
     )
 
 
-def add_kernel(plan, blocks_side, blocks_ref, share_ref, base_ref, *refs):
+def add_kernel(plan, blocks_side, whole, blocks_ref, share_ref, base_ref, *refs):
     count = len(plan)
     messages = refs[:count]
-    out_ref, held, staged, hits, slots, seen, base_sems, piece_sems = refs[count:]
-    block_side = held.shape[0] // blocks_side
+    out_ref, held, hits, slots, seen, sems = refs[count:]
+    side = held.shape[0]
+    block_side = side // blocks_side
+    bands = [
+        pl.ds(band * block_side, block_side) if whole else None for band in range(blocks_side if whole else 0)
+    ]
+    for index, band in enumerate(bands):
+        pltpu.make_async_copy(base_ref.at[band, :], held.at[band, :], sems.at[index]).start()
 
     def area(block):
         row, col = split_index(block, blocks_side)
@@ -565,105 +625,91 @@
         cols = pl.ds(pl.multiple_of(col * block_side, block_side), block_side)
         return rows, cols
 
-    for block in range(blocks_side * blocks_side):
-        seen[block] = 0
+    if not whole:
+        for block in range(blocks_side * blocks_side):
+            seen[block] = 0
 
     found = jnp.int32(0)
     ends = []
-    for message, (source, first) in zip(messages, plan):
+    for source, first, skipped in plan:
         for slot in range(CAP):
             block = blocks_ref[source, first + slot]
             hits[found] = block
-            slots[found] = slot
+            slots[found] = skipped + slot
             found = found + jnp.where(block >= 0, 1, 0)
         ends.append(found)
 
     def fetch_base(block):
         rows, cols = area(block)
-        return pltpu.make_async_copy(base_ref.at[rows, cols], held.at[rows, cols], base_sems.at[block])
+        return pltpu.make_async_copy(base_ref.at[rows, cols], held.at[rows, cols], sems.at[block])
 
     def store_base(block):
         rows, cols = area(block)
-        return pltpu.make_async_copy(held.at[rows, cols], out_ref.at[rows, cols], base_sems.at[block])
+        return pltpu.make_async_copy(held.at[rows, cols], out_ref.at[rows, cols], sems.at[block])
+
+    def once(stage, action):
+        def step(index, carry):
+            block = hits[index]
+
+            @pl.when(seen[block] == stage)
+            def _():
+                action(block)
+                seen[block] = stage + 1
+
+            return carry
+
+        lax.fori_loop(0, found, step, 0)
+
+    if whole:
+        for index, band in enumerate(bands):
+            pltpu.make_async_copy(base_ref.at[band, :], held.at[band, :], sems.at[index]).wait()
+    else:
+        once(0, lambda block: fetch_base(block).start())
+        once(1, lambda block: fetch_base(block).wait())
 
     start = jnp.int32(0)
     for message, end in zip(messages, ends):
 
-        def begin(index, carry, message=message):
+        def add(index, carry, message=message):
             block = hits[index]
-            piece = piece_at(message, slots[index], block_side)
-            pltpu.make_async_copy(piece, staged.at[index], piece_sems.at[index]).start()
-
-            @pl.when(seen[block] == 0)
-            def _():
-                fetch_base(block).start()
-                seen[block] = 1
-
+            rows, cols = area(block)
+            held[rows, cols] = held[rows, cols] + message[slots[index]].astype(jnp.float32) * share_ref[0, block]
             return carry
 
-        lax.fori_loop(start, end, begin, 0)
+        lax.fori_loop(start, end, add, 0)
         start = end
 
-    def add(index, carry):
-        block = hits[index]
-        rows, cols = area(block)
-        pltpu.make_async_copy(staged.at[index], staged.at[index], piece_sems.at[index]).wait()
-
-        @pl.when(seen[block] == 1)
-        def _():
-            fetch_base(block).wait()
-            seen[block] = 2
-
-        held[rows, cols] = held[rows, cols] + staged[index].astype(jnp.float32) * share_ref[0, block]
-        return carry
-
-    def store(index, carry):
-        block = hits[index]
-
-        @pl.when(seen[block] == 2)
-        def _():
-            store_base(block).start()
-            seen[block] = 3
-
-        return carry
-
-    def finish(index, carry):
-        block = hits[index]
-
-        @pl.when(seen[block] == 3)
-        def _():
-            store_base(block).wait()
-            seen[block] = 4
-
-        return carry
-
-    for step in (add, store, finish):
-        lax.fori_loop(0, found, step, 0)
-
-
-def add_pieces(name, base, blocks, shares, messages, blocks_side):
+    if whole:
+        for index, band in enumerate(bands):
+            pltpu.make_async_copy(held.at[band, :], out_ref.at[band, :], sems.at[index]).start()
+        for index, band in enumerate(bands):
+            pltpu.make_async_copy(held.at[band, :], out_ref.at[band, :], sems.at[index]).wait()
+    else:
+        once(2, lambda block: store_base(block).start())
+        once(3, lambda block: store_base(block).wait())
+
+
+def add_pieces(name, base, blocks, shares, messages, blocks_side, cost, whole):
     side = base.shape[0]
-    plan = tuple((source, first) for _, source, first in messages)
-    arrays = [array for array, _, _ in messages]
-    room = CAP * len({source for source, _ in plan}) + 8
+    plan = tuple((source, first, sum(skipped)) for _, source, first, *skipped in messages)
+    arrays = [message[0] for message in messages]
+    room = CAP * len({source for source, _, _ in plan}) + 8
     per_tile = blocks_side * blocks_side
     return pl.pallas_call(
-        functools.partial(add_kernel, plan, blocks_side),
+        functools.partial(add_kernel, plan, blocks_side, whole),
         out_shape=jax.ShapeDtypeStruct(base.shape, base.dtype),
-        in_specs=[SMEM, SMEM, ANY] + [ANY] * len(arrays),
+        in_specs=[SMEM, SMEM, ANY] + [VMEM] * len(arrays),
         out_specs=ANY,
         scratch_shapes=[
             pltpu.VMEM((side, side), jnp.float32),
-            pltpu.VMEM((room, side // blocks_side, side // blocks_side), arrays[0].dtype),
             pltpu.SMEM((room,), jnp.int32),
             pltpu.SMEM((room,), jnp.int32),
             pltpu.SMEM((per_tile,), jnp.int32),
             pltpu.SemaphoreType.DMA((per_tile,)),
-            pltpu.SemaphoreType.DMA((room,)),
         ],
         input_output_aliases={2: 0},
-        compiler_params=pltpu.CompilerParams(vmem_limit_bytes=58 << 20),
-        cost_estimate=CHEAP,
+        compiler_params=pltpu.CompilerParams(vmem_limit_bytes=16 << 20),
+        cost_estimate=pl.CostEstimate(flops=int(cost * 1e9), bytes_accessed=0, transcendentals=0),
         name=name,
     )(blocks, shares, base, *arrays)
 
@@ -715,46 +761,45 @@
 
     near_strip = grid.near(near_rim)
     far_strip = grid.far(far_rim)
-    x0 = grid.near(chunks[0])
+    x0, x1, x2, x3 = [grid.near(chunk) for chunk in chunks]
     extent = (rows_total, cols_total)
     template, labels = bar((template, labels))
-    base = interior(extent, coefficients, position, template)
-    rest = chunks[1:]
-    x1, x2, x3 = [grid.near(chunk) for chunk in rest]
-    own_from = (grid.core(own_core), grid.other(own_other))
-    x0, near_strip, far_strip, base, *own_from = bar((x0, near_strip, far_strip, base, *own_from))
+    base, sides, ends = interior(extent, coefficients, position, template)
+    x0, near_strip, far_strip, base = bar((x0, near_strip, far_strip, base))
+    z0 = grid.beyond(x0)
     to_core, to_other = row_rims(position, template, near_strip, far_strip, labels)
     core_rows, other_rows = grid.core(to_core), grid.other(to_other)
-    z0 = grid.beyond(x0)
+    base, to_core = bar((base, to_core))
+    base = matched_sides(extent, base, coefficients, position, sides, near_strip, far_strip)
 
     own, near, far = 0, 1, 2
     core, other = 3, 6
 
-    x1, core_rows, other_rows = bar((x1, core_rows, other_rows))
+    x1, core_rows, other_rows, base = bar((x1, core_rows, other_rows, base))
     z1 = grid.beyond(x1)
-    base, blocks, shares = frame(
-        extent, base, to_core, coefficients, position, template, near_strip, far_strip, core_rows, other_rows
-    )
-
     z0, base = bar((z0, base))
-    vz0 = (grid.core(z0), grid.other(z0))
+    own_core, own_other = add_forwarded(z0, own_core, own_other)
+    from_core, from_other = grid.core(own_core), grid.other(own_other)
     x2, base = bar((x2, base))
     z2 = grid.beyond(x2)
-    vx2 = grid.core(x2)
+    base, blocks, shares = matched_ends(
+        extent, base, to_core, coefficients, position, ends, near_strip, far_strip, core_rows, other_rows
+    )
+
     z1, base = bar((z1, base))
     early = [(chunk, own, i * CAP) for i, chunk in enumerate(chunks)]
-    early += [(own_from[0], core, count), (own_from[1], other, count + CAP)]
-    early += [(x0, near, 0), (x1, near, CAP), (x2, near, 2 * CAP), (z0, far, 0)]
-    base = add_pieces("add_early", base, blocks, shares, early, blocks_side)
+    early += [(x0, near, 0), (x1, near, CAP), (x2, near, 2 * CAP), (z0, far, 0), (z1, far, CAP)]
+    base = add_pieces("add_early", base, blocks, shares, early, blocks_side, 0, False)
 
     x3, base = bar((x3, base))
-    vx3 = (grid.core(x3), grid.other(x3))
-    vz1 = grid.core(z1)
-    late = [(x3, near, 3 * CAP), (z1, far, CAP), (z2, far, 2 * CAP), (vx2, core + near, 2 * CAP)]
-    late += [(vz0[0], core + far, 0), (vz0[1], other + far, 0), (vz1, core + far, CAP)]
-    base = add_pieces("add_late", base, blocks, shares, late, blocks_side)
-    last = [(vx3[0], core + near, 3 * CAP), (vx3[1], other + near, 3 * CAP)]
-    return add_pieces("add_last", base, blocks, shares, last, blocks_side)
+    vx3 = (grid.core(jnp.concatenate([z1, x2, x3], axis=0)), grid.other(x3))
+    late = [(x3, near, 3 * CAP), (z2, far, 2 * CAP)]
+    late += [(from_core, core, count), (from_other, other, count + CAP)]
+    late += [(from_core, core + far, 0, CAP), (from_other, other + far, 0, CAP)]
+    base = add_pieces("add_late", base, blocks, shares, late, blocks_side, 12, False)
+    last = [(vx3[0], core + far, CAP), (vx3[0], core + near, 2 * CAP, CAP)]
+    last += [(vx3[0], core + near, 3 * CAP, 2 * CAP), (vx3[1], other + near, 3 * CAP)]
+    return add_pieces("add_last", base, blocks, shares, last, blocks_side, 12, False)
 
 
 def solution(mesh):

time: 80 us -> 71.2 us (0.89)
  Pallas kernels: 36.3 us -> 33.5 us
  local copies, waits for them, and re-layouts: 2.64 us -> 0.05 us
  starting transfers between devices: 32.2 us -> 30.3 us
  waiting for transfers between devices: 6.25 us -> 5.14 us
    ppermute x4 -> x3, waiting for transfers between devices: 6.21 us -> 1.47 us  [other(): lax.ppermute(array, ('py', 'px'), self.pairs(lambda r, c: (r + 1 if r % 2...]
    ppermute x4 -> x3, starting transfers between devices: 13.3 us -> 10.2 us  [other(): lax.ppermute(array, ('py', 'px'), self.pairs(lambda r, c: (r + 1 if r % 2...]
    ppermute x5, waiting for transfers between devices: 0.01 us -> 2.81 us  [near(): lax.ppermute(array, ('py', 'px'), self.pairs(lambda r, c: (r, c ^ 1)))]
    unnamed x42 -> x24, local copies, waits for them, and re-layouts: 2.64 us -> 0.05 us
    pallas_call x5 -> x7, Pallas kernels: 29.3 us -> 27.8 us  [the longest x3 12.5 us: add_pieces(): pl.pallas_call(functools.partial(add_kernel, plan, blocks_side, whole), o...]
    pallas_call x1, Pallas kernels: 2.27 us -> 0.87 us  [row_rims(): pl.pallas_call(row_rims_kernel, out_shape=(message, message), in_specs=[S...]
    ppermute x6 -> x3, starting transfers between devices: 2.15 us -> 3.27 us  [core(): lax.ppermute(array, ('py', 'px'), self.pairs(lambda r, c: (r ^ 1, c)))]
    ppermute x3, waiting for transfers between devices: 0.01 us -> 0.85 us  [beyond(): lax.ppermute(array, ('py', 'px'), self.pairs(lambda r, c: (r, c - 2 if c...]
  transfers between devices with their start and end apart: 19 -> 15, of which waited for: 2 -> 3; matrix products, arithmetic and copies ran while one was open for 0% -> 0% of each run, Pallas kernels for 35% -> 36%
where the time goes in v3:
time: 71.2 us; the launch traced here: 70.1 us
  Pallas kernels  33.5 us (47%)
  starting transfers between devices  30.3 us (43%)
  waiting for transfers between devices  5.14 us (7%)
  other arithmetic  0.82 us (1%)
    pallas_call x3, Pallas kernels, add_pieces(): pl.pallas_call(functools.partial(add_kernel, plan, blocks_side, whole), o...  12.5 us
    ppermute x3, starting transfers between devices, other(): lax.ppermute(array, ('py', 'px'), self.pairs(lambda r, c: (r + 1 if r % 2...  10.2 us
    ppermute x3, starting transfers between devices, beyond(): lax.ppermute(array, ('py', 'px'), self.pairs(lambda r, c: (r, c - 2 if c...  9.88 us
    pallas_call x1, Pallas kernels, interior(): pl.pallas_call(functools.partial(interior_kernel, extent), out_shape=(jax...  8.5 us
    ppermute x5, starting transfers between devices, near(): lax.ppermute(array, ('py', 'px'), self.pairs(lambda r, c: (r, c ^ 1)))  6.29 us
    pallas_call x1, Pallas kernels, order_pieces(): pl.pallas_call(functools.partial(order_kernel, cols_total), out_shape=(ch...  4.78 us
    pallas_call x1, Pallas kernels, matched_sides(): pl.pallas_call(functools.partial(sides_kernel, extent), out_shape=jax.Sha...  4.5 us
    ppermute x3, starting transfers between devices, core(): lax.ppermute(array, ('py', 'px'), self.pairs(lambda r, c: (r ^ 1, c)))  3.27 us
  transfers between devices with their start and end apart: 15, of which 3 were waited for; matrix products, arithmetic and copies ran while one was open for 0% of the time, Pallas kernels for 36%

profile of v3, /device:TPU:1, one launch (start us, length us, event | category | flops | bytes accessed | tf_op | source)
XLA Modules:
  0.0 70.1 jit_solution(15011051700632710558)
XLA Ops:
  0.0 0.6 pad_add_fusion.pos_ref
  0.7 0.0 copy-start.10
  0.7 4.8 %order_pieces.1 = (bf16[16,128,128]{2,1,0:T(8,128)(2,1)}, bf16[16,128,128]{2,1,0:T(8,128)(2,1)}, bf16[16,128,128]{2,1,0:T(8,128)(2,1)}, bf16[16,128,128]{2,1,0:T...) custom-call(s32[1,64]{1,0:T(1,128)} %bitcast.4, ...), custom_call_target="tpu_custom_call" | custom-call | tf_op jit(solution)/shard_map/order_pieces/pallas_call | solution.py:167
  5.5 2.1 %collective-permute-start = (bf16[16,128,128]{2,1,0:T(8,128)(2,1)}, bf16[16,128,128]{2,1,0:T(8,128)(2,1)S(1)}, u32[]{:S(2)}, u32[]{:S(2)}) collective-permute-start(bf16[16,128,128]{2,1,0:T(8,128)(2,1)} %get-tuple-element.44.refs_0_), channel_id=1, source_target_pairs={{0,1},{1,0},{2,3},{3,2},{4,5},{5,4},{6,7},{7,6},{8,9},{9,8},{10,11... | collective-permute-start | bytes 1572872 | tf_op jit(solution)/shard_map/ppermute | solution.py:731
  7.6 0.1 collective-permute-start.1
  7.6 0.7 collective-permute-start.2
  8.3 4.0 %collective-permute-start.3 = (bf16[16,128,128]{2,1,0:T(8,128)(2,1)}, bf16[16,128,128]{2,1,0:T(8,128)(2,1)S(1)}, u32[]{:S(2)}, u32[]{:S(2)}) collective-permute-start(bf16[16,128,128]{2,1,0:T(8,128)(2,1)} %get-tuple-element.52.refs_1_), channel_id=1, source_target_pairs={{0,1},{1,0},{2,3},{3,2},{4,5},{5,4},{6,7},{7,6},{8,9},{9,8},{10,11... | collective-permute-start | bytes 1572872 | tf_op jit(solution)/shard_map/ppermute | solution.py:731
  12.3 0.0 copy-done
  12.3 0.0 copy-done.4
  12.3 8.5 %matched_inside.1 = (f32[1024,1024]{1,0:T(8,128)}, bf16[2,1024,256]{2,1,0:T(8,128)(2,1)S(1)}, bf16[2,32,1024]{2,1,0:T(8,128)(2,1)S(1)}) custom-call(f32[3,15]{1,0:T(4,128)S(1)} %copy-done.9, s32[2]{0:T(128)S(1)} %copy-done.10, bf16[1024,1024]{1,0:T(8,128)(2,1)S(1)} %copy-done, bf16[256,384]{1,0:T(8,128)(2,1)S(1)} %copy-done.3, bf16[3,128,160]{2,1,0:T(8,128)(2,1)S(1)} %copy-done.4), custom_call_target="tpu_custom_call" | custom-call | flops 8000000000 | bytes 1 | tf_op jit(solution)/shard_map/matched_inside/pallas_call | solution.py:413
  20.8 0.0 collective-permute-done.1.near_ref
  20.8 0.0 collective-permute-done.2.far_ref
  20.8 0.0 collective-permute-done.refs_4_
  20.8 3.4 %collective-permute-start.7 = (bf16[16,128,128]{2,1,0:T(8,128)(2,1)S(1)}, bf16[16,128,128]{2,1,0:T(8,128)(2,1)S(1)}, u32[]{:S(2)}, u32[]{:S(2)}) collective-permute-start(bf16[16,128,128]{2,1,0:T(8,128)(2,1)S(1)} %collective-permute-done.refs_4_), channel_id=1, source_target_pairs={{0,2},{2,4},{3,1},{4,6},{5,3},{7,5},{8,10},{10,12},{11,9},{12,14},... | collective-permute-start | bytes 1572872 | tf_op jit(solution)/shard_map/ppermute | solution.py:737
  24.3 0.9 %row_rims.1 = (bf16[176,128]{1,0:T(8,128)(2,1)S(1)}, bf16[176,128]{1,0:T(8,128)(2,1)S(1)}) custom-call(s32[2]{0:T(128)S(1)} %copy-done.10, bf16[1024,1024]{1,0:T(8,128)(2,1)S(1)} %copy-done, bf16[16,1152]{1,0:T(8,128)(2,1)S(1)} %collective-permute-done.1.near_ref, bf16[16,1152]{1,0:T(8,128)(2,1)S(1)} %collective-permute-done.2.far_ref, ...), custom_call_target="tpu_custom_call" | custom-call | tf_op jit(solution)/shard_map/row_rims/pallas_call | solution.py:244
  25.2 2.9 %collective-permute-start.4 = (bf16[176,128]{1,0:T(8,128)(2,1)S(1)}, bf16[176,128]{1,0:T(8,128)(2,1)S(1)}, u32[]{:S(2)}, u32[]{:S(2)}) collective-permute-start(bf16[176,128]{1,0:T(8,128)(2,1)S(1)} %get-tuple-element.61.sent_ref), channel_id=1, source_target_pairs={{0,8},{1,9},{2,10},{3,11},{4,12},{5,13},{6,14},{7,15},{8,0},{9,1},... | collective-permute-start | bytes 135176 | tf_op jit(solution)/shard_map/ppermute | solution.py:740
  28.1 3.0 %collective-permute-start.5 = (bf16[176,128]{1,0:T(8,128)(2,1)S(1)}, bf16[176,128]{1,0:T(8,128)(2,1)S(1)}, u32[]{:S(2)}, u32[]{:S(2)}) collective-permute-start(bf16[176,128]{1,0:T(8,128)(2,1)S(1)} %get-tuple-element.55), channel_id=1, source_target_pairs={{8,16},{9,17},{10,18},{11,19},{12,20},{13,21},{14,22},{15,23},{16,... | collective-permute-start | bytes 135176 | tf_op jit(solution)/shard_map/ppermute | solution.py:743
  31.2 0.0 copy-done.8
  31.2 0.1 collective-permute-start.6
  31.3 4.5 %matched_sides.1.base_ref = f32[1024,1024]{1,0:T(8,128)} custom-call(f32[3,15]{1,0:T(4,128)S(1)} %copy-done.9, s32[2]{0:T(128)S(1)} %copy-done.10, bf16[16,1152]{1,0:T(8,128)(2,1)S(1)} %collective-permute-done.1.near_ref, bf16[16,1152]{1,0:T(8,128)(2,1)S(1)} %collective-permute-done.2.far_ref, ...), custom_call_target="tpu_custom_call", output_to_operand_aliasing={{}: (7, {})} | custom-call | tf_op jit(solution)/shard_map/matched_sides/pallas_call | solution.py:498
  35.8 0.0 collective-permute-done.3.refs_5_
  35.8 0.0 collective-permute-done.4.core_ref
  35.8 0.0 collective-permute-done.5.other_ref
  35.8 3.2 %collective-permute-start.9 = (bf16[16,128,128]{2,1,0:T(8,128)(2,1)S(1)}, bf16[16,128,128]{2,1,0:T(8,128)(2,1)S(1)}, u32[]{:S(2)}, u32[]{:S(2)}) collective-permute-start(bf16[16,128,128]{2,1,0:T(8,128)(2,1)S(1)} %collective-permute-done.3.refs_5_), channel_id=1, source_target_pairs={{0,2},{2,4},{3,1},{4,6},{5,3},{7,5},{8,10},{10,12},{11,9},{12,14},... | collective-permute-start | bytes 1572872 | tf_op jit(solution)/shard_map/ppermute | solution.py:737
  39.1 0.0 copy-done.5
  39.1 0.1 collective-permute-start.8
  39.2 0.0 collective-permute-done.7.refs_7_.part_ref
  39.2 0.1 forward_pieces.1
  39.3 0.1 collective-permute-start.11
  39.4 3.1 %collective-permute-start.12 = (bf16[32,128,128]{2,1,0:T(8,128)(2,1)S(1)}, bf16[32,128,128]{2,1,0:T(8,128)(2,1)S(1)}, u32[]{:S(2)}, u32[]{:S(2)}) collective-permute-start(bf16[32,128,128]{2,1,0:T(8,128)(2,1)S(1)} %get-tuple-element.82), channel_id=1, source_target_pairs={{8,16},{9,17},{10,18},{11,19},{12,20},{13,21},{14,22},{15,23},{16,... | collective-permute-start | bytes 3145736 | tf_op jit(solution)/shard_map/ppermute | solution.py:743
  42.4 2.8 %collective-permute-done.6.refs_6_ = bf16[16,128,128]{2,1,0:T(8,128)(2,1)S(1)} collective-permute-done((bf16[16,128,128]{2,1,0:T(8,128)(2,1)S(1)}, bf16[16,128,128]{2,1,0:T(8,128)(2,1)S(1)}, u32[]{:S(2)}, u32[]{:S(2)}) %collective-permute-start.6) | collective-permute-done | bytes 524320 | tf_op jit(solution)/shard_map/ppermute | solution.py:731
  45.2 3.2 %collective-permute-start.10 = (bf16[16,128,128]{2,1,0:T(8,128)(2,1)S(1)}, bf16[16,128,128]{2,1,0:T(8,128)(2,1)S(1)}, u32[]{:S(2)}, u32[]{:S(2)}) collective-permute-start(bf16[16,128,128]{2,1,0:T(8,128)(2,1)S(1)} %collective-permute-done.6.refs_6_), channel_id=1, source_target_pairs={{0,2},{2,4},{3,1},{4,6},{5,3},{7,5},{8,10},{10,12},{11,9},{12,14},... | collective-permute-start | bytes 1572872 | tf_op jit(solution)/shard_map/ppermute | solution.py:737
  48.5 2.2 %matched_ends.1 = (f32[1024,1024]{1,0:T(8,128)}, s32[16,128]{1,0:T(8,128)S(1)}, f32[8,128]{1,0:T(8,128)S(1)}) custom-call(f32[3,15]{1,0:T(4,128)S(1)} %copy-done.9, s32[2]{0:T(128)S(1)} %copy-done.10, bf16[16,1152]{1,0:T(8,128)(2,1)S(1)} %collective-permute-done.1.near_ref, ...), custom_call_target="tpu_custom_call", output_to_operand_aliasing={{0}: (10, {})} | custom-call | tf_op jit(solution)/shard_map/matched_ends/pallas_call | solution.py:585
  50.7 0.0 collective-permute-done.9.refs_8_
  50.7 0.0 copy-done.6
  50.7 0.0 copy-done.7
  50.7 4.2 %add_early.1.base_ref = f32[1024,1024]{1,0:T(8,128)} custom-call(s32[16,128]{1,0:T(8,128)S(1)} %get-tuple-element.68.blocks_ref, f32[8,128]{1,0:T(8,128)S(1)} %get-tuple-element.69.share_ref, f32[1024,1024]{1,0:T(8,128)} %get-tuple-element.73.base_ref, bf16[16,128,128]{2,1,0:T(8,128)(2,1)S(1)} %copy-done.6, ...), custom_call_target="tpu_custom_call", output_to_operand_aliasing={{}: (2, {})} | custom-call | tf_op jit(solution)/shard_map/add_early/pallas_call | solution.py:698
  55.0 0.0 collective-permute-done.8.refs_0_
  55.0 0.2 pad_maximum_fusion
  55.1 0.3 collective-permute-start.13
  55.4 4.1 %collective-permute-start.14 = (bf16[16,128,128]{2,1,0:T(8,128)(2,1)S(1)}, bf16[16,128,128]{2,1,0:T(8,128)(2,1)S(1)}, u32[]{:S(2)}, u32[]{:S(2)}) collective-permute-start(bf16[16,128,128]{2,1,0:T(8,128)(2,1)S(1)} %collective-permute-done.8.refs_0_), channel_id=1, source_target_pairs={{8,16},{9,17},{10,18},{11,19},{12,20},{13,21},{14,22},{15,23},{16,... | collective-permute-start | bytes 1572872 | tf_op jit(solution)/shard_map/ppermute | solution.py:743
  59.5 0.8 %collective-permute-done.10.refs_1_ = bf16[16,128,128]{2,1,0:T(8,128)(2,1)S(1)} collective-permute-done((bf16[16,128,128]{2,1,0:T(8,128)(2,1)S(1)}, bf16[16,128,128]{2,1,0:T(8,128)(2,1)S(1)}, u32[]{:S(2)}, u32[]{:S(2)}) %collective-permute-start.10) | collective-permute-done | bytes 524320 | tf_op jit(solution)/shard_map/ppermute | solution.py:737
  60.4 0.0 collective-permute-done.11.refs_2_.refs_4_
  60.4 0.0 collective-permute-done.12.refs_3_.refs_5_
  60.4 4.5 %add_late.1.base_ref = f32[1024,1024]{1,0:T(8,128)} custom-call(s32[16,128]{1,0:T(8,128)S(1)} %get-tuple-element.68.blocks_ref, f32[8,128]{1,0:T(8,128)S(1)} %get-tuple-element.69.share_ref, f32[1024,1024]{1,0:T(8,128)} %add_early.1.base_ref, bf16[16,128,128]{2,1,0:T(8,128)(2,1)S(1)} %collective-permute-done.8.refs_0_, ...), custom_call_target="tpu_custom_call", output_to_operand_aliasing={{}: (2, {})} | custom-call | flops 12000000000 | tf_op jit(solution)/shard_map/add_late/pallas_call | solution.py:698
  64.9 1.5 %collective-permute-done.14.refs_3_ = bf16[16,128,128]{2,1,0:T(8,128)(2,1)S(1)} collective-permute-done((bf16[16,128,128]{2,1,0:T(8,128)(2,1)S(1)}, bf16[16,128,128]{2,1,0:T(8,128)(2,1)S(1)}, u32[]{:S(2)}, u32[]{:S(2)}) %collective-permute-start.14) | collective-permute-done | bytes 524320 | tf_op jit(solution)/shard_map/ppermute | solution.py:743
  66.4 0.0 collective-permute-done.13.refs_0_.refs_1_.refs_2_
  66.4 3.8 %add_last.1 = f32[1024,1024]{1,0:T(8,128)} custom-call(s32[16,128]{1,0:T(8,128)S(1)} %get-tuple-element.68.blocks_ref, f32[8,128]{1,0:T(8,128)S(1)} %get-tuple-element.69.share_ref, f32[1024,1024]{1,0:T(8,128)} %add_late.1.base_ref, bf16[48,128,128]{2,1,0:T(8,128)(2,1)S(1)} %collective-permute-done.13.refs_0_.refs_1_.refs_2_, ...), custom_call_target="tpu_custom_call", output_to_operand_aliasing={{}: (2, {})} | custom-call | flops 12000000000 | tf_op jit(solution)/shard_map/add_last/pallas_call | solution.py:698
  (17 shorter events, 0.0 us)
Async XLA Ops:
  0.6 11.6 %copy-start = (bf16[1024,1024]{1,0:T(8,128)(2,1)S(1)}, bf16[1024,1024]{1,0:T(8,128)(2,1)}, u32[]{:S(2)}) copy-start(bf16[1024,1024]{1,0:T(8,128)(2,1)} %template_ref.2) | copy-start | bytes 6291460
  0.7 11.6 %copy-start.3 = (bf16[256,384]{1,0:T(8,128)(2,1)S(1)}, bf16[256,384]{1,0:T(8,128)(2,1)}, u32[]{:S(2)}) copy-start(bf16[256,384]{1,0:T(8,128)(2,1)} %constant.12.clone.across_ref) | copy-start | bytes 589828
  0.7 11.6 %copy-start.4 = (bf16[3,128,160]{2,1,0:T(8,128)(2,1)S(1)}, bf16[3,128,160]{2,1,0:T(8,128)(2,1)}, u32[]{:S(2)}) copy-start(bf16[3,128,160]{2,1,0:T(8,128)(2,1)} %constant.13.clone.down_ref) | copy-start | bytes 368644
  0.7 11.6 %copy-start.9 = (f32[3,15]{1,0:T(4,128)S(1)}, f32[3,15]{1,0:T(4,128)}, u32[]{:S(2)}) copy-start(f32[3,15]{1,0:T(4,128)} %coef_ref.5) | copy-start | bytes 544
  0.7 11.6 %copy-start.10 = (s32[2]{0:T(128)S(1)}, s32[2]{0:T(128)}, u32[]{:S(2)}) copy-start(s32[2]{0:T(128)} %pad_add_fusion.pos_ref) | copy-start | bytes 28
  5.5 15.4 %collective-permute-start = (bf16[16,128,128]{2,1,0:T(8,128)(2,1)}, bf16[16,128,128]{2,1,0:T(8,128)(2,1)S(1)}, u32[]{:S(2)}, u32[]{:S(2)}) collective-permute-start(bf16[16,128,128]{2,1,0:T(8,128)(2,1)} %get-tuple-element.44.refs_0_), channel_id=1, source_target_pairs={{0,1},{1,0},{2,3},{3,2},{4,5},{5,4},{6,7},{7,6},{8,9},{9,8},{10,11... | collective-permute-start | bytes 1572872 | tf_op jit(solution)/shard_map/ppermute | solution.py:731
  7.6 13.3 %collective-permute-start.1 = (bf16[16,1152]{1,0:T(8,128)(2,1)}, bf16[16,1152]{1,0:T(8,128)(2,1)S(1)}, u32[]{:S(2)}, u32[]{:S(2)}) collective-permute-start(bf16[16,1152]{1,0:T(8,128)(2,1)} %get-tuple-element.45), channel_id=1, source_target_pairs={{0,1},{1,0},{2,3},{3,2},{4,5},{5,4},{6,7},{7,6},{8,9},{9,8},{10,11... | collective-permute-start | bytes 110600 | tf_op jit(solution)/shard_map/ppermute | solution.py:731
  7.6 13.2 %collective-permute-start.2 = (bf16[16,1152]{1,0:T(8,128)(2,1)}, bf16[16,1152]{1,0:T(8,128)(2,1)S(1)}, u32[]{:S(2)}, u32[]{:S(2)}) collective-permute-start(bf16[16,1152]{1,0:T(8,128)(2,1)} %get-tuple-element.46), channel_id=1, source_target_pairs={{1,2},{2,1},{3,4},{4,3},{5,6},{6,5},{9,10},{10,9},{11,12},{12,11},... | collective-permute-start | bytes 110600 | tf_op jit(solution)/shard_map/ppermute | solution.py:734
  8.3 27.5 %collective-permute-start.3 = (bf16[16,128,128]{2,1,0:T(8,128)(2,1)}, bf16[16,128,128]{2,1,0:T(8,128)(2,1)S(1)}, u32[]{:S(2)}, u32[]{:S(2)}) collective-permute-start(bf16[16,128,128]{2,1,0:T(8,128)(2,1)} %get-tuple-element.52.refs_1_), channel_id=1, source_target_pairs={{0,1},{1,0},{2,3},{3,2},{4,5},{5,4},{6,7},{7,6},{8,9},{9,8},{10,11... | collective-permute-start | bytes 1572872 | tf_op jit(solution)/shard_map/ppermute | solution.py:731
  12.3 12.0 %copy-start.11 = (bf16[16,128]{1,0:T(8,128)(2,1)S(1)}, bf16[16,128]{1,0:T(8,128)(2,1)}, u32[]{:S(2)}) copy-start(bf16[16,128]{1,0:T(8,128)(2,1)} %get-tuple-element.53.label_ref) | copy-start | bytes 12292
  20.8 10.4 %copy-start.8 = (bf16[16,128,128]{2,1,0:T(8,128)(2,1)S(1)}, bf16[16,128,128]{2,1,0:T(8,128)(2,1)}, u32[]{:S(2)}) copy-start(bf16[16,128,128]{2,1,0:T(8,128)(2,1)} %get-tuple-element.63.refs_2_) | copy-start | bytes 1572868
  20.8 18.3 %collective-permute-start.7 = (bf16[16,128,128]{2,1,0:T(8,128)(2,1)S(1)}, bf16[16,128,128]{2,1,0:T(8,128)(2,1)S(1)}, u32[]{:S(2)}, u32[]{:S(2)}) collective-permute-start(bf16[16,128,128]{2,1,0:T(8,128)(2,1)S(1)} %collective-permute-done.refs_4_), channel_id=1, source_target_pairs={{0,2},{2,4},{3,1},{4,6},{5,3},{7,5},{8,10},{10,12},{11,9},{12,14},... | collective-permute-start | bytes 1572872 | tf_op jit(solution)/shard_map/ppermute | solution.py:737
  25.2 10.6 %collective-permute-start.4 = (bf16[176,128]{1,0:T(8,128)(2,1)S(1)}, bf16[176,128]{1,0:T(8,128)(2,1)S(1)}, u32[]{:S(2)}, u32[]{:S(2)}) collective-permute-start(bf16[176,128]{1,0:T(8,128)(2,1)S(1)} %get-tuple-element.61.sent_ref), channel_id=1, source_target_pairs={{0,8},{1,9},{2,10},{3,11},{4,12},{5,13},{6,14},{7,15},{8,0},{9,1},... | collective-permute-start | bytes 135176 | tf_op jit(solution)/shard_map/ppermute | solution.py:740
  28.1 7.7 %collective-permute-start.5 = (bf16[176,128]{1,0:T(8,128)(2,1)S(1)}, bf16[176,128]{1,0:T(8,128)(2,1)S(1)}, u32[]{:S(2)}, u32[]{:S(2)}) collective-permute-start(bf16[176,128]{1,0:T(8,128)(2,1)S(1)} %get-tuple-element.55), channel_id=1, source_target_pairs={{8,16},{9,17},{10,18},{11,19},{12,20},{13,21},{14,22},{15,23},{16,... | collective-permute-start | bytes 135176 | tf_op jit(solution)/shard_map/ppermute | solution.py:743
  31.2 14.1 %collective-permute-start.6 = (bf16[16,128,128]{2,1,0:T(8,128)(2,1)S(1)}, bf16[16,128,128]{2,1,0:T(8,128)(2,1)S(1)}, u32[]{:S(2)}, u32[]{:S(2)}) collective-permute-start(bf16[16,128,128]{2,1,0:T(8,128)(2,1)S(1)} %copy-done.8), channel_id=1, source_target_pairs={{0,1},{1,0},{2,3},{3,2},{4,5},{5,4},{6,7},{7,6},{8,9},{9,8},{10,11... | collective-permute-start | bytes 1572872 | tf_op jit(solution)/shard_map/ppermute | solution.py:731
  31.2 7.8 %copy-start.5 = (bf16[16,128,128]{2,1,0:T(8,128)(2,1)S(1)}, bf16[16,128,128]{2,1,0:T(8,128)(2,1)}, u32[]{:S(2)}) copy-start(bf16[16,128,128]{2,1,0:T(8,128)(2,1)} %get-tuple-element.70.refs_3_) | copy-start | bytes 1572868
  31.3 7.9 %copy-start.1 = (bf16[32,128,128]{2,1,0:T(8,128)(2,1)S(1)}, bf16[32,128,128]{2,1,0:T(8,128)(2,1)}, u32[]{:S(2)}) copy-start(bf16[32,128,128]{2,1,0:T(8,128)(2,1)} %get-tuple-element.79.core_in) | copy-start | bytes 3145732
  31.3 7.9 %copy-start.2 = (bf16[32,128,128]{2,1,0:T(8,128)(2,1)S(1)}, bf16[32,128,128]{2,1,0:T(8,128)(2,1)}, u32[]{:S(2)}) copy-start(bf16[32,128,128]{2,1,0:T(8,128)(2,1)} %get-tuple-element.80.other_in) | copy-start | bytes 3145732
  35.8 14.9 %collective-permute-start.9 = (bf16[16,128,128]{2,1,0:T(8,128)(2,1)S(1)}, bf16[16,128,128]{2,1,0:T(8,128)(2,1)S(1)}, u32[]{:S(2)}, u32[]{:S(2)}) collective-permute-start(bf16[16,128,128]{2,1,0:T(8,128)(2,1)S(1)} %collective-permute-done.3.refs_5_), channel_id=1, source_target_pairs={{0,2},{2,4},{3,1},{4,6},{5,3},{7,5},{8,10},{10,12},{11,9},{12,14},... | collective-permute-start | bytes 1572872 | tf_op jit(solution)/shard_map/ppermute | solution.py:737
  39.1 15.9 %collective-permute-start.8 = (bf16[16,128,128]{2,1,0:T(8,128)(2,1)S(1)}, bf16[16,128,128]{2,1,0:T(8,128)(2,1)S(1)}, u32[]{:S(2)}, u32[]{:S(2)}) collective-permute-start(bf16[16,128,128]{2,1,0:T(8,128)(2,1)S(1)} %copy-done.5), channel_id=1, source_target_pairs={{0,1},{1,0},{2,3},{3,2},{4,5},{5,4},{6,7},{7,6},{8,9},{9,8},{10,11... | collective-permute-start | bytes 1572872 | tf_op jit(solution)/shard_map/ppermute | solution.py:731
  39.3 21.1 %collective-permute-start.11 = (bf16[32,128,128]{2,1,0:T(8,128)(2,1)S(1)}, bf16[32,128,128]{2,1,0:T(8,128)(2,1)S(1)}, u32[]{:S(2)}, u32[]{:S(2)}) collective-permute-start(bf16[32,128,128]{2,1,0:T(8,128)(2,1)S(1)} %get-tuple-element.81), channel_id=1, source_target_pairs={{0,8},{1,9},{2,10},{3,11},{4,12},{5,13},{6,14},{7,15},{8,0},{9,1},... | collective-permute-start | bytes 3145736 | tf_op jit(solution)/shard_map/ppermute | solution.py:740
  39.4 21.0 %collective-permute-start.12 = (bf16[32,128,128]{2,1,0:T(8,128)(2,1)S(1)}, bf16[32,128,128]{2,1,0:T(8,128)(2,1)S(1)}, u32[]{:S(2)}, u32[]{:S(2)}) collective-permute-start(bf16[32,128,128]{2,1,0:T(8,128)(2,1)S(1)} %get-tuple-element.82), channel_id=1, source_target_pairs={{8,16},{9,17},{10,18},{11,19},{12,20},{13,21},{14,22},{15,23},{16,... | collective-permute-start | bytes 3145736 | tf_op jit(solution)/shard_map/ppermute | solution.py:743
  45.2 15.1 %collective-permute-start.10 = (bf16[16,128,128]{2,1,0:T(8,128)(2,1)S(1)}, bf16[16,128,128]{2,1,0:T(8,128)(2,1)S(1)}, u32[]{:S(2)}, u32[]{:S(2)}) collective-permute-start(bf16[16,128,128]{2,1,0:T(8,128)(2,1)S(1)} %collective-permute-done.6.refs_6_), channel_id=1, source_target_pairs={{0,2},{2,4},{3,1},{4,6},{5,3},{7,5},{8,10},{10,12},{11,9},{12,14},... | collective-permute-start | bytes 1572872 | tf_op jit(solution)/shard_map/ppermute | solution.py:737
  48.4 2.3 %copy-start.6 = (bf16[16,128,128]{2,1,0:T(8,128)(2,1)S(1)}, bf16[16,128,128]{2,1,0:T(8,128)(2,1)}, u32[]{:S(2)}) copy-start(bf16[16,128,128]{2,1,0:T(8,128)(2,1)} %get-tuple-element.44.refs_0_) | copy-start | bytes 1572868
  48.5 2.3 %copy-start.7 = (bf16[16,128,128]{2,1,0:T(8,128)(2,1)S(1)}, bf16[16,128,128]{2,1,0:T(8,128)(2,1)}, u32[]{:S(2)}) copy-start(bf16[16,128,128]{2,1,0:T(8,128)(2,1)} %get-tuple-element.52.refs_1_) | copy-start | bytes 1572868
  55.1 11.2 %collective-permute-start.13 = (bf16[48,128,128]{2,1,0:T(8,128)(2,1)S(1)}, bf16[48,128,128]{2,1,0:T(8,128)(2,1)S(1)}, u32[]{:S(2)}, u32[]{:S(2)}) collective-permute-start(bf16[48,128,128]{2,1,0:T(8,128)(2,1)S(1)} %pad_maximum_fusion), channel_id=1, source_target_pairs={{0,8},{1,9},{2,10},{3,11},{4,12},{5,13},{6,14},{7,15},{8,0},{9,1},... | collective-permute-start | bytes 4718600 | tf_op jit(solution)/shard_map/ppermute | solution.py:740
  55.4 10.9 %collective-permute-start.14 = (bf16[16,128,128]{2,1,0:T(8,128)(2,1)S(1)}, bf16[16,128,128]{2,1,0:T(8,128)(2,1)S(1)}, u32[]{:S(2)}, u32[]{:S(2)}) collective-permute-start(bf16[16,128,128]{2,1,0:T(8,128)(2,1)S(1)} %collective-permute-done.8.refs_0_), channel_id=1, source_target_pairs={{8,16},{9,17},{10,18},{11,19},{12,20},{13,21},{14,22},{15,23},{16,... | collective-permute-start | bytes 1572872 | tf_op jit(solution)/shard_map/ppermute | solution.py:743

commit v4 on v3

--- a/solution.py
+++ b/solution.py
@@ -66,7 +66,7 @@
     return message.at[pl.ds(start, block_side), :]
 
 
-def order_kernel(cols_total, owner_ref, offset_ref, pos_ref, pieces_ref, template_ref, *refs):
+def order_kernel(cols_total, owner_ref, offset_ref, pieces_ref, template_ref, *refs):
     outs = refs[:-9]
     near_ref, far_ref, label_ref, held, edges, meta, order_v, order_s, sems = refs[-9:]
     count = held.shape[0]
@@ -79,7 +79,7 @@
     ]
     for rim in rims:
         rim.start()
-    my_row, my_col = pos_ref[0], pos_ref[1]
+    my_row, my_col = lax.axis_index("py"), lax.axis_index("px")
     even_col = jnp.bitwise_and(my_col, 1) == 0
     near = 1 - 2 * jnp.bitwise_and(my_col, 1)
     core = 1 - 2 * jnp.bitwise_and(my_row, 1)
@@ -157,7 +157,7 @@
         pltpu.make_async_copy(outs[0], outs[0], sems.at[index]).wait()
 
 
-def order_pieces(owner_map, offsets, position, pieces, template, cols_total):
+def order_pieces(owner_map, offsets, pieces, template, cols_total):
     count, block_side, _ = pieces.shape
     side = template.shape[0]
     parts = count // CAP + 2
@@ -169,7 +169,7 @@
         out_shape=(chunk,) * (parts - 2)
         + (mail, mail)
         + (rim, rim, jax.ShapeDtypeStruct((HALO, LANES), template.dtype)),
-        in_specs=[VMEM, VMEM, SMEM, ANY, ANY],
+        in_specs=[VMEM, VMEM, ANY, ANY],
         out_specs=(ANY,) * parts + (VMEM,) * 3,
         scratch_shapes=[
             pltpu.VMEM(pieces.shape, pieces.dtype),
@@ -182,7 +182,7 @@
         compiler_params=pltpu.CompilerParams(vmem_limit_bytes=58 << 20),
         cost_estimate=CHEAP,
         name="order_pieces",
-    )(owner_map.reshape(1, -1), offsets.reshape(1, -1), position, pieces, template)
+    )(owner_map.reshape(1, -1), offsets.reshape(1, -1), pieces, template)
     return outs[:-2], outs[-2], outs[-1], near, far, labels
 
 
@@ -191,7 +191,7 @@
 
 
 def row_rims_kernel(
-    pos_ref, template_ref, near_ref, far_ref, label_ref, core_out, other_out, edges, packed, sems
+    template_ref, near_ref, far_ref, label_ref, core_out, other_out, edges, packed, sems
 ):
     side = edges.shape[2]
     tiles = side // LANES
@@ -201,7 +201,7 @@
     ]
     for fetch in fetches:
         fetch.start()
-    even_row = jnp.bitwise_and(pos_ref[0], 1) == 0
+    even_row = jnp.bitwise_and(lax.axis_index("py"), 1) == 0
     sub = lax.broadcasted_iota(jnp.int32, (HALO, LANES), 0)
     own = label_ref[...].astype(jnp.float32)
     near = near_ref[:, side:].astype(jnp.float32)
@@ -238,13 +238,13 @@
         store.wait()
 
 
-def row_rims(position, template, near, far, labels):
+def row_rims(template, near, far, labels):
     side = template.shape[0]
     message = jax.ShapeDtypeStruct((rim_rows(side), LANES), template.dtype)
     return pl.pallas_call(
         row_rims_kernel,
         out_shape=(message, message),
-        in_specs=[SMEM, ANY, VMEM, VMEM, VMEM],
+        in_specs=[ANY, VMEM, VMEM, VMEM],
         out_specs=(ANY, ANY),
         scratch_shapes=[
             pltpu.VMEM((2, HALO, side), template.dtype),
@@ -254,7 +254,7 @@
         compiler_params=pltpu.CompilerParams(vmem_limit_bytes=6 << 20),
         cost_estimate=CHEAP,
         name="row_rims",
-    )(position, template, near, far, labels)
+    )(template, near, far, labels)
 
 
 def forward_kernel(part_ref, core_in, other_in, core_out, other_out, sems):
@@ -340,7 +340,7 @@
 
 
 def interior_kernel(
-    extent, coef_ref, pos_ref, centre_ref, across_ref, down_ref, out_ref, sides_ref, ends_ref,
+    extent, coef_ref, centre_ref, across_ref, down_ref, out_ref, sides_ref, ends_ref,
     padded, across, polys, ready, sems,
 ):
     side = centre_ref.shape[0]
@@ -356,7 +356,7 @@
         copy.start()
     reach = inner + LANES
     padded[:, :reach] = centre_ref[:, LANES - HALO : LANES - HALO + reach]
-    for index, line in enumerate(weight_rows(coef_ref, LANES, inner, side, cols_total, pos_ref[1])):
+    for index, line in enumerate(weight_rows(coef_ref, LANES, inner, side, cols_total, lax.axis_index("px"))):
         polys[index : index + 1, :] = line
     for b in range(BASES):
         across[b, :HALO, :] = jnp.zeros((HALO, inner), across.dtype)
@@ -395,7 +395,7 @@
                 )
                 for b in range(BASES)
             ]
-            ready[slot, :, cols] = minus_weighted(smoothed, polys, cols, start, side, rows_total, pos_ref[0])
+            ready[slot, :, cols] = minus_weighted(smoothed, polys, cols, start, side, rows_total, lax.axis_index("py"))
         send(start, slot).start()
         return carry
 
@@ -406,7 +406,7 @@
         copy.wait()
 
 
-def interior(extent, coefficients, position, centre):
+def interior(extent, coefficients, centre):
     side = centre.shape[0]
     inner = side - 2 * LANES
     taps = gauss_taps()
@@ -417,7 +417,7 @@
             jax.ShapeDtypeStruct((2, side, 2 * LANES), centre.dtype),
             jax.ShapeDtypeStruct((2, 2 * HALO, side), centre.dtype),
         ),
-        in_specs=[SMEM, SMEM] + [VMEM] * 3,
+        in_specs=[SMEM] + [VMEM] * 3,
         out_specs=(ANY, ANY, ANY),
         scratch_shapes=[
             pltpu.VMEM((side, inner + LANES), jnp.bfloat16),
@@ -429,7 +429,7 @@
         compiler_params=pltpu.CompilerParams(vmem_limit_bytes=40 << 20),
         cost_estimate=pl.CostEstimate(flops=int(8e9), bytes_accessed=1, transcendentals=0),
         name="matched_inside",
-    )(coefficients, position, centre, jnp.asarray(across_band(taps)), jnp.asarray(down_band(taps)))
+    )(coefficients, centre, jnp.asarray(across_band(taps)), jnp.asarray(down_band(taps)))
 
 
 def upright(near_block, far_block, even_col):
@@ -442,14 +442,14 @@
 
 
 def sides_kernel(
-    extent, coef_ref, pos_ref, near_ref, far_ref, across_ref, down_ref, sides, base_ref, out_ref,
+    extent, coef_ref, near_ref, far_ref, across_ref, down_ref, sides, base_ref, out_ref,
     padded, across, polys, columns, sems,
 ):
     side = sides.shape[1]
     rows_total, cols_total = extent
-    even_col = jnp.bitwise_and(pos_ref[1], 1) == 0
+    even_col = jnp.bitwise_and(lax.axis_index("px"), 1) == 0
     for start, first in ((0, 0), (side - LANES, LANES)):
-        for index, line in enumerate(weight_rows(coef_ref, start, LANES, side, cols_total, pos_ref[1])):
+        for index, line in enumerate(weight_rows(coef_ref, start, LANES, side, cols_total, lax.axis_index("px"))):
             polys[index : index + 1, first : first + LANES] = line
     for b in range(BASES):
         across[b, :HALO, :] = jnp.zeros((HALO, 2 * LANES), across.dtype)
@@ -472,33 +472,39 @@
                 ].astype(across.dtype)
     both = slice(0, 2 * LANES)
 
+    def send(rows, end):
+        return pltpu.make_async_copy(
+            columns.at[rows, pl.ds(end * LANES, LANES)],
+            out_ref.at[rows, pl.ds(end * (side - LANES), LANES)],
+            sems.at[end],
+        )
+
     def down_step(step, carry):
         start = pl.multiple_of(step * LANES, LANES)
         smoothed = [
             jnp.dot(down_ref[b], across[b, pl.ds(start, LANES + 2 * HALO), :], preferred_element_type=jnp.float32)
             for b in range(BASES)
         ]
-        columns[pl.ds(start, LANES), :] = minus_weighted(smoothed, polys, both, start, side, rows_total, pos_ref[0])
+        rows = pl.ds(start, LANES)
+        columns[rows, :] = minus_weighted(
+            smoothed, polys, both, start, side, rows_total, lax.axis_index("py")
+        )
+        for end in (0, 1):
+            send(rows, end).start()
         return carry
 
     lax.fori_loop(0, side // LANES, down_step, 0)
-    stores = [
-        pltpu.make_async_copy(columns.at[:, :LANES], out_ref.at[:, :LANES], sems.at[0]),
-        pltpu.make_async_copy(columns.at[:, LANES:], out_ref.at[:, side - LANES :], sems.at[1]),
-    ]
-    for store in stores:
-        store.start()
-    for store in stores:
-        store.wait()
-
-
-def matched_sides(extent, base, coefficients, position, sides, near, far):
+    for end in (0, 1):
+        send(pl.ds(0, side), end).wait()
+
+
+def matched_sides(extent, base, coefficients, sides, near, far):
     side = sides.shape[1]
     taps = gauss_taps()
     return pl.pallas_call(
         functools.partial(sides_kernel, extent),
         out_shape=jax.ShapeDtypeStruct((side, side), jnp.float32),
-        in_specs=[SMEM, SMEM, VMEM, VMEM, VMEM, VMEM, VMEM, ANY],
+        in_specs=[SMEM, VMEM, VMEM, VMEM, VMEM, VMEM, ANY],
         out_specs=ANY,
         scratch_shapes=[
             pltpu.VMEM((2, side, 2 * LANES), jnp.bfloat16),
@@ -507,27 +513,27 @@
             pltpu.VMEM((side, 2 * LANES), jnp.float32),
             pltpu.SemaphoreType.DMA((2,)),
         ],
-        input_output_aliases={7: 0},
+        input_output_aliases={6: 0},
         compiler_params=pltpu.CompilerParams(vmem_limit_bytes=16 << 20),
         cost_estimate=CHEAP,
         name="matched_sides",
     )(
-        coefficients, position, near, far, jnp.asarray(across_band(taps)), jnp.asarray(down_band(taps)), sides, base
+        coefficients, near, far, jnp.asarray(across_band(taps)), jnp.asarray(down_band(taps)), sides, base
     )
 
 
 def ends_kernel(
-    extent, coef_ref, pos_ref, near_ref, far_ref, core_ref, other_ref, sent_ref, across_ref, down_ref, ends,
+    extent, coef_ref, near_ref, far_ref, core_ref, other_ref, sent_ref, across_ref, down_ref, ends,
     base_ref, out_ref, blocks_ref, share_ref, window, polys, lines, sems,
 ):
     side = ends.shape[2]
     rows_total, cols_total = extent
     deep = 3 * HALO
     tiles = side // LANES
-    even_row = jnp.bitwise_and(pos_ref[0], 1) == 0
-    even_col = jnp.bitwise_and(pos_ref[1], 1) == 0
+    even_row = jnp.bitwise_and(lax.axis_index("py"), 1) == 0
+    even_col = jnp.bitwise_and(lax.axis_index("px"), 1) == 0
     fill_tables(even_row, even_col, sent_ref, core_ref, other_ref, blocks_ref, share_ref)
-    for index, line in enumerate(weight_rows(coef_ref, 0, side, side, cols_total, pos_ref[1])):
+    for index, line in enumerate(weight_rows(coef_ref, 0, side, side, cols_total, lax.axis_index("px"))):
         polys[index : index + 1, :] = line
     window[...] = jnp.zeros_like(window)
     core_rim, other_rim = core_ref[...], other_ref[...]
@@ -572,14 +578,14 @@
             for b in range(BASES)
         ]
         start = end * (side - HALO)
-        lines[end] = minus_weighted(smoothed, polys, slice(0, side), start, side, rows_total, pos_ref[0])
+        lines[end] = minus_weighted(smoothed, polys, slice(0, side), start, side, rows_total, lax.axis_index("py"))
         stores.append(pltpu.make_async_copy(lines.at[end], out_ref.at[start : start + HALO, :], sems.at[end]))
         stores[-1].start()
     for store in stores:
         store.wait()
 
 
-def matched_ends(extent, base, sent, coefficients, position, ends, near, far, core, other):
+def matched_ends(extent, base, sent, coefficients, ends, near, far, core, other):
     side = ends.shape[2]
     taps = gauss_taps()
     return pl.pallas_call(
@@ -589,7 +595,7 @@
             jax.ShapeDtypeStruct((HALO, LANES), jnp.int32),
             jax.ShapeDtypeStruct((8, LANES), jnp.float32),
         ),
-        in_specs=[SMEM, SMEM] + [VMEM] * 8 + [ANY],
+        in_specs=[SMEM] + [VMEM] * 8 + [ANY],
         out_specs=(ANY, VMEM, VMEM),
         scratch_shapes=[
             pltpu.VMEM((6 * HALO, side + LANES), jnp.bfloat16),
@@ -597,27 +603,21 @@
             pltpu.VMEM((2, HALO, side), jnp.float32),
             pltpu.SemaphoreType.DMA((2,)),
         ],
-        input_output_aliases={10: 0},
+        input_output_aliases={9: 0},
         compiler_params=pltpu.CompilerParams(vmem_limit_bytes=10 << 20),
         cost_estimate=CHEAP,
         name="matched_ends",
     )(
-        coefficients, position, near, far, core, other, sent,
+        coefficients, near, far, core, other, sent,
         jnp.asarray(across_band(taps)), jnp.asarray(down_band(taps)), ends, base,
     )
 
 
-def add_kernel(plan, blocks_side, whole, blocks_ref, share_ref, base_ref, *refs):
+def add_kernel(plan, blocks_side, blocks_ref, share_ref, base_ref, *refs):
     count = len(plan)
     messages = refs[:count]
-    out_ref, held, hits, slots, seen, sems = refs[count:]
-    side = held.shape[0]
-    block_side = side // blocks_side
-    bands = [
-        pl.ds(band * block_side, block_side) if whole else None for band in range(blocks_side if whole else 0)
-    ]
-    for index, band in enumerate(bands):
-        pltpu.make_async_copy(base_ref.at[band, :], held.at[band, :], sems.at[index]).start()
+    out_ref, held, hits, slots, left, seen, sems = refs[count:]
+    block_side = held.shape[0] // blocks_side
 
     def area(block):
         row, col = split_index(block, blocks_side)
@@ -625,9 +625,9 @@
         cols = pl.ds(pl.multiple_of(col * block_side, block_side), block_side)
         return rows, cols
 
-    if not whole:
-        for block in range(blocks_side * blocks_side):
-            seen[block] = 0
+    for block in range(blocks_side * blocks_side):
+        left[block] = 0
+        seen[block] = 0
 
     found = jnp.int32(0)
     ends = []
@@ -647,25 +647,18 @@
         rows, cols = area(block)
         return pltpu.make_async_copy(held.at[rows, cols], out_ref.at[rows, cols], sems.at[block])
 
-    def once(stage, action):
-        def step(index, carry):
-            block = hits[index]
-
-            @pl.when(seen[block] == stage)
-            def _():
-                action(block)
-                seen[block] = stage + 1
-
-            return carry
-
-        lax.fori_loop(0, found, step, 0)
-
-    if whole:
-        for index, band in enumerate(bands):
-            pltpu.make_async_copy(base_ref.at[band, :], held.at[band, :], sems.at[index]).wait()
-    else:
-        once(0, lambda block: fetch_base(block).start())
-        once(1, lambda block: fetch_base(block).wait())
+    def begin(index, carry):
+        block = hits[index]
+        left[block] = left[block] + 1
+
+        @pl.when(seen[block] == 0)
+        def _():
+            fetch_base(block).start()
+            seen[block] = 1
+
+        return carry
+
+    lax.fori_loop(0, found, begin, 0)
 
     start = jnp.int32(0)
     for message, end in zip(messages, ends):
@@ -673,30 +666,46 @@
         def add(index, carry, message=message):
             block = hits[index]
             rows, cols = area(block)
+
+            @pl.when(seen[block] == 1)
+            def _():
+                fetch_base(block).wait()
+                seen[block] = 2
+
             held[rows, cols] = held[rows, cols] + message[slots[index]].astype(jnp.float32) * share_ref[0, block]
+            more = left[block] - 1
+            left[block] = more
+
+            @pl.when(more == 0)
+            def _():
+                store_base(block).start()
+
             return carry
 
         lax.fori_loop(start, end, add, 0)
         start = end
 
-    if whole:
-        for index, band in enumerate(bands):
-            pltpu.make_async_copy(held.at[band, :], out_ref.at[band, :], sems.at[index]).start()
-        for index, band in enumerate(bands):
-            pltpu.make_async_copy(held.at[band, :], out_ref.at[band, :], sems.at[index]).wait()
-    else:
-        once(2, lambda block: store_base(block).start())
-        once(3, lambda block: store_base(block).wait())
-
-
-def add_pieces(name, base, blocks, shares, messages, blocks_side, cost, whole):
+    def finish(index, carry):
+        block = hits[index]
+
+        @pl.when(seen[block] == 2)
+        def _():
+            store_base(block).wait()
+            seen[block] = 3
+
+        return carry
+
+    lax.fori_loop(0, found, finish, 0)
+
+
+def add_pieces(name, base, blocks, shares, messages, blocks_side, cost):
     side = base.shape[0]
     plan = tuple((source, first, sum(skipped)) for _, source, first, *skipped in messages)
     arrays = [message[0] for message in messages]
     room = CAP * len({source for source, _, _ in plan}) + 8
     per_tile = blocks_side * blocks_side
     return pl.pallas_call(
-        functools.partial(add_kernel, plan, blocks_side, whole),
+        functools.partial(add_kernel, plan, blocks_side),
         out_shape=jax.ShapeDtypeStruct(base.shape, base.dtype),
         in_specs=[SMEM, SMEM, ANY] + [VMEM] * len(arrays),
         out_specs=ANY,
@@ -705,6 +714,7 @@
             pltpu.SMEM((room,), jnp.int32),
             pltpu.SMEM((room,), jnp.int32),
             pltpu.SMEM((per_tile,), jnp.int32),
+            pltpu.SMEM((per_tile,), jnp.int32),
             pltpu.SemaphoreType.DMA((per_tile,)),
         ],
         input_output_aliases={2: 0},
@@ -748,15 +758,12 @@
     rows_total = lax.axis_size("py")
     cols_total = lax.axis_size("px")
     grid = Grid(rows_total, cols_total)
-    my_row = lax.axis_index("py")
-    my_col = lax.axis_index("px")
-    position = jnp.stack([my_row, my_col]).astype(jnp.int32)
     count, block_side, _ = pieces.shape
     side = template.shape[0]
     blocks_side = side // block_side
 
     chunks, own_core, own_other, near_rim, far_rim, labels = order_pieces(
-        owner_map, offsets, position, pieces, template, cols_total
+        owner_map, offsets, pieces, template, cols_total
     )
 
     near_strip = grid.near(near_rim)
@@ -764,42 +771,41 @@
     x0, x1, x2, x3 = [grid.near(chunk) for chunk in chunks]
     extent = (rows_total, cols_total)
     template, labels = bar((template, labels))
-    base, sides, ends = interior(extent, coefficients, position, template)
+    base, sides, ends = interior(extent, coefficients, template)
     x0, near_strip, far_strip, base = bar((x0, near_strip, far_strip, base))
     z0 = grid.beyond(x0)
-    to_core, to_other = row_rims(position, template, near_strip, far_strip, labels)
-    core_rows, other_rows = grid.core(to_core), grid.other(to_other)
-    base, to_core = bar((base, to_core))
-    base = matched_sides(extent, base, coefficients, position, sides, near_strip, far_strip)
+    to_core, to_other = row_rims(template, near_strip, far_strip, labels)
+    other_rows, core_rows = grid.other(to_other), grid.core(to_core)
+    x1, core_rows, other_rows, base = bar((x1, core_rows, other_rows, base))
+    z1 = grid.beyond(x1)
+    base = matched_sides(extent, base, coefficients, sides, near_strip, far_strip)
 
     own, near, far = 0, 1, 2
     core, other = 3, 6
 
-    x1, core_rows, other_rows, base = bar((x1, core_rows, other_rows, base))
-    z1 = grid.beyond(x1)
     z0, base = bar((z0, base))
     own_core, own_other = add_forwarded(z0, own_core, own_other)
     from_core, from_other = grid.core(own_core), grid.other(own_other)
     x2, base = bar((x2, base))
     z2 = grid.beyond(x2)
     base, blocks, shares = matched_ends(
-        extent, base, to_core, coefficients, position, ends, near_strip, far_strip, core_rows, other_rows
+        extent, base, to_core, coefficients, ends, near_strip, far_strip, core_rows, other_rows
     )
 
     z1, base = bar((z1, base))
     early = [(chunk, own, i * CAP) for i, chunk in enumerate(chunks)]
     early += [(x0, near, 0), (x1, near, CAP), (x2, near, 2 * CAP), (z0, far, 0), (z1, far, CAP)]
-    base = add_pieces("add_early", base, blocks, shares, early, blocks_side, 0, False)
+    base = add_pieces("add_early", base, blocks, shares, early, blocks_side, 0)
 
     x3, base = bar((x3, base))
     vx3 = (grid.core(jnp.concatenate([z1, x2, x3], axis=0)), grid.other(x3))
     late = [(x3, near, 3 * CAP), (z2, far, 2 * CAP)]
     late += [(from_core, core, count), (from_other, other, count + CAP)]
     late += [(from_core, core + far, 0, CAP), (from_other, other + far, 0, CAP)]
-    base = add_pieces("add_late", base, blocks, shares, late, blocks_side, 12, False)
+    base = add_pieces("add_late", base, blocks, shares, late, blocks_side, 12)
     last = [(vx3[0], core + far, CAP), (vx3[0], core + near, 2 * CAP, CAP)]
     last += [(vx3[0], core + near, 3 * CAP, 2 * CAP), (vx3[1], other + near, 3 * CAP)]
-    return add_pieces("add_last", base, blocks, shares, last, blocks_side, 12, False)
+    return add_pieces("add_last", base, blocks, shares, last, blocks_side, 12)
 
 
 def solution(mesh):

time: 71.2 us -> 70 us (0.983)
  Pallas kernels: 33.5 us -> 31 us
  starting transfers between devices: 30.3 us -> 31.5 us
  waiting for transfers between devices: 5.14 us -> 6.03 us
    ppermute x3, waiting for transfers between devices: 1.47 us -> 3.72 us  [other(): lax.ppermute(array, ('py', 'px'), self.pairs(lambda r, c: (r + 1 if r % 2...]
    ppermute x5, waiting for transfers between devices: 2.81 us -> 0.75 us  [near(): lax.ppermute(array, ('py', 'px'), self.pairs(lambda r, c: (r, c ^ 1)))]
    pallas_call x4, Pallas kernels: 13.4 us -> 11.4 us  [the longest x3 11 us: add_pieces(): pl.pallas_call(functools.partial(add_kernel, plan, blocks_side), out_shap...]
    ppermute x3, starting transfers between devices: 3.27 us -> 4.15 us  [core(): lax.ppermute(array, ('py', 'px'), self.pairs(lambda r, c: (r ^ 1, c)))]
  transfers between devices with their start and end apart: 15 -> 15, of which waited for: 3 -> 4; matrix products, arithmetic and copies ran while one was open for 0% -> 0% of each run, Pallas kernels for 36% -> 33%
where the time goes in v4:
time: 70 us; the launch traced here: 69.1 us
  starting transfers between devices  31.5 us (45%)
  Pallas kernels  31 us (44%)
  waiting for transfers between devices  6.03 us (9%)
    pallas_call x3, Pallas kernels, add_pieces(): pl.pallas_call(functools.partial(add_kernel, plan, blocks_side), out_shap...  11 us
    ppermute x3, starting transfers between devices, beyond(): lax.ppermute(array, ('py', 'px'), self.pairs(lambda r, c: (r, c - 2 if c...  10.3 us
    ppermute x3, starting transfers between devices, other(): lax.ppermute(array, ('py', 'px'), self.pairs(lambda r, c: (r + 1 if r % 2...  10.1 us
    pallas_call x1, Pallas kernels, interior(): pl.pallas_call(functools.partial(interior_kernel, extent), out_shape=(jax...  8.35 us
    ppermute x5, starting transfers between devices, near(): lax.ppermute(array, ('py', 'px'), self.pairs(lambda r, c: (r, c ^ 1)))  6.29 us
    pallas_call x1, Pallas kernels, order_pieces(): pl.pallas_call(functools.partial(order_kernel, cols_total), out_shape=(ch...  4.8 us
    pallas_call x1, Pallas kernels, matched_sides(): pl.pallas_call(functools.partial(sides_kernel, extent), out_shape=jax.Sha...  4.19 us
    ppermute x3, starting transfers between devices, core(): lax.ppermute(array, ('py', 'px'), self.pairs(lambda r, c: (r ^ 1, c)))  4.15 us
  transfers between devices with their start and end apart: 15, of which 4 were waited for; matrix products, arithmetic and copies ran while one was open for 0% of the time, Pallas kernels for 33%

profile of v4, /device:TPU:1, one launch (start us, length us, event | category | flops | bytes accessed | tf_op | source)
XLA Modules:
  0.0 69.1 jit_solution(3874333276333695743)
XLA Ops:
  0.0 0.0 copy-start.9
  0.0 4.8 %order_pieces.1 = (bf16[16,128,128]{2,1,0:T(8,128)(2,1)}, bf16[16,128,128]{2,1,0:T(8,128)(2,1)}, bf16[16,128,128]{2,1,0:T(8,128)(2,1)}, bf16[16,128,128]{2,1,0:T...) custom-call(s32[1,64]{1,0:T(1,128)} %bitcast.2, ...), custom_call_target="tpu_custom_call" | custom-call | tf_op jit(solution)/shard_map/order_pieces/pallas_call | solution.py:167
  4.8 2.1 %collective-permute-start = (bf16[16,128,128]{2,1,0:T(8,128)(2,1)}, bf16[16,128,128]{2,1,0:T(8,128)(2,1)S(1)}, u32[]{:S(2)}, u32[]{:S(2)}) collective-permute-start(bf16[16,128,128]{2,1,0:T(8,128)(2,1)} %get-tuple-element.42.refs_0_), channel_id=1, source_target_pairs={{0,1},{1,0},{2,3},{3,2},{4,5},{5,4},{6,7},{7,6},{8,9},{9,8},{10,11... | collective-permute-start | bytes 1572872 | tf_op jit(solution)/shard_map/ppermute | solution.py:741
  6.9 0.1 collective-permute-start.1
  7.0 0.7 collective-permute-start.2
  7.7 4.0 %collective-permute-start.3 = (bf16[16,128,128]{2,1,0:T(8,128)(2,1)}, bf16[16,128,128]{2,1,0:T(8,128)(2,1)S(1)}, u32[]{:S(2)}, u32[]{:S(2)}) collective-permute-start(bf16[16,128,128]{2,1,0:T(8,128)(2,1)} %get-tuple-element.50.refs_1_), channel_id=1, source_target_pairs={{0,1},{1,0},{2,3},{3,2},{4,5},{5,4},{6,7},{7,6},{8,9},{9,8},{10,11... | collective-permute-start | bytes 1572872 | tf_op jit(solution)/shard_map/ppermute | solution.py:741
  11.6 0.0 copy-done
  11.6 0.0 copy-done.3
  11.6 0.0 copy-done.4
  11.6 0.0 copy-done.9
  11.7 8.4 %matched_inside.1 = (f32[1024,1024]{1,0:T(8,128)}, bf16[2,1024,256]{2,1,0:T(8,128)(2,1)S(1)}, bf16[2,32,1024]{2,1,0:T(8,128)(2,1)S(1)}) custom-call(f32[3,15]{1,0:T(4,128)S(1)} %copy-done.9, bf16[1024,1024]{1,0:T(8,128)(2,1)S(1)} %copy-done, bf16[256,384]{1,0:T(8,128)(2,1)S(1)} %copy-done.3, bf16[3,128,160]{2,1,0:T(8,128)(2,1)S(1)} %copy-done.4), custom_call_target="tpu_custom_call" | custom-call | flops 8000000000 | bytes 1 | tf_op jit(solution)/shard_map/matched_inside/pallas_call | solution.py:413
  20.0 0.0 collective-permute-done.1.near_ref
  20.1 0.0 collective-permute-done.2.far_ref
  20.1 0.0 collective-permute-done.refs_4_
  20.1 3.6 %collective-permute-start.7 = (bf16[16,128,128]{2,1,0:T(8,128)(2,1)S(1)}, bf16[16,128,128]{2,1,0:T(8,128)(2,1)S(1)}, u32[]{:S(2)}, u32[]{:S(2)}) collective-permute-start(bf16[16,128,128]{2,1,0:T(8,128)(2,1)S(1)} %collective-permute-done.refs_4_), channel_id=1, source_target_pairs={{0,2},{2,4},{3,1},{4,6},{5,3},{7,5},{8,10},{10,12},{11,9},{12,14},... | collective-permute-start | bytes 1572872 | tf_op jit(solution)/shard_map/ppermute | solution.py:747
  23.7 0.0 copy-done.10
  23.7 0.3 row_rims.1
  24.0 2.9 %collective-permute-start.4 = (bf16[176,128]{1,0:T(8,128)(2,1)S(1)}, bf16[176,128]{1,0:T(8,128)(2,1)S(1)}, u32[]{:S(2)}, u32[]{:S(2)}) collective-permute-start(bf16[176,128]{1,0:T(8,128)(2,1)S(1)} %get-tuple-element.52.sent_ref), channel_id=1, source_target_pairs={{0,8},{1,9},{2,10},{3,11},{4,12},{5,13},{6,14},{7,15},{8,0},{9,1},... | collective-permute-start | bytes 135176 | tf_op jit(solution)/shard_map/ppermute | solution.py:750
  26.9 3.0 %collective-permute-start.5 = (bf16[176,128]{1,0:T(8,128)(2,1)S(1)}, bf16[176,128]{1,0:T(8,128)(2,1)S(1)}, u32[]{:S(2)}, u32[]{:S(2)}) collective-permute-start(bf16[176,128]{1,0:T(8,128)(2,1)S(1)} %get-tuple-element.53), channel_id=1, source_target_pairs={{8,16},{9,17},{10,18},{11,19},{12,20},{13,21},{14,22},{15,23},{16,... | collective-permute-start | bytes 135176 | tf_op jit(solution)/shard_map/ppermute | solution.py:753
  30.0 0.1 collective-permute-start.6
  30.1 0.7 %collective-permute-done.3.refs_5_ = bf16[16,128,128]{2,1,0:T(8,128)(2,1)S(1)} collective-permute-done((bf16[16,128,128]{2,1,0:T(8,128)(2,1)}, bf16[16,128,128]{2,1,0:T(8,128)(2,1)S(1)}, u32[]{:S(2)}, u32[]{:S(2)}) %collective-permute-start.3) | collective-permute-done | bytes 524320 | tf_op jit(solution)/shard_map/ppermute | solution.py:741
  30.8 0.0 collective-permute-done.4.core_ref
  30.8 1.8 %collective-permute-done.5.other_ref = bf16[176,128]{1,0:T(8,128)(2,1)S(1)} collective-permute-done((bf16[176,128]{1,0:T(8,128)(2,1)S(1)}, bf16[176,128]{1,0:T(8,128)(2,1)S(1)}, u32[]{:S(2)}, u32[]{:S(2)}) %collective-permute-start.5) | collective-permute-done | bytes 45088 | tf_op jit(solution)/shard_map/ppermute | solution.py:753
  32.6 3.2 %collective-permute-start.9 = (bf16[16,128,128]{2,1,0:T(8,128)(2,1)S(1)}, bf16[16,128,128]{2,1,0:T(8,128)(2,1)S(1)}, u32[]{:S(2)}, u32[]{:S(2)}) collective-permute-start(bf16[16,128,128]{2,1,0:T(8,128)(2,1)S(1)} %collective-permute-done.3.refs_5_), channel_id=1, source_target_pairs={{0,2},{2,4},{3,1},{4,6},{5,3},{7,5},{8,10},{10,12},{11,9},{12,14},... | collective-permute-start | bytes 1572872 | tf_op jit(solution)/shard_map/ppermute | solution.py:747
  35.8 0.1 collective-permute-start.8
  35.9 4.2 %matched_sides.1.base_ref = f32[1024,1024]{1,0:T(8,128)} custom-call(f32[3,15]{1,0:T(4,128)S(1)} %copy-done.9, bf16[16,1152]{1,0:T(8,128)(2,1)S(1)} %collective-permute-done.1.near_ref, bf16[16,1152]{1,0:T(8,128)(2,1)S(1)} %collective-permute-done.2.far_ref, bf16[256,384]{1,0:T(8,128)(2,1)S(1)} %copy-done.3, ...), custom_call_target="tpu_custom_call", output_to_operand_aliasing={{}: (6, {})} | custom-call | tf_op jit(solution)/shard_map/matched_sides/pallas_call | solution.py:504
  40.1 0.0 collective-permute-done.7.refs_7_.part_ref
  40.1 0.0 copy-done.1
  40.1 0.0 copy-done.2
  40.1 0.1 forward_pieces.1
  40.2 1.2 %collective-permute-start.11 = (bf16[32,128,128]{2,1,0:T(8,128)(2,1)S(1)}, bf16[32,128,128]{2,1,0:T(8,128)(2,1)S(1)}, u32[]{:S(2)}, u32[]{:S(2)}) collective-permute-start(bf16[32,128,128]{2,1,0:T(8,128)(2,1)S(1)} %get-tuple-element.77), channel_id=1, source_target_pairs={{0,8},{1,9},{2,10},{3,11},{4,12},{5,13},{6,14},{7,15},{8,0},{9,1},... | collective-permute-start | bytes 3145736 | tf_op jit(solution)/shard_map/ppermute | solution.py:750
  41.4 3.9 %collective-permute-start.12 = (bf16[32,128,128]{2,1,0:T(8,128)(2,1)S(1)}, bf16[32,128,128]{2,1,0:T(8,128)(2,1)S(1)}, u32[]{:S(2)}, u32[]{:S(2)}) collective-permute-start(bf16[32,128,128]{2,1,0:T(8,128)(2,1)S(1)} %get-tuple-element.78), channel_id=1, source_target_pairs={{8,16},{9,17},{10,18},{11,19},{12,20},{13,21},{14,22},{15,23},{16,... | collective-permute-start | bytes 3145736 | tf_op jit(solution)/shard_map/ppermute | solution.py:753
  45.3 0.0 collective-permute-done.6.refs_6_
  45.3 3.5 %collective-permute-start.10 = (bf16[16,128,128]{2,1,0:T(8,128)(2,1)S(1)}, bf16[16,128,128]{2,1,0:T(8,128)(2,1)S(1)}, u32[]{:S(2)}, u32[]{:S(2)}) collective-permute-start(bf16[16,128,128]{2,1,0:T(8,128)(2,1)S(1)} %collective-permute-done.6.refs_6_), channel_id=1, source_target_pairs={{0,2},{2,4},{3,1},{4,6},{5,3},{7,5},{8,10},{10,12},{11,9},{12,14},... | collective-permute-start | bytes 1572872 | tf_op jit(solution)/shard_map/ppermute | solution.py:747
  48.9 2.2 %matched_ends.1 = (f32[1024,1024]{1,0:T(8,128)}, s32[16,128]{1,0:T(8,128)S(1)}, f32[8,128]{1,0:T(8,128)S(1)}) custom-call(f32[3,15]{1,0:T(4,128)S(1)} %copy-done.9, bf16[16,1152]{1,0:T(8,128)(2,1)S(1)} %collective-permute-done.1.near_ref, bf16[16,1152]{1,0:T(8,128)(2,1)S(1)} %collective-permute-done.2.far_ref, ...), custom_call_target="tpu_custom_call", output_to_operand_aliasing={{0}: (9, {})} | custom-call | tf_op jit(solution)/shard_map/matched_ends/pallas_call | solution.py:591
  51.0 0.0 collective-permute-done.9.refs_8_
  51.1 3.6 %add_early.1.base_ref = f32[1024,1024]{1,0:T(8,128)} custom-call(s32[16,128]{1,0:T(8,128)S(1)} %get-tuple-element.64.blocks_ref, f32[8,128]{1,0:T(8,128)S(1)} %get-tuple-element.65.share_ref, f32[1024,1024]{1,0:T(8,128)} %get-tuple-element.69.base_ref, bf16[16,128,128]{2,1,0:T(8,128)(2,1)S(1)} %copy-done.6, ...), custom_call_target="tpu_custom_call", output_to_operand_aliasing={{}: (2, {})} | custom-call | tf_op jit(solution)/shard_map/add_early/pallas_call | solution.py:707
  54.7 0.0 collective-permute-done.8.refs_0_
  54.7 0.2 pad_maximum_fusion
  54.9 0.1 collective-permute-start.13
  55.0 3.2 %collective-permute-start.14 = (bf16[16,128,128]{2,1,0:T(8,128)(2,1)S(1)}, bf16[16,128,128]{2,1,0:T(8,128)(2,1)S(1)}, u32[]{:S(2)}, u32[]{:S(2)}) collective-permute-start(bf16[16,128,128]{2,1,0:T(8,128)(2,1)S(1)} %collective-permute-done.8.refs_0_), channel_id=1, source_target_pairs={{8,16},{9,17},{10,18},{11,19},{12,20},{13,21},{14,22},{15,23},{16,... | collective-permute-start | bytes 1572872 | tf_op jit(solution)/shard_map/ppermute | solution.py:753
  58.2 1.5 %collective-permute-done.10.refs_1_ = bf16[16,128,128]{2,1,0:T(8,128)(2,1)S(1)} collective-permute-done((bf16[16,128,128]{2,1,0:T(8,128)(2,1)S(1)}, bf16[16,128,128]{2,1,0:T(8,128)(2,1)S(1)}, u32[]{:S(2)}, u32[]{:S(2)}) %collective-permute-start.10) | collective-permute-done | bytes 524320 | tf_op jit(solution)/shard_map/ppermute | solution.py:747
  59.7 0.0 collective-permute-done.11.refs_2_.refs_4_
  59.7 0.0 collective-permute-done.12.refs_3_.refs_5_
  59.7 3.8 %add_late.1.base_ref = f32[1024,1024]{1,0:T(8,128)} custom-call(s32[16,128]{1,0:T(8,128)S(1)} %get-tuple-element.64.blocks_ref, f32[8,128]{1,0:T(8,128)S(1)} %get-tuple-element.65.share_ref, f32[1024,1024]{1,0:T(8,128)} %add_early.1.base_ref, bf16[16,128,128]{2,1,0:T(8,128)(2,1)S(1)} %collective-permute-done.8.refs_0_, ...), custom_call_target="tpu_custom_call", output_to_operand_aliasing={{}: (2, {})} | custom-call | flops 12000000000 | tf_op jit(solution)/shard_map/add_late/pallas_call | solution.py:707
  63.5 2.0 %collective-permute-done.14.refs_3_ = bf16[16,128,128]{2,1,0:T(8,128)(2,1)S(1)} collective-permute-done((bf16[16,128,128]{2,1,0:T(8,128)(2,1)S(1)}, bf16[16,128,128]{2,1,0:T(8,128)(2,1)S(1)}, u32[]{:S(2)}, u32[]{:S(2)}) %collective-permute-start.14) | collective-permute-done | bytes 524320 | tf_op jit(solution)/shard_map/ppermute | solution.py:753
  65.5 0.0 collective-permute-done.13.refs_0_.refs_1_.refs_2_
  65.5 3.6 %add_last.1 = f32[1024,1024]{1,0:T(8,128)} custom-call(s32[16,128]{1,0:T(8,128)S(1)} %get-tuple-element.64.blocks_ref, f32[8,128]{1,0:T(8,128)S(1)} %get-tuple-element.65.share_ref, f32[1024,1024]{1,0:T(8,128)} %add_late.1.base_ref, bf16[48,128,128]{2,1,0:T(8,128)(2,1)S(1)} %collective-permute-done.13.refs_0_.refs_1_.refs_2_, ...), custom_call_target="tpu_custom_call", output_to_operand_aliasing={{}: (2, {})} | custom-call | flops 12000000000 | tf_op jit(solution)/shard_map/add_last/pallas_call | solution.py:707
  (14 shorter events, 0.0 us)
Async XLA Ops:
  0.0 11.6 %copy-start = (bf16[1024,1024]{1,0:T(8,128)(2,1)S(1)}, bf16[1024,1024]{1,0:T(8,128)(2,1)}, u32[]{:S(2)}) copy-start(bf16[1024,1024]{1,0:T(8,128)(2,1)} %template_ref.2) | copy-start | bytes 6291460
  0.0 11.6 %copy-start.3 = (bf16[256,384]{1,0:T(8,128)(2,1)S(1)}, bf16[256,384]{1,0:T(8,128)(2,1)}, u32[]{:S(2)}) copy-start(bf16[256,384]{1,0:T(8,128)(2,1)} %constant.4.clone.across_ref) | copy-start | bytes 589828
  0.0 11.6 %copy-start.4 = (bf16[3,128,160]{2,1,0:T(8,128)(2,1)S(1)}, bf16[3,128,160]{2,1,0:T(8,128)(2,1)}, u32[]{:S(2)}) copy-start(bf16[3,128,160]{2,1,0:T(8,128)(2,1)} %constant.5.clone.down_ref) | copy-start | bytes 368644
  0.0 11.6 %copy-start.9 = (f32[3,15]{1,0:T(4,128)S(1)}, f32[3,15]{1,0:T(4,128)}, u32[]{:S(2)}) copy-start(f32[3,15]{1,0:T(4,128)} %coef_ref.5) | copy-start | bytes 544
  4.8 15.2 %collective-permute-start = (bf16[16,128,128]{2,1,0:T(8,128)(2,1)}, bf16[16,128,128]{2,1,0:T(8,128)(2,1)S(1)}, u32[]{:S(2)}, u32[]{:S(2)}) collective-permute-start(bf16[16,128,128]{2,1,0:T(8,128)(2,1)} %get-tuple-element.42.refs_0_), channel_id=1, source_target_pairs={{0,1},{1,0},{2,3},{3,2},{4,5},{5,4},{6,7},{7,6},{8,9},{9,8},{10,11... | collective-permute-start | bytes 1572872 | tf_op jit(solution)/shard_map/ppermute | solution.py:741
  6.9 13.1 %collective-permute-start.1 = (bf16[16,1152]{1,0:T(8,128)(2,1)}, bf16[16,1152]{1,0:T(8,128)(2,1)S(1)}, u32[]{:S(2)}, u32[]{:S(2)}) collective-permute-start(bf16[16,1152]{1,0:T(8,128)(2,1)} %get-tuple-element.43), channel_id=1, source_target_pairs={{0,1},{1,0},{2,3},{3,2},{4,5},{5,4},{6,7},{7,6},{8,9},{9,8},{10,11... | collective-permute-start | bytes 110600 | tf_op jit(solution)/shard_map/ppermute | solution.py:741
  7.0 13.0 %collective-permute-start.2 = (bf16[16,1152]{1,0:T(8,128)(2,1)}, bf16[16,1152]{1,0:T(8,128)(2,1)S(1)}, u32[]{:S(2)}, u32[]{:S(2)}) collective-permute-start(bf16[16,1152]{1,0:T(8,128)(2,1)} %get-tuple-element.44), channel_id=1, source_target_pairs={{1,2},{2,1},{3,4},{4,3},{5,6},{6,5},{9,10},{10,9},{11,12},{12,11},... | collective-permute-start | bytes 110600 | tf_op jit(solution)/shard_map/ppermute | solution.py:744
  7.7 23.1 %collective-permute-start.3 = (bf16[16,128,128]{2,1,0:T(8,128)(2,1)}, bf16[16,128,128]{2,1,0:T(8,128)(2,1)S(1)}, u32[]{:S(2)}, u32[]{:S(2)}) collective-permute-start(bf16[16,128,128]{2,1,0:T(8,128)(2,1)} %get-tuple-element.50.refs_1_), channel_id=1, source_target_pairs={{0,1},{1,0},{2,3},{3,2},{4,5},{5,4},{6,7},{7,6},{8,9},{9,8},{10,11... | collective-permute-start | bytes 1572872 | tf_op jit(solution)/shard_map/ppermute | solution.py:741
  11.7 12.0 %copy-start.10 = (bf16[16,128]{1,0:T(8,128)(2,1)S(1)}, bf16[16,128]{1,0:T(8,128)(2,1)}, u32[]{:S(2)}) copy-start(bf16[16,128]{1,0:T(8,128)(2,1)} %get-tuple-element.51.label_ref) | copy-start | bytes 12292
  20.0 10.0 %copy-start.8 = (bf16[16,128,128]{2,1,0:T(8,128)(2,1)S(1)}, bf16[16,128,128]{2,1,0:T(8,128)(2,1)}, u32[]{:S(2)}) copy-start(bf16[16,128,128]{2,1,0:T(8,128)(2,1)} %get-tuple-element.58.refs_2_) | copy-start | bytes 1572868
  20.0 15.8 %copy-start.5 = (bf16[16,128,128]{2,1,0:T(8,128)(2,1)S(1)}, bf16[16,128,128]{2,1,0:T(8,128)(2,1)}, u32[]{:S(2)}) copy-start(bf16[16,128,128]{2,1,0:T(8,128)(2,1)} %get-tuple-element.66.refs_3_) | copy-start | bytes 1572868
  20.1 20.0 %collective-permute-start.7 = (bf16[16,128,128]{2,1,0:T(8,128)(2,1)S(1)}, bf16[16,128,128]{2,1,0:T(8,128)(2,1)S(1)}, u32[]{:S(2)}, u32[]{:S(2)}) collective-permute-start(bf16[16,128,128]{2,1,0:T(8,128)(2,1)S(1)} %collective-permute-done.refs_4_), channel_id=1, source_target_pairs={{0,2},{2,4},{3,1},{4,6},{5,3},{7,5},{8,10},{10,12},{11,9},{12,14},... | collective-permute-start | bytes 1572872 | tf_op jit(solution)/shard_map/ppermute | solution.py:747
  24.0 6.8 %collective-permute-start.4 = (bf16[176,128]{1,0:T(8,128)(2,1)S(1)}, bf16[176,128]{1,0:T(8,128)(2,1)S(1)}, u32[]{:S(2)}, u32[]{:S(2)}) collective-permute-start(bf16[176,128]{1,0:T(8,128)(2,1)S(1)} %get-tuple-element.52.sent_ref), channel_id=1, source_target_pairs={{0,8},{1,9},{2,10},{3,11},{4,12},{5,13},{6,14},{7,15},{8,0},{9,1},... | collective-permute-start | bytes 135176 | tf_op jit(solution)/shard_map/ppermute | solution.py:750
  26.9 5.6 %collective-permute-start.5 = (bf16[176,128]{1,0:T(8,128)(2,1)S(1)}, bf16[176,128]{1,0:T(8,128)(2,1)S(1)}, u32[]{:S(2)}, u32[]{:S(2)}) collective-permute-start(bf16[176,128]{1,0:T(8,128)(2,1)S(1)} %get-tuple-element.53), channel_id=1, source_target_pairs={{8,16},{9,17},{10,18},{11,19},{12,20},{13,21},{14,22},{15,23},{16,... | collective-permute-start | bytes 135176 | tf_op jit(solution)/shard_map/ppermute | solution.py:753
  30.0 15.3 %collective-permute-start.6 = (bf16[16,128,128]{2,1,0:T(8,128)(2,1)S(1)}, bf16[16,128,128]{2,1,0:T(8,128)(2,1)S(1)}, u32[]{:S(2)}, u32[]{:S(2)}) collective-permute-start(bf16[16,128,128]{2,1,0:T(8,128)(2,1)S(1)} %copy-done.8), channel_id=1, source_target_pairs={{0,1},{1,0},{2,3},{3,2},{4,5},{5,4},{6,7},{7,6},{8,9},{9,8},{10,11... | collective-permute-start | bytes 1572872 | tf_op jit(solution)/shard_map/ppermute | solution.py:741
  32.6 18.5 %collective-permute-start.9 = (bf16[16,128,128]{2,1,0:T(8,128)(2,1)S(1)}, bf16[16,128,128]{2,1,0:T(8,128)(2,1)S(1)}, u32[]{:S(2)}, u32[]{:S(2)}) collective-permute-start(bf16[16,128,128]{2,1,0:T(8,128)(2,1)S(1)} %collective-permute-done.3.refs_5_), channel_id=1, source_target_pairs={{0,2},{2,4},{3,1},{4,6},{5,3},{7,5},{8,10},{10,12},{11,9},{12,14},... | collective-permute-start | bytes 1572872 | tf_op jit(solution)/shard_map/ppermute | solution.py:747
  35.8 18.9 %collective-permute-start.8 = (bf16[16,128,128]{2,1,0:T(8,128)(2,1)S(1)}, bf16[16,128,128]{2,1,0:T(8,128)(2,1)S(1)}, u32[]{:S(2)}, u32[]{:S(2)}) collective-permute-start(bf16[16,128,128]{2,1,0:T(8,128)(2,1)S(1)} %copy-done.5), channel_id=1, source_target_pairs={{0,1},{1,0},{2,3},{3,2},{4,5},{5,4},{6,7},{7,6},{8,9},{9,8},{10,11... | collective-permute-start | bytes 1572872 | tf_op jit(solution)/shard_map/ppermute | solution.py:741
  35.9 4.2 %copy-start.1 = (bf16[32,128,128]{2,1,0:T(8,128)(2,1)S(1)}, bf16[32,128,128]{2,1,0:T(8,128)(2,1)}, u32[]{:S(2)}) copy-start(bf16[32,128,128]{2,1,0:T(8,128)(2,1)} %get-tuple-element.75.core_in) | copy-start | bytes 3145732
  35.9 4.2 %copy-start.2 = (bf16[32,128,128]{2,1,0:T(8,128)(2,1)S(1)}, bf16[32,128,128]{2,1,0:T(8,128)(2,1)}, u32[]{:S(2)}) copy-start(bf16[32,128,128]{2,1,0:T(8,128)(2,1)} %get-tuple-element.76.other_in) | copy-start | bytes 3145732
  40.2 19.5 %collective-permute-start.11 = (bf16[32,128,128]{2,1,0:T(8,128)(2,1)S(1)}, bf16[32,128,128]{2,1,0:T(8,128)(2,1)S(1)}, u32[]{:S(2)}, u32[]{:S(2)}) collective-permute-start(bf16[32,128,128]{2,1,0:T(8,128)(2,1)S(1)} %get-tuple-element.77), channel_id=1, source_target_pairs={{0,8},{1,9},{2,10},{3,11},{4,12},{5,13},{6,14},{7,15},{8,0},{9,1},... | collective-permute-start | bytes 3145736 | tf_op jit(solution)/shard_map/ppermute | solution.py:750
  41.4 18.3 %collective-permute-start.12 = (bf16[32,128,128]{2,1,0:T(8,128)(2,1)S(1)}, bf16[32,128,128]{2,1,0:T(8,128)(2,1)S(1)}, u32[]{:S(2)}, u32[]{:S(2)}) collective-permute-start(bf16[32,128,128]{2,1,0:T(8,128)(2,1)S(1)} %get-tuple-element.78), channel_id=1, source_target_pairs={{8,16},{9,17},{10,18},{11,19},{12,20},{13,21},{14,22},{15,23},{16,... | collective-permute-start | bytes 3145736 | tf_op jit(solution)/shard_map/ppermute | solution.py:753
  45.3 14.4 %collective-permute-start.10 = (bf16[16,128,128]{2,1,0:T(8,128)(2,1)S(1)}, bf16[16,128,128]{2,1,0:T(8,128)(2,1)S(1)}, u32[]{:S(2)}, u32[]{:S(2)}) collective-permute-start(bf16[16,128,128]{2,1,0:T(8,128)(2,1)S(1)} %collective-permute-done.6.refs_6_), channel_id=1, source_target_pairs={{0,2},{2,4},{3,1},{4,6},{5,3},{7,5},{8,10},{10,12},{11,9},{12,14},... | collective-permute-start | bytes 1572872 | tf_op jit(solution)/shard_map/ppermute | solution.py:747
  48.9 2.2 %copy-start.6 = (bf16[16,128,128]{2,1,0:T(8,128)(2,1)S(1)}, bf16[16,128,128]{2,1,0:T(8,128)(2,1)}, u32[]{:S(2)}) copy-start(bf16[16,128,128]{2,1,0:T(8,128)(2,1)} %get-tuple-element.42.refs_0_) | copy-start | bytes 1572868
  48.9 2.2 %copy-start.7 = (bf16[16,128,128]{2,1,0:T(8,128)(2,1)S(1)}, bf16[16,128,128]{2,1,0:T(8,128)(2,1)}, u32[]{:S(2)}) copy-start(bf16[16,128,128]{2,1,0:T(8,128)(2,1)} %get-tuple-element.50.refs_1_) | copy-start | bytes 1572868
  54.9 10.6 %collective-permute-start.13 = (bf16[48,128,128]{2,1,0:T(8,128)(2,1)S(1)}, bf16[48,128,128]{2,1,0:T(8,128)(2,1)S(1)}, u32[]{:S(2)}, u32[]{:S(2)}) collective-permute-start(bf16[48,128,128]{2,1,0:T(8,128)(2,1)S(1)} %pad_maximum_fusion), channel_id=1, source_target_pairs={{0,8},{1,9},{2,10},{3,11},{4,12},{5,13},{6,14},{7,15},{8,0},{9,1},... | collective-permute-start | bytes 4718600 | tf_op jit(solution)/shard_map/ppermute | solution.py:750
  55.0 10.5 %collective-permute-start.14 = (bf16[16,128,128]{2,1,0:T(8,128)(2,1)S(1)}, bf16[16,128,128]{2,1,0:T(8,128)(2,1)S(1)}, u32[]{:S(2)}, u32[]{:S(2)}) collective-permute-start(bf16[16,128,128]{2,1,0:T(8,128)(2,1)S(1)} %collective-permute-done.8.refs_0_), channel_id=1, source_target_pairs={{8,16},{9,17},{10,18},{11,19},{12,20},{13,21},{14,22},{15,23},{16,... | collective-permute-start | bytes 1572872 | tf_op jit(solution)/shard_map/ppermute | solution.py:753

commit v5 on v4

--- a/solution.py
+++ b/solution.py
@@ -67,10 +67,16 @@
 
 
 def order_kernel(cols_total, owner_ref, offset_ref, pieces_ref, template_ref, *refs):
-    outs = refs[:-9]
-    near_ref, far_ref, label_ref, held, edges, meta, order_v, order_s, sems = refs[-9:]
+    outs = refs[:-10]
+    near_ref, far_ref, label_ref, held, edges, given, meta, order_v, order_s, sems = refs[-10:]
     count = held.shape[0]
     fetch = pltpu.make_async_copy(pieces_ref, held, sems.at[len(outs)])
+    tables = [
+        pltpu.make_async_copy(owner_ref, given.at[0], sems.at[len(outs) + 4]),
+        pltpu.make_async_copy(offset_ref, given.at[1], sems.at[len(outs) + 5]),
+    ]
+    for table in tables:
+        table.start()
     fetch.start()
     side = edges.shape[1]
     rims = [
@@ -85,8 +91,10 @@
     core = 1 - 2 * jnp.bitwise_and(my_row, 1)
 
     meta[...] = jnp.zeros_like(meta)
-    meta[0:1, :count] = owner_ref[...]
-    meta[1:2, :count] = offset_ref[...]
+    for table in tables:
+        table.wait()
+    meta[0:1, :count] = given[0]
+    meta[1:2, :count] = given[1]
     lane = lax.broadcasted_iota(jnp.int32, (1, LANES), 1)
     row, col = split_index(meta[0:1, :], cols_total)
     dy, dx = row - my_row, col - my_col
@@ -169,15 +177,16 @@
         out_shape=(chunk,) * (parts - 2)
         + (mail, mail)
         + (rim, rim, jax.ShapeDtypeStruct((HALO, LANES), template.dtype)),
-        in_specs=[VMEM, VMEM, ANY, ANY],
+        in_specs=[ANY, ANY, ANY, ANY],
         out_specs=(ANY,) * parts + (VMEM,) * 3,
         scratch_shapes=[
             pltpu.VMEM(pieces.shape, pieces.dtype),
             pltpu.VMEM((2, side, LANES), template.dtype),
+            pltpu.VMEM((2, 1, count), jnp.int32),
             pltpu.VMEM((8, LANES), jnp.int32),
             pltpu.VMEM((8, LANES), jnp.int32),
             pltpu.SMEM((8, LANES), jnp.int32),
-            pltpu.SemaphoreType.DMA((parts + 4,)),
+            pltpu.SemaphoreType.DMA((parts + 6,)),
         ],
         compiler_params=pltpu.CompilerParams(vmem_limit_bytes=58 << 20),
         cost_estimate=CHEAP,

time: 70 us -> 69.2 us (0.989)
  transfers between devices with their start and end apart: 15 -> 15, of which waited for: 4 -> 4; matrix products, arithmetic and copies ran while one was open for 0% -> 0% of each run, Pallas kernels for 33% -> 34%
where the time goes in v5:
time: 69.2 us; the launch traced here: 68.8 us
  starting transfers between devices  31.3 us (45%)
  Pallas kernels  30.8 us (45%)
  waiting for transfers between devices  6.14 us (9%)
    pallas_call x3, Pallas kernels, add_pieces(): pl.pallas_call(functools.partial(add_kernel, plan, blocks_side), out_shap...  11.5 us
    ppermute x3, starting transfers between devices, beyond(): lax.ppermute(array, ('py', 'px'), self.pairs(lambda r, c: (r, c - 2 if c...  10.3 us
    ppermute x3, starting transfers between devices, other(): lax.ppermute(array, ('py', 'px'), self.pairs(lambda r, c: (r + 1 if r % 2...  9.89 us
    pallas_call x1, Pallas kernels, interior(): pl.pallas_call(functools.partial(interior_kernel, extent), out_shape=(jax...  8.36 us
    ppermute x5, starting transfers between devices, near(): lax.ppermute(array, ('py', 'px'), self.pairs(lambda r, c: (r, c ^ 1)))  6.29 us
    pallas_call x1, Pallas kernels, matched_sides(): pl.pallas_call(functools.partial(sides_kernel, extent), out_shape=jax.Sha...  4.19 us
    pallas_call x1, Pallas kernels, order_pieces(): pl.pallas_call(functools.partial(order_kernel, cols_total), out_shape=(ch...  4.17 us
    ppermute x3, starting transfers between devices, core(): lax.ppermute(array, ('py', 'px'), self.pairs(lambda r, c: (r ^ 1, c)))  4.15 us
  transfers between devices with their start and end apart: 15, of which 4 were waited for; matrix products, arithmetic and copies ran while one was open for 0% of the time, Pallas kernels for 34%

profile of v5, /device:TPU:1, one launch (start us, length us, event | category | flops | bytes accessed | tf_op | source)
XLA Modules:
  0.0 68.8 jit_solution(12763207530575829855)
XLA Ops:
  0.0 4.2 %order_pieces.1 = (bf16[16,128,128]{2,1,0:T(8,128)(2,1)}, bf16[16,128,128]{2,1,0:T(8,128)(2,1)}, bf16[16,128,128]{2,1,0:T(8,128)(2,1)}, bf16[16,128,128]{2,1,0:T...) custom-call(s32[1,64]{1,0:T(1,128)} %bitcast.2, ...), custom_call_target="tpu_custom_call" | custom-call | tf_op jit(solution)/shard_map/order_pieces/pallas_call | solution.py:175
  4.2 2.1 %collective-permute-start = (bf16[16,128,128]{2,1,0:T(8,128)(2,1)}, bf16[16,128,128]{2,1,0:T(8,128)(2,1)S(1)}, u32[]{:S(2)}, u32[]{:S(2)}) collective-permute-start(bf16[16,128,128]{2,1,0:T(8,128)(2,1)} %get-tuple-element.42.refs_0_), channel_id=1, source_target_pairs={{0,1},{1,0},{2,3},{3,2},{4,5},{5,4},{6,7},{7,6},{8,9},{9,8},{10,11... | collective-permute-start | bytes 1572872 | tf_op jit(solution)/shard_map/ppermute | solution.py:750
  6.3 0.1 collective-permute-start.1
  6.4 0.7 collective-permute-start.2
  7.0 4.0 %collective-permute-start.3 = (bf16[16,128,128]{2,1,0:T(8,128)(2,1)}, bf16[16,128,128]{2,1,0:T(8,128)(2,1)S(1)}, u32[]{:S(2)}, u32[]{:S(2)}) collective-permute-start(bf16[16,128,128]{2,1,0:T(8,128)(2,1)} %get-tuple-element.50.refs_1_), channel_id=1, source_target_pairs={{0,1},{1,0},{2,3},{3,2},{4,5},{5,4},{6,7},{7,6},{8,9},{9,8},{10,11... | collective-permute-start | bytes 1572872 | tf_op jit(solution)/shard_map/ppermute | solution.py:750
  11.0 0.0 copy-done
  11.0 0.0 copy-start.10
  11.0 8.4 %matched_inside.1 = (f32[1024,1024]{1,0:T(8,128)}, bf16[2,1024,256]{2,1,0:T(8,128)(2,1)S(1)}, bf16[2,32,1024]{2,1,0:T(8,128)(2,1)S(1)}) custom-call(f32[3,15]{1,0:T(4,128)S(1)} %copy-done.9, bf16[1024,1024]{1,0:T(8,128)(2,1)S(1)} %copy-done, bf16[256,384]{1,0:T(8,128)(2,1)S(1)} %copy-done.3, bf16[3,128,160]{2,1,0:T(8,128)(2,1)S(1)} %copy-done.4), custom_call_target="tpu_custom_call" | custom-call | flops 8000000000 | bytes 1 | tf_op jit(solution)/shard_map/matched_inside/pallas_call | solution.py:422
  19.4 0.0 copy-start.8
  19.4 0.0 copy-start.5
  19.4 0.0 collective-permute-done.1.near_ref
  19.4 0.0 collective-permute-done.2.far_ref
  19.4 0.0 collective-permute-done.refs_4_
  19.4 3.6 %collective-permute-start.7 = (bf16[16,128,128]{2,1,0:T(8,128)(2,1)S(1)}, bf16[16,128,128]{2,1,0:T(8,128)(2,1)S(1)}, u32[]{:S(2)}, u32[]{:S(2)}) collective-permute-start(bf16[16,128,128]{2,1,0:T(8,128)(2,1)S(1)} %collective-permute-done.refs_4_), channel_id=1, source_target_pairs={{0,2},{2,4},{3,1},{4,6},{5,3},{7,5},{8,10},{10,12},{11,9},{12,14},... | collective-permute-start | bytes 1572872 | tf_op jit(solution)/shard_map/ppermute | solution.py:756
  23.1 0.3 row_rims.1
  23.4 2.9 %collective-permute-start.4 = (bf16[176,128]{1,0:T(8,128)(2,1)S(1)}, bf16[176,128]{1,0:T(8,128)(2,1)S(1)}, u32[]{:S(2)}, u32[]{:S(2)}) collective-permute-start(bf16[176,128]{1,0:T(8,128)(2,1)S(1)} %get-tuple-element.52.sent_ref), channel_id=1, source_target_pairs={{0,8},{1,9},{2,10},{3,11},{4,12},{5,13},{6,14},{7,15},{8,0},{9,1},... | collective-permute-start | bytes 135176 | tf_op jit(solution)/shard_map/ppermute | solution.py:759
  26.3 3.0 %collective-permute-start.5 = (bf16[176,128]{1,0:T(8,128)(2,1)S(1)}, bf16[176,128]{1,0:T(8,128)(2,1)S(1)}, u32[]{:S(2)}, u32[]{:S(2)}) collective-permute-start(bf16[176,128]{1,0:T(8,128)(2,1)S(1)} %get-tuple-element.53), channel_id=1, source_target_pairs={{8,16},{9,17},{10,18},{11,19},{12,20},{13,21},{14,22},{15,23},{16,... | collective-permute-start | bytes 135176 | tf_op jit(solution)/shard_map/ppermute | solution.py:762
  29.4 0.0 copy-done.8
  29.4 0.1 collective-permute-start.6
  29.4 0.7 %collective-permute-done.3.refs_5_ = bf16[16,128,128]{2,1,0:T(8,128)(2,1)S(1)} collective-permute-done((bf16[16,128,128]{2,1,0:T(8,128)(2,1)}, bf16[16,128,128]{2,1,0:T(8,128)(2,1)S(1)}, u32[]{:S(2)}, u32[]{:S(2)}) %collective-permute-start.3) | collective-permute-done | bytes 524320 | tf_op jit(solution)/shard_map/ppermute | solution.py:750
  30.2 0.0 collective-permute-done.4.core_ref
  30.2 1.8 %collective-permute-done.5.other_ref = bf16[176,128]{1,0:T(8,128)(2,1)S(1)} collective-permute-done((bf16[176,128]{1,0:T(8,128)(2,1)S(1)}, bf16[176,128]{1,0:T(8,128)(2,1)S(1)}, u32[]{:S(2)}, u32[]{:S(2)}) %collective-permute-start.5) | collective-permute-done | bytes 45088 | tf_op jit(solution)/shard_map/ppermute | solution.py:762
  31.9 3.2 %collective-permute-start.9 = (bf16[16,128,128]{2,1,0:T(8,128)(2,1)S(1)}, bf16[16,128,128]{2,1,0:T(8,128)(2,1)S(1)}, u32[]{:S(2)}, u32[]{:S(2)}) collective-permute-start(bf16[16,128,128]{2,1,0:T(8,128)(2,1)S(1)} %collective-permute-done.3.refs_5_), channel_id=1, source_target_pairs={{0,2},{2,4},{3,1},{4,6},{5,3},{7,5},{8,10},{10,12},{11,9},{12,14},... | collective-permute-start | bytes 1572872 | tf_op jit(solution)/shard_map/ppermute | solution.py:756
  35.2 0.1 collective-permute-start.8
  35.3 4.2 %matched_sides.1.base_ref = f32[1024,1024]{1,0:T(8,128)} custom-call(f32[3,15]{1,0:T(4,128)S(1)} %copy-done.9, bf16[16,1152]{1,0:T(8,128)(2,1)S(1)} %collective-permute-done.1.near_ref, bf16[16,1152]{1,0:T(8,128)(2,1)S(1)} %collective-permute-done.2.far_ref, bf16[256,384]{1,0:T(8,128)(2,1)S(1)} %copy-done.3, ...), custom_call_target="tpu_custom_call", output_to_operand_aliasing={{}: (6, {})} | custom-call | tf_op jit(solution)/shard_map/matched_sides/pallas_call | solution.py:513
  39.5 0.0 collective-permute-done.7.refs_7_.part_ref
  39.5 0.0 copy-done.1
  39.5 0.0 copy-done.2
  39.5 0.1 forward_pieces.1
  39.6 1.2 %collective-permute-start.11 = (bf16[32,128,128]{2,1,0:T(8,128)(2,1)S(1)}, bf16[32,128,128]{2,1,0:T(8,128)(2,1)S(1)}, u32[]{:S(2)}, u32[]{:S(2)}) collective-permute-start(bf16[32,128,128]{2,1,0:T(8,128)(2,1)S(1)} %get-tuple-element.77), channel_id=1, source_target_pairs={{0,8},{1,9},{2,10},{3,11},{4,12},{5,13},{6,14},{7,15},{8,0},{9,1},... | collective-permute-start | bytes 3145736 | tf_op jit(solution)/shard_map/ppermute | solution.py:759
  40.8 3.9 %collective-permute-start.12 = (bf16[32,128,128]{2,1,0:T(8,128)(2,1)S(1)}, bf16[32,128,128]{2,1,0:T(8,128)(2,1)S(1)}, u32[]{:S(2)}, u32[]{:S(2)}) collective-permute-start(bf16[32,128,128]{2,1,0:T(8,128)(2,1)S(1)} %get-tuple-element.78), channel_id=1, source_target_pairs={{8,16},{9,17},{10,18},{11,19},{12,20},{13,21},{14,22},{15,23},{16,... | collective-permute-start | bytes 3145736 | tf_op jit(solution)/shard_map/ppermute | solution.py:762
  44.7 0.0 collective-permute-done.6.refs_6_
  44.7 3.5 %collective-permute-start.10 = (bf16[16,128,128]{2,1,0:T(8,128)(2,1)S(1)}, bf16[16,128,128]{2,1,0:T(8,128)(2,1)S(1)}, u32[]{:S(2)}, u32[]{:S(2)}) collective-permute-start(bf16[16,128,128]{2,1,0:T(8,128)(2,1)S(1)} %collective-permute-done.6.refs_6_), channel_id=1, source_target_pairs={{0,2},{2,4},{3,1},{4,6},{5,3},{7,5},{8,10},{10,12},{11,9},{12,14},... | collective-permute-start | bytes 1572872 | tf_op jit(solution)/shard_map/ppermute | solution.py:756
  48.2 0.0 copy-start.6
  48.2 2.2 %matched_ends.1 = (f32[1024,1024]{1,0:T(8,128)}, s32[16,128]{1,0:T(8,128)S(1)}, f32[8,128]{1,0:T(8,128)S(1)}) custom-call(f32[3,15]{1,0:T(4,128)S(1)} %copy-done.9, bf16[16,1152]{1,0:T(8,128)(2,1)S(1)} %collective-permute-done.1.near_ref, bf16[16,1152]{1,0:T(8,128)(2,1)S(1)} %collective-permute-done.2.far_ref, ...), custom_call_target="tpu_custom_call", output_to_operand_aliasing={{0}: (9, {})} | custom-call | tf_op jit(solution)/shard_map/matched_ends/pallas_call | solution.py:600
  50.4 0.0 collective-permute-done.9.refs_8_
  50.5 4.2 %add_early.1.base_ref = f32[1024,1024]{1,0:T(8,128)} custom-call(s32[16,128]{1,0:T(8,128)S(1)} %get-tuple-element.64.blocks_ref, f32[8,128]{1,0:T(8,128)S(1)} %get-tuple-element.65.share_ref, f32[1024,1024]{1,0:T(8,128)} %get-tuple-element.69.base_ref, bf16[16,128,128]{2,1,0:T(8,128)(2,1)S(1)} %copy-done.6, ...), custom_call_target="tpu_custom_call", output_to_operand_aliasing={{}: (2, {})} | custom-call | tf_op jit(solution)/shard_map/add_early/pallas_call | solution.py:716
  54.6 0.0 collective-permute-done.8.refs_0_
  54.6 0.2 pad_maximum_fusion
  54.8 0.1 collective-permute-start.13
  54.9 2.9 %collective-permute-start.14 = (bf16[16,128,128]{2,1,0:T(8,128)(2,1)S(1)}, bf16[16,128,128]{2,1,0:T(8,128)(2,1)S(1)}, u32[]{:S(2)}, u32[]{:S(2)}) collective-permute-start(bf16[16,128,128]{2,1,0:T(8,128)(2,1)S(1)} %collective-permute-done.8.refs_0_), channel_id=1, source_target_pairs={{8,16},{9,17},{10,18},{11,19},{12,20},{13,21},{14,22},{15,23},{16,... | collective-permute-start | bytes 1572872 | tf_op jit(solution)/shard_map/ppermute | solution.py:762
  57.8 1.3 %collective-permute-done.10.refs_1_ = bf16[16,128,128]{2,1,0:T(8,128)(2,1)S(1)} collective-permute-done((bf16[16,128,128]{2,1,0:T(8,128)(2,1)S(1)}, bf16[16,128,128]{2,1,0:T(8,128)(2,1)S(1)}, u32[]{:S(2)}, u32[]{:S(2)}) %collective-permute-start.10) | collective-permute-done | bytes 524320 | tf_op jit(solution)/shard_map/ppermute | solution.py:756
  59.1 0.0 collective-permute-done.11.refs_2_.refs_4_
  59.1 0.0 collective-permute-done.12.refs_3_.refs_5_
  59.1 3.9 %add_late.1.base_ref = f32[1024,1024]{1,0:T(8,128)} custom-call(s32[16,128]{1,0:T(8,128)S(1)} %get-tuple-element.64.blocks_ref, f32[8,128]{1,0:T(8,128)S(1)} %get-tuple-element.65.share_ref, f32[1024,1024]{1,0:T(8,128)} %add_early.1.base_ref, bf16[16,128,128]{2,1,0:T(8,128)(2,1)S(1)} %collective-permute-done.8.refs_0_, ...), custom_call_target="tpu_custom_call", output_to_operand_aliasing={{}: (2, {})} | custom-call | flops 12000000000 | tf_op jit(solution)/shard_map/add_late/pallas_call | solution.py:716
  63.0 2.4 %collective-permute-done.14.refs_3_ = bf16[16,128,128]{2,1,0:T(8,128)(2,1)S(1)} collective-permute-done((bf16[16,128,128]{2,1,0:T(8,128)(2,1)S(1)}, bf16[16,128,128]{2,1,0:T(8,128)(2,1)S(1)}, u32[]{:S(2)}, u32[]{:S(2)}) %collective-permute-start.14) | collective-permute-done | bytes 524320 | tf_op jit(solution)/shard_map/ppermute | solution.py:762
  65.4 0.0 collective-permute-done.13.refs_0_.refs_1_.refs_2_
  65.4 3.4 %add_last.1 = f32[1024,1024]{1,0:T(8,128)} custom-call(s32[16,128]{1,0:T(8,128)S(1)} %get-tuple-element.64.blocks_ref, f32[8,128]{1,0:T(8,128)S(1)} %get-tuple-element.65.share_ref, f32[1024,1024]{1,0:T(8,128)} %add_late.1.base_ref, bf16[48,128,128]{2,1,0:T(8,128)(2,1)S(1)} %collective-permute-done.13.refs_0_.refs_1_.refs_2_, ...), custom_call_target="tpu_custom_call", output_to_operand_aliasing={{}: (2, {})} | custom-call | flops 12000000000 | tf_op jit(solution)/shard_map/add_last/pallas_call | solution.py:716
  (14 shorter events, 0.0 us)
Async XLA Ops:
  0.0 11.0 %copy-start = (bf16[1024,1024]{1,0:T(8,128)(2,1)S(1)}, bf16[1024,1024]{1,0:T(8,128)(2,1)}, u32[]{:S(2)}) copy-start(bf16[1024,1024]{1,0:T(8,128)(2,1)} %template_ref.2) | copy-start | bytes 6291460
  0.0 11.0 %copy-start.3 = (bf16[256,384]{1,0:T(8,128)(2,1)S(1)}, bf16[256,384]{1,0:T(8,128)(2,1)}, u32[]{:S(2)}) copy-start(bf16[256,384]{1,0:T(8,128)(2,1)} %constant.4.clone.across_ref) | copy-start | bytes 589828
  0.0 11.0 %copy-start.4 = (bf16[3,128,160]{2,1,0:T(8,128)(2,1)S(1)}, bf16[3,128,160]{2,1,0:T(8,128)(2,1)}, u32[]{:S(2)}) copy-start(bf16[3,128,160]{2,1,0:T(8,128)(2,1)} %constant.5.clone.down_ref) | copy-start | bytes 368644
  0.0 11.0 %copy-start.9 = (f32[3,15]{1,0:T(4,128)S(1)}, f32[3,15]{1,0:T(4,128)}, u32[]{:S(2)}) copy-start(f32[3,15]{1,0:T(4,128)} %coef_ref.5) | copy-start | bytes 544
  4.2 15.2 %collective-permute-start = (bf16[16,128,128]{2,1,0:T(8,128)(2,1)}, bf16[16,128,128]{2,1,0:T(8,128)(2,1)S(1)}, u32[]{:S(2)}, u32[]{:S(2)}) collective-permute-start(bf16[16,128,128]{2,1,0:T(8,128)(2,1)} %get-tuple-element.42.refs_0_), channel_id=1, source_target_pairs={{0,1},{1,0},{2,3},{3,2},{4,5},{5,4},{6,7},{7,6},{8,9},{9,8},{10,11... | collective-permute-start | bytes 1572872 | tf_op jit(solution)/shard_map/ppermute | solution.py:750
  6.3 13.1 %collective-permute-start.1 = (bf16[16,1152]{1,0:T(8,128)(2,1)}, bf16[16,1152]{1,0:T(8,128)(2,1)S(1)}, u32[]{:S(2)}, u32[]{:S(2)}) collective-permute-start(bf16[16,1152]{1,0:T(8,128)(2,1)} %get-tuple-element.43), channel_id=1, source_target_pairs={{0,1},{1,0},{2,3},{3,2},{4,5},{5,4},{6,7},{7,6},{8,9},{9,8},{10,11... | collective-permute-start | bytes 110600 | tf_op jit(solution)/shard_map/ppermute | solution.py:750
  6.4 13.0 %collective-permute-start.2 = (bf16[16,1152]{1,0:T(8,128)(2,1)}, bf16[16,1152]{1,0:T(8,128)(2,1)S(1)}, u32[]{:S(2)}, u32[]{:S(2)}) collective-permute-start(bf16[16,1152]{1,0:T(8,128)(2,1)} %get-tuple-element.44), channel_id=1, source_target_pairs={{1,2},{2,1},{3,4},{4,3},{5,6},{6,5},{9,10},{10,9},{11,12},{12,11},... | collective-permute-start | bytes 110600 | tf_op jit(solution)/shard_map/ppermute | solution.py:753
  7.0 23.1 %collective-permute-start.3 = (bf16[16,128,128]{2,1,0:T(8,128)(2,1)}, bf16[16,128,128]{2,1,0:T(8,128)(2,1)S(1)}, u32[]{:S(2)}, u32[]{:S(2)}) collective-permute-start(bf16[16,128,128]{2,1,0:T(8,128)(2,1)} %get-tuple-element.50.refs_1_), channel_id=1, source_target_pairs={{0,1},{1,0},{2,3},{3,2},{4,5},{5,4},{6,7},{7,6},{8,9},{9,8},{10,11... | collective-permute-start | bytes 1572872 | tf_op jit(solution)/shard_map/ppermute | solution.py:750
  11.0 12.0 %copy-start.10 = (bf16[16,128]{1,0:T(8,128)(2,1)S(1)}, bf16[16,128]{1,0:T(8,128)(2,1)}, u32[]{:S(2)}) copy-start(bf16[16,128]{1,0:T(8,128)(2,1)} %get-tuple-element.51.label_ref) | copy-start | bytes 12292
  19.4 10.0 %copy-start.8 = (bf16[16,128,128]{2,1,0:T(8,128)(2,1)S(1)}, bf16[16,128,128]{2,1,0:T(8,128)(2,1)}, u32[]{:S(2)}) copy-start(bf16[16,128,128]{2,1,0:T(8,128)(2,1)} %get-tuple-element.58.refs_2_) | copy-start | bytes 1572868
  19.4 15.7 %copy-start.5 = (bf16[16,128,128]{2,1,0:T(8,128)(2,1)S(1)}, bf16[16,128,128]{2,1,0:T(8,128)(2,1)}, u32[]{:S(2)}) copy-start(bf16[16,128,128]{2,1,0:T(8,128)(2,1)} %get-tuple-element.66.refs_3_) | copy-start | bytes 1572868
  19.4 20.0 %collective-permute-start.7 = (bf16[16,128,128]{2,1,0:T(8,128)(2,1)S(1)}, bf16[16,128,128]{2,1,0:T(8,128)(2,1)S(1)}, u32[]{:S(2)}, u32[]{:S(2)}) collective-permute-start(bf16[16,128,128]{2,1,0:T(8,128)(2,1)S(1)} %collective-permute-done.refs_4_), channel_id=1, source_target_pairs={{0,2},{2,4},{3,1},{4,6},{5,3},{7,5},{8,10},{10,12},{11,9},{12,14},... | collective-permute-start | bytes 1572872 | tf_op jit(solution)/shard_map/ppermute | solution.py:756
  23.4 6.8 %collective-permute-start.4 = (bf16[176,128]{1,0:T(8,128)(2,1)S(1)}, bf16[176,128]{1,0:T(8,128)(2,1)S(1)}, u32[]{:S(2)}, u32[]{:S(2)}) collective-permute-start(bf16[176,128]{1,0:T(8,128)(2,1)S(1)} %get-tuple-element.52.sent_ref), channel_id=1, source_target_pairs={{0,8},{1,9},{2,10},{3,11},{4,12},{5,13},{6,14},{7,15},{8,0},{9,1},... | collective-permute-start | bytes 135176 | tf_op jit(solution)/shard_map/ppermute | solution.py:759
  26.3 5.6 %collective-permute-start.5 = (bf16[176,128]{1,0:T(8,128)(2,1)S(1)}, bf16[176,128]{1,0:T(8,128)(2,1)S(1)}, u32[]{:S(2)}, u32[]{:S(2)}) collective-permute-start(bf16[176,128]{1,0:T(8,128)(2,1)S(1)} %get-tuple-element.53), channel_id=1, source_target_pairs={{8,16},{9,17},{10,18},{11,19},{12,20},{13,21},{14,22},{15,23},{16,... | collective-permute-start | bytes 135176 | tf_op jit(solution)/shard_map/ppermute | solution.py:762
  29.4 15.3 %collective-permute-start.6 = (bf16[16,128,128]{2,1,0:T(8,128)(2,1)S(1)}, bf16[16,128,128]{2,1,0:T(8,128)(2,1)S(1)}, u32[]{:S(2)}, u32[]{:S(2)}) collective-permute-start(bf16[16,128,128]{2,1,0:T(8,128)(2,1)S(1)} %copy-done.8), channel_id=1, source_target_pairs={{0,1},{1,0},{2,3},{3,2},{4,5},{5,4},{6,7},{7,6},{8,9},{9,8},{10,11... | collective-permute-start | bytes 1572872 | tf_op jit(solution)/shard_map/ppermute | solution.py:750
  31.9 18.5 %collective-permute-start.9 = (bf16[16,128,128]{2,1,0:T(8,128)(2,1)S(1)}, bf16[16,128,128]{2,1,0:T(8,128)(2,1)S(1)}, u32[]{:S(2)}, u32[]{:S(2)}) collective-permute-start(bf16[16,128,128]{2,1,0:T(8,128)(2,1)S(1)} %collective-permute-done.3.refs_5_), channel_id=1, source_target_pairs={{0,2},{2,4},{3,1},{4,6},{5,3},{7,5},{8,10},{10,12},{11,9},{12,14},... | collective-permute-start | bytes 1572872 | tf_op jit(solution)/shard_map/ppermute | solution.py:756
  35.2 19.5 %collective-permute-start.8 = (bf16[16,128,128]{2,1,0:T(8,128)(2,1)S(1)}, bf16[16,128,128]{2,1,0:T(8,128)(2,1)S(1)}, u32[]{:S(2)}, u32[]{:S(2)}) collective-permute-start(bf16[16,128,128]{2,1,0:T(8,128)(2,1)S(1)} %copy-done.5), channel_id=1, source_target_pairs={{0,1},{1,0},{2,3},{3,2},{4,5},{5,4},{6,7},{7,6},{8,9},{9,8},{10,11... | collective-permute-start | bytes 1572872 | tf_op jit(solution)/shard_map/ppermute | solution.py:750
  35.2 4.2 %copy-start.1 = (bf16[32,128,128]{2,1,0:T(8,128)(2,1)S(1)}, bf16[32,128,128]{2,1,0:T(8,128)(2,1)}, u32[]{:S(2)}) copy-start(bf16[32,128,128]{2,1,0:T(8,128)(2,1)} %get-tuple-element.75.core_in) | copy-start | bytes 3145732
  35.2 4.2 %copy-start.2 = (bf16[32,128,128]{2,1,0:T(8,128)(2,1)S(1)}, bf16[32,128,128]{2,1,0:T(8,128)(2,1)}, u32[]{:S(2)}) copy-start(bf16[32,128,128]{2,1,0:T(8,128)(2,1)} %get-tuple-element.76.other_in) | copy-start | bytes 3145732
  39.6 19.5 %collective-permute-start.11 = (bf16[32,128,128]{2,1,0:T(8,128)(2,1)S(1)}, bf16[32,128,128]{2,1,0:T(8,128)(2,1)S(1)}, u32[]{:S(2)}, u32[]{:S(2)}) collective-permute-start(bf16[32,128,128]{2,1,0:T(8,128)(2,1)S(1)} %get-tuple-element.77), channel_id=1, source_target_pairs={{0,8},{1,9},{2,10},{3,11},{4,12},{5,13},{6,14},{7,15},{8,0},{9,1},... | collective-permute-start | bytes 3145736 | tf_op jit(solution)/shard_map/ppermute | solution.py:759
  40.8 18.3 %collective-permute-start.12 = (bf16[32,128,128]{2,1,0:T(8,128)(2,1)S(1)}, bf16[32,128,128]{2,1,0:T(8,128)(2,1)S(1)}, u32[]{:S(2)}, u32[]{:S(2)}) collective-permute-start(bf16[32,128,128]{2,1,0:T(8,128)(2,1)S(1)} %get-tuple-element.78), channel_id=1, source_target_pairs={{8,16},{9,17},{10,18},{11,19},{12,20},{13,21},{14,22},{15,23},{16,... | collective-permute-start | bytes 3145736 | tf_op jit(solution)/shard_map/ppermute | solution.py:762
  44.7 14.4 %collective-permute-start.10 = (bf16[16,128,128]{2,1,0:T(8,128)(2,1)S(1)}, bf16[16,128,128]{2,1,0:T(8,128)(2,1)S(1)}, u32[]{:S(2)}, u32[]{:S(2)}) collective-permute-start(bf16[16,128,128]{2,1,0:T(8,128)(2,1)S(1)} %collective-permute-done.6.refs_6_), channel_id=1, source_target_pairs={{0,2},{2,4},{3,1},{4,6},{5,3},{7,5},{8,10},{10,12},{11,9},{12,14},... | collective-permute-start | bytes 1572872 | tf_op jit(solution)/shard_map/ppermute | solution.py:756
  48.2 2.2 %copy-start.6 = (bf16[16,128,128]{2,1,0:T(8,128)(2,1)S(1)}, bf16[16,128,128]{2,1,0:T(8,128)(2,1)}, u32[]{:S(2)}) copy-start(bf16[16,128,128]{2,1,0:T(8,128)(2,1)} %get-tuple-element.42.refs_0_) | copy-start | bytes 1572868
  48.2 2.2 %copy-start.7 = (bf16[16,128,128]{2,1,0:T(8,128)(2,1)S(1)}, bf16[16,128,128]{2,1,0:T(8,128)(2,1)}, u32[]{:S(2)}) copy-start(bf16[16,128,128]{2,1,0:T(8,128)(2,1)} %get-tuple-element.50.refs_1_) | copy-start | bytes 1572868
  54.8 10.6 %collective-permute-start.13 = (bf16[48,128,128]{2,1,0:T(8,128)(2,1)S(1)}, bf16[48,128,128]{2,1,0:T(8,128)(2,1)S(1)}, u32[]{:S(2)}, u32[]{:S(2)}) collective-permute-start(bf16[48,128,128]{2,1,0:T(8,128)(2,1)S(1)} %pad_maximum_fusion), channel_id=1, source_target_pairs={{0,8},{1,9},{2,10},{3,11},{4,12},{5,13},{6,14},{7,15},{8,0},{9,1},... | collective-permute-start | bytes 4718600 | tf_op jit(solution)/shard_map/ppermute | solution.py:759
  54.9 10.5 %collective-permute-start.14 = (bf16[16,128,128]{2,1,0:T(8,128)(2,1)S(1)}, bf16[16,128,128]{2,1,0:T(8,128)(2,1)S(1)}, u32[]{:S(2)}, u32[]{:S(2)}) collective-permute-start(bf16[16,128,128]{2,1,0:T(8,128)(2,1)S(1)} %collective-permute-done.8.refs_0_), channel_id=1, source_target_pairs={{8,16},{9,17},{10,18},{11,19},{12,20},{13,21},{14,22},{15,23},{16,... | collective-permute-start | bytes 1572872 | tf_op jit(solution)/shard_map/ppermute | solution.py:762
